TPU v7x, 32 devices: a whole 2x2x4 slice. The times are simulated.
32 devices in a mesh: groups: 2 (over x), tensor: 8 (over z, y), pool: 2 (over core).
Axes of the slice: x: 2, y: 2, z: 4, core: 2. Of those that a mesh axis runs over, the one named last changes fastest.
Arguments:
- tokens: bfloat16 [16, 32, 8192], P(('groups', 'pool'), None, 'tensor'), parts along dimension 0, may hold values from -6 to 6
- mamba_in_weight: bfloat16 [8192, 2, 8192], P(None, None, 'tensor'), may hold values from -0.0625 to 0.0625
- state_projection: bfloat16 [8192, 640], P('tensor'), may hold values from -0.0625 to 0.0625
- inner_taps: bfloat16 [4, 8192], P(None, 'tensor'), may hold values from -3 to 3
- state_taps: bfloat16 [4, 512], replicated, may hold values from -3 to 3
- inner_history: bfloat16 [16, 3, 8192], P(('groups', 'pool'), None, 'tensor'), parts along dimension 0, may hold values from -6 to 6
- state_history: float32 [16, 3, 512], P(('groups', 'pool')), parts along dimension 0, may hold values from -6 to 6
- step_size_bias: float32 [128], P('tensor'), may hold values from -3 to 0
- log_decay_rate: float32 [128], P('tensor'), may hold values from -2 to 2
- skip_factor: float32 [128], P('tensor'), may hold values from 0.5 to 1.5
- gated_norm_gain: float32 [8192], P('tensor'), may hold values from 0.5 to 1.5
- mamba_out_weight: bfloat16 [8192, 8192], P('tensor'), may hold values from -0.0625 to 0.0625
- saved_state_pool: float32 [24, 128, 64, 256], P(('groups', 'pool'), 'tensor'), parts along dimension 0, may hold values from -6 to 6
- tenant_state_slot: int32 [16], P(('groups', 'pool')), parts along dimension 0, may hold values from 0 to 11, as said below
- attention_gain: float32 [8192], replicated, may hold values from 0.5 to 1.5
- query_matrix: bfloat16 [8192, 8192], P(None, 'tensor'), may hold values from -1 to 1
- adapter_down: bfloat16 [16, 8192, 64], P(None, 'tensor'), may hold values from -0.0625 to 0.0625
- adapter_up: bfloat16 [16, 64, 8192], P(None, None, 'tensor'), may hold values from -0.75 to 0.75
- tenant_adapter: int32 [16], P(('groups', 'pool')), parts along dimension 0, may hold values from 0 to 15
- key_value_weight: bfloat16 [8192, 2048], P('tensor'), may hold values from -0.0625 to 0.0625
- key_value_pool: bfloat16 [128, 32, 2048], P(('groups', 'tensor')), parts along dimension 0, may hold values from -6 to 6
- tenant_blocks: int32 [16, 8], P(('groups', 'pool')), parts along dimension 0, may hold values from 0 to 63, as said below
- cached_length: int32 [16], P(('groups', 'pool')), parts along dimension 0, may hold values from 1 to 256
- attention_out_weight: bfloat16 [8192, 8192], P('tensor'), may hold values from -0.0625 to 0.0625
Outputs:
- second: bfloat16 [16, 32, 8192], P(('groups', 'pool'), None, 'tensor'), parts along dimension 0
- final_state: float32 [16, 128, 64, 256], P(('groups', 'pool'), 'tensor'), parts along dimension 0
There are 2 independent parts, one for each index of `groups`. A program takes and returns all parts, laid end to end along the dimension named above; an argument that names none is the same for every part. Nothing has to cross between parts.
Inputs may be any that keep to these rules, and one draw needn't show every extreme that they name: `tenant_state_slot`: distinct slots. `tenant_blocks`: every pool block appears exactly once in the table.
All inputs are finite; a program needn't handle non-finite values.
Results may differ from a plain program's by a relative error of at most 0.0095.
Values may be sent and summed in bfloat16 or wider, within the bound.
No kernel may reach another device: no remote copies, remote signals or barrier semaphores. Data moves between devices by JAX's collectives and lax.ppermute only.
A program may use at most 320 MiB of HBM per device.

v0:
```python
import jax
import jax.numpy as jnp
from jax import lax
from jax.sharding import PartitionSpec as P

HDIM = 64
STATE = 256
QUERY_HEADS = 64
KEY_HEADS = 8
HEAD_SIZE = 128
INNER = 8192


epsilon = 1e-05
adapter_scale = 2.0
highest = lax.Precision.HIGHEST


def causal_conv(series, history, kernel):
    joined = jnp.concatenate([history.astype(jnp.float32), series.astype(jnp.float32)], axis=1)
    token_length = series.shape[1]
    summed_taps = kernel[0].astype(jnp.float32) * joined[:, 0:token_length]
    for offset in range(1, 4):
        summed_taps = (
            summed_taps
            + kernel[offset].astype(jnp.float32) * joined[:, offset : offset + token_length]
        )
    return jax.nn.silu(summed_taps)


def state_space(values, in_state, out_state, step_sizes, decay_rates, skip_terms, initial):
    log_decay = -step_sizes * decay_rates
    running = jnp.cumsum(log_decay, axis=1)
    token_length = values.shape[1]
    places = jnp.arange(token_length)
    lower_part = (places[:, None] >= places[None, :])[None, :, :, None]
    spread = running[:, :, None, :] - running[:, None, :, :]
    decays = jnp.where(lower_part, jnp.exp(jnp.where(lower_part, spread, 0.0)), 0.0)
    intersection = jnp.einsum("btn,bsn->bts", out_state, in_state, precision=highest)
    mixing = intersection[:, :, :, None] * decays * step_sizes[:, None, :, :]
    within = jnp.einsum("btsh,bshp->bthp", mixing, values, precision=highest)
    carried = (
        jnp.einsum("btn,bhpn->bthp", out_state, initial, precision=highest)
        * jnp.exp(running)[:, :, :, None]
    )
    result = within + carried + skip_terms[None, None, :, None] * values
    remain = jnp.exp(running[:, -1:, :] - running) * step_sizes
    final_state = jnp.exp(running[:, -1, :])[:, :, None, None] * initial + jnp.einsum(
        "bsh,bshp,bsn->bhpn", remain, values, in_state, precision=highest
    )
    return (result, final_state)


def tensor_sum(partial_value):
    return lax.psum(partial_value, "tensor")


def per_device(
    tokens,
    mamba_in_weight,
    state_projection,
    inner_taps,
    state_taps,
    inner_history,
    state_history,
    step_size_bias,
    log_decay_rate,
    skip_factor,
    gated_norm_gain,
    mamba_out_weight,
    saved_state_pool,
    tenant_state_slot,
    attention_gain,
    query_matrix,
    adapter_down,
    adapter_up,
    tenant_adapter,
    key_value_weight,
    key_value_pool,
    tenant_blocks,
    cached_length,
    attention_out_weight,
):
    tenant_count, token_length, columns = tokens.shape
    tensor_place = lax.axis_index("tensor")
    row_count = tenant_count * token_length
    own_tokens = tokens.reshape(row_count, columns)
    whole_tokens = lax.all_gather(own_tokens, "tensor", axis=1, tiled=True)
    width = whole_tokens.shape[1]
    inner_cols = mamba_in_weight.shape[2]
    inner = jnp.dot(
        whole_tokens,
        mamba_in_weight.reshape(width, 2 * inner_cols),
        preferred_element_type=jnp.float32,
    )
    inner = inner.astype(jnp.bfloat16).reshape(tenant_count, token_length, 2, inner_cols)
    projected = tensor_sum(
        jnp.dot(own_tokens, state_projection, preferred_element_type=jnp.float32)
    ).reshape(tenant_count, token_length, -1)
    head_count = step_size_bias.shape[0]
    conv_values = causal_conv(inner[:, :, 0], inner_history, inner_taps).reshape(
        tenant_count, token_length, head_count, HDIM
    )
    conv_bc = causal_conv(projected[:, :, : 2 * STATE], state_history, state_taps)
    raw_steps = lax.dynamic_slice_in_dim(
        projected, 2 * STATE + tensor_place * head_count, head_count, 2
    )
    step_sizes = jax.nn.softplus(raw_steps + step_size_bias)
    slot_states = lax.all_gather(
        saved_state_pool.astype(jnp.bfloat16), "pool", axis=0, tiled=True
    ).astype(saved_state_pool.dtype)
    initial = jnp.take(slot_states, tenant_state_slot, axis=0)
    result, final_state = state_space(
        conv_values,
        conv_bc[:, :, :STATE],
        conv_bc[:, :, STATE:],
        step_sizes,
        jnp.exp(log_decay_rate),
        skip_factor,
        initial,
    )
    gated = result.reshape(tenant_count, token_length, inner_cols) * jax.nn.silu(
        inner[:, :, 1].astype(jnp.float32)
    )
    gated_energy = tensor_sum(jnp.sum(gated * gated, axis=-1, keepdims=True))
    normed = (
        (gated * lax.rsqrt(gated_energy / INNER + epsilon) * gated_norm_gain)
        .astype(jnp.bfloat16)
        .reshape(row_count, inner_cols)
    )
    mixer_whole = lax.psum(
        jnp.dot(normed, mamba_out_weight, preferred_element_type=jnp.float32), "tensor"
    )
    first_full = (whole_tokens.astype(jnp.float32) + mixer_whole).astype(jnp.bfloat16)
    wide_full = lax.optimization_barrier(first_full).astype(jnp.float32)
    attn_full = (
        wide_full
        * lax.rsqrt(jnp.mean(wide_full * wide_full, axis=-1, keepdims=True) + epsilon)
        * attention_gain
    ).astype(jnp.bfloat16)
    own_first = lax.dynamic_slice_in_dim(first_full, tensor_place * columns, columns, 1)
    attn_own = lax.dynamic_slice_in_dim(attn_full, tensor_place * columns, columns, 1)
    query_cols = query_matrix.shape[1]
    query_rows = jnp.dot(attn_full, query_matrix, preferred_element_type=jnp.float32).reshape(
        tenant_count, token_length, query_cols
    )
    picked_down = jnp.take(adapter_down, tenant_adapter, axis=0)
    low_part = jnp.einsum(
        "bld,bdr->blr",
        attn_own.reshape(tenant_count, token_length, columns),
        picked_down,
        preferred_element_type=jnp.float32,
    )
    kv_part = jnp.dot(attn_own, key_value_weight, preferred_element_type=jnp.float32)
    low_total, kv_total = tensor_sum((low_part, kv_part))
    picked_up = jnp.take(adapter_up, tenant_adapter, axis=0)
    raised_rows = jnp.einsum(
        "blr,brc->blc",
        low_total.astype(jnp.bfloat16),
        picked_up,
        preferred_element_type=jnp.float32,
    )
    local_heads = query_cols // HEAD_SIZE
    query_rows = (
        (query_rows + adapter_scale * raised_rows)
        .astype(jnp.bfloat16)
        .reshape(tenant_count, token_length, local_heads, HEAD_SIZE)
    )
    group_size = QUERY_HEADS // KEY_HEADS
    key_head = tensor_place * local_heads // group_size
    fresh = kv_total.astype(jnp.bfloat16).reshape(
        tenant_count, token_length, 2, KEY_HEADS, HEAD_SIZE
    )
    fresh = lax.dynamic_index_in_dim(fresh, key_head, 3, keepdims=False)
    block_len = key_value_pool.shape[1]
    every_block = lax.all_gather(key_value_pool, "tensor", axis=0, tiled=True)
    layered = every_block.reshape(-1, block_len, 2, KEY_HEADS, HEAD_SIZE)
    own_cache = lax.dynamic_index_in_dim(layered, key_head, 3, keepdims=False)
    cached = jnp.take(own_cache, tenant_blocks, axis=0).reshape(tenant_count, -1, 2, HEAD_SIZE)
    context = cached.shape[1]
    keys_all = jnp.concatenate([cached[:, :, 0], fresh[:, :, 0]], axis=1)
    values_all = jnp.concatenate([cached[:, :, 1], fresh[:, :, 1]], axis=1)
    places = jnp.arange(context + token_length)
    positions = jnp.arange(token_length)
    visible = jnp.where(
        places[None, None, :] < context,
        places[None, None, :] < cached_length[:, None, None],
        places[None, None, :] - context <= positions[None, :, None],
    )
    scores = jnp.einsum(
        "bthd,bjd->bhtj", query_rows, keys_all, preferred_element_type=jnp.float32
    ) * HEAD_SIZE ** (-0.5)
    masked = jnp.where(visible[:, None], scores, -jnp.inf)
    highest_score = jnp.max(masked, axis=-1, keepdims=True)
    raised = jnp.where(visible[:, None], jnp.exp(masked - highest_score), 0.0)
    weights = (raised / jnp.sum(raised, axis=-1, keepdims=True)).astype(jnp.bfloat16)
    heads_out = jnp.einsum(
        "bhtj,bjd->bthd", weights, values_all, preferred_element_type=jnp.float32
    )
    heads_out = heads_out.astype(jnp.bfloat16).reshape(row_count, query_cols)
    attn_part = lax.psum_scatter(
        lax.dot_general(
            attention_out_weight,
            heads_out,
            (((0,), (1,)), ((), ())),
            preferred_element_type=jnp.float32,
        ),
        "tensor",
        scatter_dimension=0,
        tiled=True,
    )
    second = (lax.optimization_barrier(own_first).astype(jnp.float32) + attn_part.T).astype(
        jnp.bfloat16
    )
    return (second.reshape(tenant_count, token_length, columns), final_state)


def solution(mesh):
    in_specs = (
        P(("groups", "pool"), None, "tensor"),
        P(None, None, "tensor"),
        P("tensor", None),
        P(None, "tensor"),
        P(),
        P(("groups", "pool"), None, "tensor"),
        P(("groups", "pool"), None, None),
        P("tensor"),
        P("tensor"),
        P("tensor"),
        P("tensor"),
        P("tensor", None),
        P(("groups", "pool"), "tensor", None, None),
        P(("groups", "pool")),
        P(),
        P(None, "tensor"),
        P(None, "tensor", None),
        P(None, None, "tensor"),
        P(("groups", "pool")),
        P("tensor", None),
        P(("groups", "tensor"), None, None),
        P(("groups", "pool"), None),
        P(("groups", "pool")),
        P("tensor", None),
    )
    out_specs = (P(("groups", "pool"), None, "tensor"), P(("groups", "pool"), "tensor", None, None))
    return jax.shard_map(
        per_device, mesh=mesh, in_specs=in_specs, out_specs=out_specs, check_vma=False
    )
```

profile of v0, /device:TPU:0, one launch (start us, length us, event | category | flops | bytes accessed | tf_op | source)
XLA Modules:
  0.0 655.9 jit_solution(9330474383063445209)
XLA Ops:
  7.2 2.7 fusion.103
  10.7 4.9 convert_element_type.172
  15.8 23.3 %copy.98 = bf16[1024,8,2,1024]{3,1,2,0:T(8,128)(2,1)} copy(bf16[1024,8,2,1024]{3,2,1,0:T(2,128)(2,1)} %bitcast.151) | data formatting | bytes 67108864
  41.6 43.5 %all-reduce.5.cloned.1.call-done = f32[4,32,640]{2,1,0:T(8,128)} async-done(((f32[4,32,640]{2,1,0:T(8,128)}), f32[4,32,640]{2,1,0:T(8,128)}) %all-reduce.5.cloned.1.call-update) | async-done | bytes 327696 | tf_op jit(solution)/shard_map/psum | solution.py:55
  90.2 45.7 %all-gather.4.cloned.1.call-done = bf16[128,8192]{1,0:T(8,128)(2,1)} async-done(((bf16[128,1024]{1,0:T(8,128)(2,1)}), bf16[128,8192]{1,0:T(8,128)(2,1)}) %all-gather.4.cloned.1.call-update) | async-done | bytes 2097168 | tf_op jit(solution)/shard_map/all_gather | solution.py:88
  136.0 17.9 %convolution_convert_fusion = bf16[128,2048]{1,0:T(8,128)(2,1)S(1)} fusion(bf16[128,8192]{1,0:T(8,128)(2,1)} %all-gather.4.cloned.1.call-done, bf16[8192,2048]{1,0:T(8,128)(2,1)} %bitcast.150), kind=kOutput, calls=%fused_computation.15 | convolution fusion | flops 4295229440 | bytes 36175872 | tf_op jit(solution)/shard_map/dot_general | solution.py:91
  158.9 3.7 convolution_bitcast_fusion.1
  162.7 8.9 %convert_element_type.173 = f32[12,16,64,256]{3,2,1,0:T(8,128)} convert(bf16[12,16,64,256]{3,2,1,0:T(8,128)(2,1)} %all-gather.6.cloned.1.call-done) | non-fusion elementwise | flops 3145728 | bytes 18874368 | tf_op jit(solution)/shard_map/convert_element_type | solution.py:111
  171.5 7.5 %gather_fusion = f32[4,16,64,256]{3,2,1,0:T(8,128)} fusion(f32[12,16,64,256]{3,2,1,0:T(8,128)} %convert_element_type.173, s32[1024]{0:T(1024)} %pad_clamp_fusion.2), kind=kCustom, calls=%fused_computation | custom fusion | bytes 8388624 | tf_op jit(solution)/shard_map/jit(_take)/gather | solution.py:112
  179.1 9.7 %multiply_reduce_fusion = (f32[4,32]{1,0:T(4,128)S(1)}, f32[4,32,16,64]{3,1,2,0:T(8,128)S(1)}) fusion(f32[4,32,16,64]{3,2,1,0:T(8,128)} %reshape.248, f32[4,32,16,64]{3,2,1,0:T(8,128)} %reshape.228, f32[16]{0:T(128)S(1)} %copy-done.25, f32[4,32,16,64]{3,1,2,0:T(8,128)} %convolution_bitcast_fusion.1, f32[4,32,16]{1,2,0:T(8,128)S(1)} %copy-done.10, ...), kind=kOutput, calls=%fused_computation.34 | convolution fusion | flops 405143424 | bytes 6456832 | tf_op jit(solution)/shard_map/btn,bhpn->bthp/dot_general | solution.py:43
  191.9 17.6 %psum.36 = f32[4,32,1]{1,0,2:T(4,128)S(1)} all-reduce(f32[4,32,1]{1,0,2:T(4,128)S(1)} %bitcast.176), channel_id=1, replica_groups=mesh['groups'=2,'tensor'=8,'pool'=2] {'tensor'}, use_global_device_ids=true, to_apply=%region_3.4 | all-reduce | flops 128 | bytes 1024 | tf_op jit(solution)/shard_map/psum | solution.py:55
  209.8 10.1 %fusion.104 = f32[128,8192]{1,0:T(8,128)} fusion(bf16[128,1024]{1,0:T(8,128)(2,1)S(1)} %fusion.53, bf16[1024,8192]{1,0:T(8,128)(2,1)} %param.35), kind=kOutput, calls=%fused_computation.168 | convolution fusion | flops 2147483648 | bytes 21233664 | tf_op jit(solution)/shard_map/dot_general | solution.py:132
  222.0 3.0 gather_fusion.3
  226.0 148.6 %all-reduce.7.cloned.1.call-done = f32[128,8192]{1,0:T(8,128)} async-done(((f32[128,8192]{1,0:T(8,128)}), f32[128,8192]{1,0:T(8,128)}) %all-reduce.7.cloned.1.call-update) | async-done | bytes 4194320 | tf_op jit(solution)/shard_map/psum | solution.py:131
  374.5 3.3 add_convert_fusion
  382.6 91.5 %all-reduce.8 = (bf16[128,2048]{1,0:T(8,128)(2,1)}, bf16[4,32,64]{2,1,0:T(8,128)(2,1)}) all-reduce(f32[128,2048]{1,0:T(8,128)S(1)} %fusion.105, f32[4,32,64]{2,1,0:T(8,128)S(1)} %fusion.46), channel_id=1, replica_groups=mesh['groups'=2,'tensor'=8,'pool'=2] {'tensor'}, use_global_device_ids=true, to_apply=%region_6.7 | all-reduce | flops 270336 | bytes 1622016 | tf_op jit(solution)/shard_map/psum | solution.py:55
  475.5 8.9 %fusion.106 = f32[128,1024]{1,0:T(8,128)S(1)} fusion(bf16[128,8192]{1,0:T(8,128)(2,1)} %copy-done.2, bf16[8192,1024]{1,0:T(8,128)(2,1)} %param.39), kind=kOutput, calls=%fused_computation.170 | convolution fusion | flops 2147483648 | bytes 19398656 | tf_op jit(solution)/shard_map/dot_general | solution.py:144
  486.0 40.0 %all-gather.8.cloned.1.call-done = bf16[64,32,2048]{2,1,0:T(8,128)(2,1)} async-done(((bf16[8,32,2048]{2,1,0:T(8,128)(2,1)}), bf16[64,32,2048]{2,1,0:T(8,128)(2,1)}) %all-gather.8.cloned.1.call-update) | async-done | bytes 8388624 | tf_op jit(solution)/shard_map/all_gather | solution.py:176
  526.0 9.8 %copy.99 = bf16[256,8,16,128]{3,2,1,0:T(8,128)(2,1)} copy(bf16[256,8,16,128]{3,1,2,0:T(8,128)(2,1)} %bitcast.153) | data formatting | bytes 16777216
  535.7 6.1 constant_dynamic-slice_fusion.2
  544.8 2.8 fusion.100
  549.7 10.1 %convolution_bitcast_fusion = f32[8192,128]{0,1:T(8,128)} fusion(bf16[1024,8192]{1,0:T(8,128)(2,1)} %param.47, bf16[16,8,8,128]{3,2,1,0:T(8,128)(2,1)S(1)} %bitcast.161), kind=kOutput, calls=%fused_computation.5 | convolution fusion | flops 2147483648 | bytes 21233664 | tf_op jit(solution)/shard_map/dot_general | solution.py:202
  561.3 7.2 %multiply_add_fusion = f32[4,16,64,256]{3,2,1,0:T(8,128)} fusion(f32[4,16,64,256]{3,2,1,0:T(8,128)} %gather_fusion, f32[4,16]{1,0:T(4,128)S(1)} %exp.54, pred[4]{0:T(512)(128)(4,1)S(1)} %copy-done.21, f32[4,32,16,64]{3,2,1,0:T(8,128)S(1)} %broadcast_multiply_fusion, f32[4,32,512]{2,1,0:T(8,128)S(1)} %divide_multiply_fusion.1), kind=kOutput, calls=%fused_computation.11 | convolution fusion | flops 405798912 | bytes 9570816 | tf_op jit(solution)/shard_map/bsh,bshp,bsn->bhpn/dot_general | solution.py:48
  569.5 77.6 %reduce-scatter.2.cloned.1.call-done = f32[1024,128]{0,1:T(8,128)} async-done(((f32[8192,128]{0,1:T(8,128)}), f32[1024,128]{0,1:T(8,128)}) %reduce-scatter.2.cloned.1.call-update) | async-done | bytes 524304 | tf_op jit(solution)/shard_map/reduce_scatter | solution.py:201
  (135 shorter events, 36.9 us)
Async XLA Ops:
  7.2 213.4 %copy-start = (bf16[16,1024,64]{1,2,0:T(8,128)(2,1)S(1)}, bf16[16,1024,64]{1,2,0:T(8,128)(2,1)}, u32[]{:S(2)}) copy-start(bf16[16,1024,64]{1,2,0:T(8,128)(2,1)} %param.40) | copy-start | bytes 6291460
  7.2 77.9 %all-reduce.5.cloned.1.call-start = ((), (), s32[]{:S(2)}) async-start(), calls=%async_computation.2 | async-start | bytes 655360 | tf_op jit(solution)/shard_map/psum | solution.py:55
  9.9 126.1 %all-gather.4.cloned.1.call-start = ((), (), s32[]{:S(2)}) async-start(), calls=%async_computation.1 | async-start | bytes 2359296 | tf_op jit(solution)/shard_map/all_gather | solution.py:88
  10.7 152.0 %all-gather.6.cloned.1.call-start = ((), (), s32[]{:S(2)}) async-start(), calls=%async_computation.3 | async-start | bytes 9437184 | tf_op jit(solution)/shard_map/all_gather | solution.py:109
  15.7 358.9 %all-reduce.7.cloned.1.call-start = ((), (), s32[]{:S(2)}) async-start(), calls=%async_computation.4 | async-start | bytes 8388608 | tf_op jit(solution)/shard_map/psum | solution.py:131
  15.7 23.4 %copy-start.14 = (bf16[4,3,1024]{2,0,1:T(4,128)(2,1)S(1)}, bf16[4,3,1024]{2,0,1:T(4,128)(2,1)}, u32[]{:S(2)}) copy-start(bf16[4,3,1024]{2,0,1:T(4,128)(2,1)} %param.29) | copy-start | bytes 73732
  15.7 23.4 %copy-start.13 = (f32[4,3,512]{2,0,1:T(4,128)S(1)}, f32[4,3,512]{2,0,1:T(4,128)}, u32[]{:S(2)}) copy-start(f32[4,3,512]{2,0,1:T(4,128)} %param.30) | copy-start | bytes 73732
  15.7 23.4 %copy-start.23 = (f32[16]{0:T(128)S(1)}, f32[16]{0:T(128)}, u32[]{:S(2)}) copy-start(f32[16]{0:T(128)} %param.32) | copy-start | bytes 196
  15.8 24.0 %copy-start.24 = (s32[4]{0:T(128)S(1)}, s32[4]{0:T(128)}, u32[]{:S(2)}) copy-start(s32[4]{0:T(128)} %param.37) | copy-start | bytes 52
  15.8 25.2 %copy-start.15 = (bf16[4,512]{1,0:T(4,128)(2,1)S(1)}, bf16[4,512]{1,0:T(4,128)(2,1)}, u32[]{:S(2)}) copy-start(bf16[4,512]{1,0:T(4,128)(2,1)} %param.28) | copy-start | bytes 12292
  15.8 25.2 %copy-start.12 = (bf16[4,1024]{1,0:T(4,128)(2,1)S(1)}, bf16[4,1024]{1,0:T(4,128)(2,1)}, u32[]{:S(2)}) copy-start(bf16[4,1024]{1,0:T(4,128)(2,1)} %param.27) | copy-start | bytes 24580
  15.8 69.3 %copy-start.19 = (f32[16]{0:T(128)S(1)}, f32[16]{0:T(128)}, u32[]{:S(2)}) copy-start(f32[16]{0:T(128)} %param.31) | copy-start | bytes 196
  171.5 7.5 %copy-start.10 = (f32[4,32,16]{1,2,0:T(8,128)S(1)}, f32[4,32,16]{1,2,0:T(8,128)}, u32[]{:S(2)}) copy-start(f32[4,32,16]{1,2,0:T(8,128)} %copy.79) | copy-start | bytes 24580
  171.5 7.5 %copy-start.20 = (pred[4]{0:T(512)(128)(4,1)S(1)}, pred[4]{0:T(512)(128)(4,1)}, u32[]{:S(2)}) copy-start(pred[4]{0:T(512)(128)(4,1)} %compare_and_fusion.2) | copy-start | bytes 16
  171.5 7.5 %copy-start.25 = (f32[16]{0:T(128)S(1)}, f32[16]{0:T(128)}, u32[]{:S(2)}) copy-start(f32[16]{0:T(128)} %param.33) | copy-start | bytes 196
  179.1 30.5 %copy-start.17 = (f32[1024]{0:T(1024)S(1)}, f32[1024]{0:T(1024)}, u32[]{:S(2)}) copy-start(f32[1024]{0:T(1024)} %param.34) | copy-start | bytes 12292
  219.9 5.1 copy-start.16
  219.9 5.4 copy-start.22
  219.9 306.1 %all-gather.8.cloned.1.call-start = ((), (), s32[]{:S(2)}) async-start(), calls=%async_computation.5 | async-start | bytes 9437184 | tf_op jit(solution)/shard_map/all_gather | solution.py:176
  220.5 426.5 %reduce-scatter.2.cloned.1.call-start = ((), (), s32[]{:S(2)}) async-start(), calls=%async_computation.6 | async-start | bytes 4718592 | tf_op jit(solution)/shard_map/reduce_scatter | solution.py:201
  226.0 152.4 %copy-start.9 = (f32[8192]{0:T(1024)S(1)}, f32[8192]{0:T(1024)}, u32[]{:S(2)}) copy-start(f32[8192]{0:T(1024)} %param.38) | copy-start | bytes 98308
  377.8 4.4 copy-start.1
  475.4 8.9 %copy-start.6 = (bf16[4,64,1024]{2,1,0:T(8,128)(2,1)S(1)}, bf16[4,64,1024]{2,1,0:T(8,128)(2,1)}, u32[]{:S(2)}) copy-start(bf16[4,64,1024]{2,1,0:T(8,128)(2,1)} %gather_fusion.3) | copy-start | bytes 1572868
  475.4 8.9 %copy-start.11 = (bf16[4,32,64]{2,1,0:T(8,128)(2,1)S(1)}, bf16[4,32,64]{2,1,0:T(8,128)(2,1)}, u32[]{:S(2)}) copy-start(bf16[4,32,64]{2,1,0:T(8,128)(2,1)} %get-tuple-element.3) | copy-start | bytes 49156
  (9 other events, 22.9 us)
Sparse Core Ops, SparseCore 0:
  11.4 73.6 all-reduce.4
  87.5 48.4 all-gather.3
  138.2 15.2 all-gather.5
  220.0 154.4 all-reduce.6
  376.7 149.1 all-gather.7
  559.9 87.0 reduce-scatter.1
where the time goes:
time: 667 us; the launch traced here: 656 us
  waiting for transfers between devices  357 us (54%)
  blocking collectives  109 us (16%)
  matrix products  77.8 us (12%)
  local copies, waits for them, and re-layouts  70.9 us (11%)
  other arithmetic  26.3 us (4%)
  between operations  14.9 us (2%)
    psum x1, waiting for transfers between devices, per_device(): lax.psum(jnp.dot(normed, mamba_out_weight, preferred_element_type=jnp.flo...  149 us
    psum x2, blocking collectives, tensor_sum(): return lax.psum(partial_value, 'tensor')  109 us
    reduce_scatter x1, waiting for transfers between devices, per_device(): lax.psum_scatter(lax.dot_general(attention_out_weight, heads_out, (((0,),...  77.6 us
    all_gather x1, waiting for transfers between devices, per_device(): whole_tokens = lax.all_gather(own_tokens, 'tensor', axis=1, tiled=True)  45.7 us
    psum x1, waiting for transfers between devices, tensor_sum(): return lax.psum(partial_value, 'tensor')  43.5 us
    all_gather x1, waiting for transfers between devices, per_device(): every_block = lax.all_gather(key_value_pool, 'tensor', axis=0, tiled=True)  40 us
    unnamed x58, local copies, waits for them, and re-layouts  38.1 us
    dot_general x1, matrix products, per_device(): jnp.dot(whole_tokens, mamba_in_weight.reshape(width, 2 * inner_cols), pre...  17.9 us
  transfers between devices with their start and end apart: 6, of which 5 were waited for; matrix products, arithmetic and copies ran while one was open for 14% of the time, Pallas kernels for 0%

commit v1 on v0

v1 whole, which is shorter than its diff:
```python
import functools

import jax
import jax.numpy as jnp
from jax import lax
from jax.experimental import pallas as pl
from jax.experimental.pallas import tpu as pltpu
from jax.sharding import PartitionSpec as P

HDIM = 64
STATE = 256
QUERY_HEADS = 64
KEY_HEADS = 8
HEAD_SIZE = 128

epsilon = 1e-05
adapter_scale = 2.0
highest = lax.Precision.HIGHEST
f32 = jnp.float32
bf16 = jnp.bfloat16
VMEM_BYTES = 56 << 20


def ring_order(n):
    cols = 1
    for c in range(2, n):
        if n % c == 0 and (n // c) % 2 == 0 and c <= n // c:
            cols = c
    if cols == 1:
        return list(range(n))
    rows = n // cols
    order = [r * cols for r in range(rows)]
    for k, r in enumerate(reversed(range(rows))):
        across = list(range(1, cols))
        order += [r * cols + c for c in (across if k % 2 == 0 else across[::-1])]
    return order


class Ring:
    def __init__(self, n):
        self.n = n
        self.order = ring_order(n)
        place = {d: i for i, d in enumerate(self.order)}
        self.table = [[self.order[(place[d] + s) % n] for s in range(n)] for d in range(n)]
        self.cw = [(self.order[i], self.order[(i + 1) % n]) for i in range(n)]
        self.ccw = [(self.order[i], self.order[(i - 1) % n]) for i in range(n)]

    def near(self):
        me = lax.axis_index("tensor")
        return lax.dynamic_slice_in_dim(jnp.array(self.table, jnp.int32), me, 1, 0)[0]

    def right(self, x):
        return lax.ppermute(x, "tensor", self.cw)

    def left(self, x):
        return lax.ppermute(x, "tensor", self.ccw)

    def gather(self, x):
        n, half = self.n, self.n // 2
        h = x.shape[0] // 2
        stages = [[(0, x)]]
        a = b = x
        for s in range(1, half):
            a, b = self.right(a), self.left(b)
            stages.append([(n - s, a), (s, b)])
        last = jnp.concatenate([self.right(a[:h]), self.left(b[h:])], axis=0)
        stages.append([(half, last)])
        return stages

    def reduce(self, part):
        n, half = self.n, self.n // 2
        p = part(half).astype(bf16)
        h = p.shape[0] // 2
        a, b = self.right(p[:h]), self.left(p[h:])
        for d in range(half - 1, 0, -1):
            pa, pb = part(d), part(n - d)
            if d == half - 1:
                pa = jnp.concatenate([pa[:h] + a.astype(f32), pa[h:]], axis=0)
                pb = jnp.concatenate([pb[:h], pb[h:] + b.astype(f32)], axis=0)
            else:
                pa, pb = pa + a.astype(f32), pb + b.astype(f32)
            a, b = self.right(pa.astype(bf16)), self.left(pb.astype(bf16))
        own = part(0)
        if half == 1:
            return own + jnp.concatenate([a, b], axis=0).astype(f32)
        return own + a.astype(f32) + b.astype(f32)

    def masks(self):
        m, found = 1, []
        while m < self.n:
            found.append([(i, i ^ m) for i in range(self.n)])
            m *= 2
        return found

    def total(self, x):
        for pairs in self.masks():
            x = x + lax.ppermute(x, "tensor", pairs)
        return x

    def total_halves(self, x):
        pairs = self.masks()
        me = lax.axis_index("tensor")
        h = x.shape[0] // 2
        odd = (me % 2) == 1
        keep = jnp.where(odd, x[h:], x[:h])
        give = jnp.where(odd, x[:h], x[h:])
        keep = keep + lax.ppermute(give, "tensor", pairs[0])
        for p in pairs[1:]:
            keep = keep + lax.ppermute(keep, "tensor", p)
        other = lax.ppermute(keep, "tensor", pairs[0])
        return jnp.where(
            odd, jnp.concatenate([other, keep], axis=0), jnp.concatenate([keep, other], axis=0)
        )


def in_kernel(count, steps, first_call, which, *refs):
    blocks = refs[:count]
    w_ref = refs[count]
    o_ref = refs[-2]
    spread = refs[-1]
    j, k = pl.program_id(0), pl.program_id(1)
    kb = w_ref.shape[0]
    rows = blocks[0].shape[0]

    @pl.when((j == 0) & (k == 0))
    def _():
        if first_call:
            o_ref[...] = jnp.zeros_like(o_ref)
        else:
            o_ref[...] = refs[count + 1][...]

    lane = lax.broadcasted_iota(jnp.int32, (128, 512), 1)
    sub = lax.broadcasted_iota(jnp.int32, (128, 512), 0)
    target = jnp.where(lane < 256, 2 * sub, 2 * sub + 257)
    widen = jnp.where(lane == target, 1.0, 0.0).astype(bf16)

    for b in range(count):
        for s in range(steps):

            @pl.when((j == b) & (k == s))
            def _():
                for p in range(kb // 128):
                    piece = blocks[b][:, s * kb + p * 128 : s * kb + (p + 1) * 128]
                    both = jnp.dot(piece, widen, preferred_element_type=f32).astype(bf16)
                    spread[:rows, p * 256 : (p + 1) * 256] = both[:, :256]
                    spread[rows:, p * 256 : (p + 1) * 256] = both[:, 256:]

    w = w_ref[...].reshape(2 * kb, w_ref.shape[2])
    o_ref[...] += jnp.dot(spread[...], w, preferred_element_type=f32)


def in_product(ids, blocks, weight, acc):
    count = len(blocks)
    rows, depth = blocks[0].shape
    cols = weight.shape[2]
    kb = min(512, depth)
    steps = depth // kb
    in_specs = [pl.BlockSpec((rows, depth), lambda j, k, w: (0, 0)) for _ in blocks]
    in_specs.append(pl.BlockSpec((kb, 2, cols), lambda j, k, w: (w[j] * steps + k, 0, 0)))
    operands = [ids, *blocks, weight]
    aliases = {}
    if acc is not None:
        in_specs.append(pl.BlockSpec((2 * rows, cols), lambda j, k, w: (0, 0)))
        operands.append(acc)
        aliases = {len(operands) - 1: 0}
    return pl.pallas_call(
        functools.partial(in_kernel, count, steps, acc is None),
        grid_spec=pltpu.PrefetchScalarGridSpec(
            num_scalar_prefetch=1,
            grid=(count, steps),
            in_specs=in_specs,
            out_specs=pl.BlockSpec((2 * rows, cols), lambda j, k, w: (0, 0)),
            scratch_shapes=[pltpu.VMEM((2 * rows, 2 * kb), bf16)],
        ),
        out_shape=jax.ShapeDtypeStruct((2 * rows, cols), f32),
        input_output_aliases=aliases,
        compiler_params=pltpu.CompilerParams(vmem_limit_bytes=VMEM_BYTES),
        cost_estimate=pl.CostEstimate(
            flops=count * 8 * rows * depth * cols,
            bytes_accessed=count * depth * cols * 8,
            transcendentals=0,
        ),
        name="in_product",
    )(*operands)


def shifted(history, x, k):
    if k == 3:
        return x
    return jnp.concatenate([history[k:3], x[: x.shape[0] - 3 + k]], axis=0)


def conv_silu(history, x, taps):
    total = taps[0:1] * shifted(history, x, 0)
    for k in range(1, 4):
        total = total + taps[k : k + 1] * shifted(history, x, k)
    return total * jax.nn.sigmoid(total)


def spans(heads, width):
    lane = lax.broadcasted_iota(jnp.int32, (heads, heads * width), 1)
    row = lax.broadcasted_iota(jnp.int32, (heads, heads * width), 0)
    return jnp.where(lane // width == row, 1.0, 0.0).astype(f32)


def state_kernel(
    own_id,
    far_id,
    is_own,
    x_ref,
    z_ref,
    bc_ref,
    raw_ref,
    hx_ref,
    hbc_ref,
    tx_ref,
    tbc_ref,
    bias_ref,
    rate_ref,
    skip_ref,
    gain_ref,
    own_ref,
    far_ref,
    gated_ref,
    energy_ref,
    final_ref,
    initial,
):
    i = pl.program_id(0)

    @pl.when(is_own[i] == 1)
    def _():
        initial[...] = own_ref[0]

    @pl.when(is_own[i] == 0)
    def _():
        initial[...] = far_ref[0].astype(f32)

    length = x_ref.shape[0]
    heads = raw_ref.shape[1]
    values = conv_silu(hx_ref[0], x_ref[...].astype(bf16).astype(f32), tx_ref[...])
    bc = conv_silu(hbc_ref[0], bc_ref[...], tbc_ref[...])
    in_state = bc[:, :STATE].astype(bf16)
    out_state = bc[:, STATE:].astype(bf16)
    raw = raw_ref[...] + bias_ref[...]
    steps = jnp.maximum(raw, 0.0) + jnp.log1p(jnp.exp(-jnp.abs(raw)))
    log_decay = -steps * jnp.exp(rate_ref[...])
    row = lax.broadcasted_iota(jnp.int32, (length, length), 0)
    col = lax.broadcasted_iota(jnp.int32, (length, length), 1)
    lower = jnp.where(row >= col, 1.0, 0.0).astype(f32)
    running = jnp.dot(lower, log_decay, precision=highest, preferred_element_type=f32)
    last = running[length - 1 : length]

    wide = spans(heads, length)
    both = jnp.dot(
        jnp.concatenate([running, steps], axis=0), wide, precision=highest, preferred_element_type=f32
    )
    run_t, step_t = both[:length], both[length:]
    lane = lax.broadcasted_iota(jnp.int32, (length, heads * length), 1) % length
    place = lax.broadcasted_iota(jnp.int32, (length, heads * length), 0)
    diagonal = lane == place
    run_s = jnp.sum(jnp.where(diagonal, run_t, 0.0), axis=0, keepdims=True)
    step_s = jnp.sum(jnp.where(diagonal, step_t, 0.0), axis=0, keepdims=True)
    seen = place >= lane
    decays = jnp.where(seen, jnp.exp(jnp.where(seen, run_t - run_s, 0.0)), 0.0)
    overlap = lax.dot_general(
        out_state,
        jnp.concatenate([in_state] * heads, axis=0),
        (((1,), (1,)), ((), ())),
        preferred_element_type=f32,
    )
    mixing = (overlap * decays * step_s).astype(bf16)
    short = values.astype(bf16)
    group = min(4, heads)
    gl, gw = group * length, group * HDIM
    own_block = (
        lax.broadcasted_iota(jnp.int32, (gl, gw), 0) // length
        == lax.broadcasted_iota(jnp.int32, (gl, gw), 1) // HDIM
    )
    within = []
    for g in range(heads // group):
        v = jnp.concatenate([values[:, g * gw : (g + 1) * gw]] * group, axis=0)
        v = jnp.where(own_block, v, 0.0).astype(bf16)
        within.append(jnp.dot(mixing[:, g * gl : (g + 1) * gl], v, preferred_element_type=f32))
    within = within[0] if len(within) == 1 else jnp.concatenate(within, axis=1)

    narrow = spans(heads, HDIM)
    scales = jnp.dot(
        jnp.concatenate([jnp.exp(running), jnp.exp(last - running) * steps], axis=0),
        narrow,
        precision=highest,
        preferred_element_type=f32,
    )
    start = initial[...]
    carried = lax.dot_general(
        out_state, start.astype(bf16), (((1,), (1,)), ((), ())), preferred_element_type=f32
    )
    result = within + carried * scales[:length] + skip_ref[...] * values
    z = z_ref[...].astype(bf16).astype(f32)
    gated = result * (z * jax.nn.sigmoid(z))
    energy_ref[...] = jnp.sum(gated * gated, axis=1, keepdims=True)
    gated_ref[...] = (gated * gain_ref[...]).astype(bf16)

    kept = jnp.exp(
        lax.dot_general(
            log_decay,
            jnp.ones((length, STATE), f32),
            (((0,), (0,)), ((), ())),
            precision=highest,
            preferred_element_type=f32,
        )
    )
    update = lax.dot_general(
        (values * scales[length:]).astype(bf16),
        in_state,
        (((0,), (0,)), ((), ())),
        preferred_element_type=f32,
    )
    for h in range(heads):
        at = slice(h * HDIM, (h + 1) * HDIM)
        final_ref[0, at, :] = update[at] + start[at] * kept[h : h + 1]


def state_pass(
    inner, bc, raw, hx, hbc, tx, tbc, bias, rate, skip, gain, own_pool, far_pool, own_id, far_id, is_own
):
    tenants = own_id.shape[0]
    length = raw.shape[0] // tenants
    heads = raw.shape[1]
    cols = inner.shape[1]

    def rows(width):
        return pl.BlockSpec((length, width), lambda i, *s: (i, 0))

    def whole(a):
        return pl.BlockSpec(a.shape, lambda i, *s: (0,) * a.ndim)

    pooled = (1, cols, STATE)
    return pl.pallas_call(
        state_kernel,
        grid_spec=pltpu.PrefetchScalarGridSpec(
            num_scalar_prefetch=3,
            grid=(tenants,),
            in_specs=[
                rows(cols),
                pl.BlockSpec((length, cols), lambda i, *s: (tenants + i, 0)),
                rows(2 * STATE),
                rows(heads),
                pl.BlockSpec((1, 3, cols), lambda i, *s: (i, 0, 0)),
                pl.BlockSpec((1, 3, 2 * STATE), lambda i, *s: (i, 0, 0)),
                whole(tx),
                whole(tbc),
                whole(bias),
                whole(rate),
                whole(skip),
                whole(gain),
                pl.BlockSpec(pooled, lambda i, own, far, is_own: (own[i], 0, 0)),
                pl.BlockSpec(pooled, lambda i, own, far, is_own: (far[i], 0, 0)),
            ],
            out_specs=[
                rows(cols),
                rows(1),
                pl.BlockSpec(pooled, lambda i, *s: (i, 0, 0)),
            ],
            scratch_shapes=[pltpu.VMEM((cols, STATE), f32)],
        ),
        out_shape=[
            jax.ShapeDtypeStruct((tenants * length, cols), bf16),
            jax.ShapeDtypeStruct((tenants * length, 1), f32),
            jax.ShapeDtypeStruct((tenants, cols, STATE), f32),
        ],
        compiler_params=pltpu.CompilerParams(vmem_limit_bytes=VMEM_BYTES),
        cost_estimate=pl.CostEstimate(
            flops=tenants * 6 * length * cols * STATE,
            bytes_accessed=tenants * cols * STATE * 10,
            transcendentals=0,
        ),
        name="state_pass",
    )(
        own_id, far_id, is_own, inner, inner, bc, raw, hx, hbc, tx, tbc, bias, rate, skip, gain,
        own_pool, far_pool,
    )


def attend_kernel(
    table, limit, adapter, core, q_ref, low_ref, fresh_ref, norm_ref, up_ref, near_ref, far_ref, o_ref
):
    i = pl.program_id(0)
    length = q_ref.shape[0]
    heads = q_ref.shape[1] // HEAD_SIZE
    blocks = table.shape[1]
    part = near_ref.shape[1]
    norm = norm_ref[...]
    low = (low_ref[...] * norm).astype(bf16)
    raised = jnp.dot(low, up_ref[0], preferred_element_type=f32)
    q = (q_ref[...] * norm + adapter_scale * raised).astype(bf16)
    q = jnp.concatenate([q[:, h * HEAD_SIZE : (h + 1) * HEAD_SIZE] for h in range(heads)], axis=0)
    fresh = (fresh_ref[...] * norm).astype(bf16)
    pieces = []
    for j in range(blocks):
        at = table[i, j]
        pieces += [near_ref[at], far_ref[at]]
    cached = jnp.concatenate(pieces, axis=0)
    context = cached.shape[0]
    nt = (((1,), (1,)), ((), ()))
    scale = HEAD_SIZE ** (-0.5)
    old = lax.dot_general(q, cached[:, :HEAD_SIZE], nt, preferred_element_type=f32) * scale
    new = lax.dot_general(q, fresh[:, :HEAD_SIZE], nt, preferred_element_type=f32) * scale
    lane = lax.broadcasted_iota(jnp.int32, old.shape, 1)
    inside = lane % (2 * part)
    far_side = jnp.where(inside >= part, 1, 0)
    half = jnp.where(core[0] == 0, far_side, 1 - far_side)
    place = (lane // (2 * part)) * (2 * part) + half * part + inside % part
    old_seen = place < limit[i]
    token = lax.broadcasted_iota(jnp.int32, new.shape, 0) % length
    new_seen = lax.broadcasted_iota(jnp.int32, new.shape, 1) <= token
    old = jnp.where(old_seen, old, -jnp.inf)
    new = jnp.where(new_seen, new, -jnp.inf)
    top = jnp.maximum(jnp.max(old, axis=1, keepdims=True), jnp.max(new, axis=1, keepdims=True))
    old = jnp.where(old_seen, jnp.exp(old - top), 0.0)
    new = jnp.where(new_seen, jnp.exp(new - top), 0.0)
    share = 1.0 / (jnp.sum(old, axis=1, keepdims=True) + jnp.sum(new, axis=1, keepdims=True))
    out = jnp.dot((old * share).astype(bf16), cached[:, HEAD_SIZE:], preferred_element_type=f32)
    out += jnp.dot((new * share).astype(bf16), fresh[:, HEAD_SIZE:], preferred_element_type=f32)
    out = out.astype(bf16)
    for h in range(heads):
        o_ref[:, h * HEAD_SIZE : (h + 1) * HEAD_SIZE] = out[h * length : (h + 1) * length]


def attend(table, limit, adapter, core, q, low, fresh, norm, up, near, far):
    tenants = table.shape[0]
    length = q.shape[0] // tenants
    cols = q.shape[1]

    def rows(a):
        return pl.BlockSpec((length, a.shape[1]), lambda i, *s: (i, 0))

    def whole(a):
        return pl.BlockSpec(a.shape, lambda i, *s: (0,) * a.ndim)

    return pl.pallas_call(
        attend_kernel,
        grid_spec=pltpu.PrefetchScalarGridSpec(
            num_scalar_prefetch=4,
            grid=(tenants,),
            in_specs=[
                rows(q),
                rows(low),
                rows(fresh),
                rows(norm),
                pl.BlockSpec((1, *up.shape[1:]), lambda i, t, n, a, c: (a[i], 0, 0)),
                whole(near),
                whole(far),
            ],
            out_specs=rows(q),
        ),
        out_shape=jax.ShapeDtypeStruct(q.shape, bf16),
        compiler_params=pltpu.CompilerParams(vmem_limit_bytes=VMEM_BYTES),
        cost_estimate=pl.CostEstimate(
            flops=tenants * 4 * length * cols * 288,
            bytes_accessed=near.size * 4 + q.size * 6 + up.size,
            transcendentals=0,
        ),
        name="attend",
    )(table, limit, adapter, core, q, low, fresh, norm, up, near, far)


def per_device(
    ring,
    pools,
    tokens,
    mamba_in_weight,
    state_projection,
    inner_taps,
    state_taps,
    inner_history,
    state_history,
    step_size_bias,
    log_decay_rate,
    skip_factor,
    gated_norm_gain,
    mamba_out_weight,
    saved_state_pool,
    tenant_state_slot,
    attention_gain,
    query_matrix,
    adapter_down,
    adapter_up,
    tenant_adapter,
    key_value_weight,
    key_value_pool,
    tenant_blocks,
    cached_length,
    attention_out_weight,
):
    n = ring.n
    tenants, length, depth = tokens.shape
    me = lax.axis_index("tensor")
    core = lax.axis_index("pool")
    rows = tenants * length
    width = depth * n
    own_tokens = tokens.reshape(rows, depth)
    near = ring.near()
    heads = step_size_bias.shape[0]
    cols = mamba_in_weight.shape[2]

    stages = ring.gather(own_tokens)
    projected = ring.total_halves(
        jnp.dot(own_tokens, state_projection, preferred_element_type=f32)
    )
    inner = None
    for stage in stages:
        ids = jnp.stack([near[s] for s, _ in stage])
        inner = in_product(ids, [x for _, x in stage], mamba_in_weight, inner)

    slots = saved_state_pool.shape[0]
    flat_pool = saved_state_pool.reshape(slots, heads * HDIM, STATE)
    far_pool = lax.ppermute(
        flat_pool.astype(bf16), "pool", [(i, (i + 1) % pools) for i in range(pools)]
    )
    local_slot = tenant_state_slot - core * slots
    is_own = ((local_slot >= 0) & (local_slot < slots)).astype(jnp.int32)
    own_id = jnp.clip(local_slot, 0, slots - 1)
    far_id = jnp.clip(tenant_state_slot - (1 - core) * slots, 0, slots - 1)

    local_heads = query_matrix.shape[1] // HEAD_SIZE
    group_size = QUERY_HEADS // KEY_HEADS
    count, block_len, _ = key_value_pool.shape
    part = block_len // pools
    mine = lax.dynamic_slice_in_dim(key_value_pool, core * part, part, 1)
    mine = mine.reshape(count, part, 2, KEY_HEADS, HEAD_SIZE).transpose(3, 0, 1, 2, 4)
    mine = mine.reshape(KEY_HEADS, count, part, 2 * HEAD_SIZE)

    def for_device(d):
        return lax.dynamic_index_in_dim(mine, d * local_heads // group_size, 0, keepdims=False)

    if n <= 8:
        got = [for_device(me)]
        for s in range(1, n):
            got.append(
                lax.ppermute(
                    for_device((me + s) % n), "tensor", [(i, (i + s) % n) for i in range(n)]
                )
            )
        cache = jnp.concatenate(got, axis=0)
        owner = (me - tenant_blocks // count) % n
    else:
        every = jnp.stack([mine[d * local_heads // group_size] for d in range(n)])
        cache = lax.all_to_all(every, "tensor", 0, 0, tiled=True)
        cache = cache.reshape(n * count, part, 2 * HEAD_SIZE)
        owner = tenant_blocks // count
    table = owner * count + tenant_blocks % count
    far_cache = lax.ppermute(cache, "pool", [(i, (i + 1) % pools) for i in range(pools)])

    raw = lax.dynamic_slice_in_dim(projected, 2 * STATE + me * heads, heads, 1)
    gated, energy, final_state = state_pass(
        inner,
        projected,
        raw,
        inner_history.astype(f32),
        state_history,
        inner_taps.astype(f32),
        state_taps.astype(f32),
        step_size_bias[None],
        log_decay_rate[None],
        jnp.repeat(skip_factor, HDIM)[None],
        gated_norm_gain[None],
        flat_pool,
        far_pool,
        own_id,
        far_id,
        is_own,
    )
    energy = ring.total(energy)

    def out_part(left_side, weight):
        def part(s):
            block = lax.dynamic_slice_in_dim(weight, near[s] * depth, depth, 1)
            return jnp.dot(left_side, block, preferred_element_type=f32)

        return part

    mixed = ring.reduce(out_part(gated, mamba_out_weight))
    scale = lax.rsqrt(energy / (cols * n) + epsilon)
    first = (own_tokens.astype(f32) + mixed * scale).astype(bf16)
    wide_first = lax.optimization_barrier(first).astype(f32)
    gain = lax.dynamic_slice_in_dim(attention_gain, me * depth, depth, 0)
    attn_own = (wide_first * gain).astype(bf16)

    stages = ring.gather(attn_own)
    picked_down = jnp.take(adapter_down, tenant_adapter, axis=0)
    low = jnp.einsum(
        "bld,bdr->blr",
        attn_own.reshape(tenants, length, depth),
        picked_down,
        preferred_element_type=f32,
    ).reshape(rows, -1)
    rank = low.shape[1]
    square = jnp.sum(wide_first * wide_first, axis=-1, keepdims=True)
    sums = ring.total(jnp.concatenate([low, square], axis=1))
    kv = jnp.dot(attn_own, key_value_weight, preferred_element_type=f32)

    def kv_part(s):
        head = near[s] * local_heads // group_size
        key = lax.dynamic_slice_in_dim(kv, head * HEAD_SIZE, HEAD_SIZE, 1)
        value = lax.dynamic_slice_in_dim(kv, (KEY_HEADS + head) * HEAD_SIZE, HEAD_SIZE, 1)
        return jnp.concatenate([key, value], axis=1)

    fresh = ring.reduce(kv_part)
    query = None
    for stage in stages:
        for s, x in stage:
            block = lax.dynamic_slice_in_dim(query_matrix, near[s] * depth, depth, 0)
            term = jnp.dot(x, block, preferred_element_type=f32)
            query = term if query is None else query + term
    norm = lax.rsqrt(sums[:, rank:] / width + epsilon)
    heads_out = attend(
        table,
        cached_length,
        tenant_adapter,
        core[None].astype(jnp.int32),
        query,
        sums[:, :rank],
        fresh,
        norm,
        adapter_up,
        cache,
        far_cache,
    )
    out = ring.reduce(out_part(heads_out, attention_out_weight))
    second = (lax.optimization_barrier(first).astype(f32) + out).astype(bf16)
    return (
        second.reshape(tenants, length, depth),
        final_state.reshape(tenants, heads, HDIM, STATE),
    )


def solution(mesh):
    in_specs = (
        P(("groups", "pool"), None, "tensor"),
        P(None, None, "tensor"),
        P("tensor", None),
        P(None, "tensor"),
        P(),
        P(("groups", "pool"), None, "tensor"),
        P(("groups", "pool"), None, None),
        P("tensor"),
        P("tensor"),
        P("tensor"),
        P("tensor"),
        P("tensor", None),
        P(("groups", "pool"), "tensor", None, None),
        P(("groups", "pool")),
        P(),
        P(None, "tensor"),
        P(None, "tensor", None),
        P(None, None, "tensor"),
        P(("groups", "pool")),
        P("tensor", None),
        P(("groups", "tensor"), None, None),
        P(("groups", "pool"), None),
        P(("groups", "pool")),
        P("tensor", None),
    )
    out_specs = (P(("groups", "pool"), None, "tensor"), P(("groups", "pool"), "tensor", None, None))
    ring = Ring(mesh.shape["tensor"])
    return jax.shard_map(
        functools.partial(per_device, ring, mesh.shape["pool"]),
        mesh=mesh,
        in_specs=in_specs,
        out_specs=out_specs,
        check_vma=False,
    )
```

time: 667 us -> 281 us (0.42); the launches traced: 656 us -> 280 us
  waiting for transfers between devices: 357 us -> 73 us
  blocking collectives: 109 us -> 0 us
  local copies, waits for them, and re-layouts: 70.9 us -> 6.98 us
  starting transfers between devices: 0.24 us -> 59.9 us
  Pallas kernels: 0 us -> 52.7 us
  matrix products: 77.8 us -> 56.4 us
  other arithmetic: 26.3 us -> 18.5 us
    psum x2 -> x0, waiting for transfers between devices: 192 us -> none  [the longest x1 149 us: per_device(): lax.psum(jnp.dot(normed, mamba_out_weight, preferred_element_type=jnp.flo...]
    psum x2 -> x0, blocking collectives: 109 us -> none  [tensor_sum(): return lax.psum(partial_value, 'tensor')]
    all_gather x3 -> x0, waiting for transfers between devices: 85.7 us -> none  [the longest x1 45.7 us: per_device(): whole_tokens = lax.all_gather(own_tokens, 'tensor', axis=1, tiled=True)]
    reduce_scatter x1 -> x0, waiting for transfers between devices: 77.6 us -> none  [per_device(): lax.psum_scatter(lax.dot_general(attention_out_weight, heads_out, (((0,),...]
    ppermute x0 -> x59, waiting for transfers between devices: none -> 73 us  [the longest x20 26.7 us: right(): return lax.ppermute(x, 'tensor', self.cw)]
    ppermute x0 -> x59, starting transfers between devices: none -> 59.9 us  [the longest x20 24.5 us: right(): return lax.ppermute(x, 'tensor', self.cw)]
    pallas_call x0 -> x7, Pallas kernels: none -> 52.7 us  [the longest x5 37.4 us: in_product(): pl.pallas_call(functools.partial(in_kernel, count, steps, acc is None), g...]
    unnamed x58 -> x61, local copies, waits for them, and re-layouts: 38.1 us -> 0.9 us
  transfers between devices with their start and end apart: 6 -> 59, of which waited for: 5 -> 29; matrix products, arithmetic and copies ran while one was open for 14% -> 27% of each run, Pallas kernels for 0% -> 17%
where the time goes in v1:
time: 281 us; the launch traced here: 280 us
  waiting for transfers between devices  73 us (26%)
  starting transfers between devices  59.9 us (21%)
  matrix products  56.4 us (20%)
  Pallas kernels  52.7 us (19%)
  other arithmetic  18.5 us (7%)
  between operations  12.1 us (4%)
  local copies, waits for them, and re-layouts  6.98 us (2%)
    pallas_call x5, Pallas kernels, in_product(): pl.pallas_call(functools.partial(in_kernel, count, steps, acc is None), g...  37.4 us
    dot_general x16, matrix products, part(): return jnp.dot(left_side, block, preferred_element_type=f32)  34.1 us
    ppermute x20, waiting for transfers between devices, right(): return lax.ppermute(x, 'tensor', self.cw)  26.7 us
    ppermute x20, waiting for transfers between devices, left(): return lax.ppermute(x, 'tensor', self.ccw)  26.5 us
    ppermute x20, starting transfers between devices, right(): return lax.ppermute(x, 'tensor', self.cw)  24.5 us
    dot_general x8, matrix products, per_device(): term = jnp.dot(x, block, preferred_element_type=f32)  17.3 us
    ppermute x20, starting transfers between devices, left(): return lax.ppermute(x, 'tensor', self.ccw)  13.6 us
    ppermute x6, waiting for transfers between devices, total(): x = x + lax.ppermute(x, 'tensor', pairs)  10.9 us
  transfers between devices with their start and end apart: 59, of which 29 were waited for; matrix products, arithmetic and copies ran while one was open for 27% of the time, Pallas kernels for 17%

profile of v1, /device:TPU:0, one launch (start us, length us, event | category | flops | bytes accessed | tf_op | source)
XLA Modules:
  0.0 279.6 jit_solution(16691399454603964019)
XLA Ops:
  0.6 3.0 %collective-permute-start.4 = (bf16[128,1024]{1,0:T(8,128)(2,1)}, bf16[128,1024]{1,0:T(8,128)(2,1)}, u32[]{:S(2)}, u32[]{:S(2)}) collective-permute-start(bf16[128,1024]{1,0:T(8,128)(2,1)} %bitcast.88), channel_id=1, source_target_pairs={{0,2},{4,0},{8,4},{12,8},{14,12},{10,14},{6,10},{2,6},{1,3},{5,1},... | collective-permute-start | bytes 786440 | tf_op jit(solution)/shard_map/ppermute | solution.py:56
  8.2 4.8 %bitcast_convert_fusion = bf16[6,1024,256]{2,1,0:T(8,128)(2,1)} fusion(f32[6,16,64,256]{3,2,1,0:T(8,128)} %param.37), kind=kLoop, calls=%fused_computation.231 | loop fusion | flops 1572864 | bytes 9437184 | tf_op jit(solution)/shard_map/convert_element_type | solution.py:519
  24.5 5.5 %in_product.5.refs_3_ = f32[256,1024]{1,0:T(8,128)} custom-call(s32[1]{0:T(128)} %bitcast.8.which, bf16[128,1024]{1,0:T(8,128)(2,1)} %bitcast.91, bf16[8192,2,1024]{2,1,0:T(2,128)(2,1)} %refs_1_.3), custom_call_target="tpu_custom_call" | custom-call | flops 1073741824 | bytes 8388608 | tf_op jit(solution)/shard_map/in_product/pallas_call | solution.py:166
  46.1 3.6 %collective-permute-start.45 = (bf16[8,16,256]{2,1,0:T(8,128)(2,1)}, bf16[8,16,256]{2,1,0:T(8,128)(2,1)S(1)}, u32[]{:S(2)}, u32[]{:S(2)}) collective-permute-start(bf16[8,16,256]{2,1,0:T(8,128)(2,1)} %get-tuple-element.28), channel_id=1, source_target_pairs={{0,6},{2,8},{4,10},{6,12},{8,14},{10,0},{12,2},{14,4},{1,7},{3,9},... | collective-permute-start | bytes 196616 | tf_op jit(solution)/shard_map/ppermute | solution.py:541
  50.9 3.7 %collective-permute-done.45 = bf16[8,16,256]{2,1,0:T(8,128)(2,1)S(1)} collective-permute-done((bf16[8,16,256]{2,1,0:T(8,128)(2,1)}, bf16[8,16,256]{2,1,0:T(8,128)(2,1)S(1)}, u32[]{:S(2)}, u32[]{:S(2)}) %collective-permute-start.45) | collective-permute-done | bytes 65568 | tf_op jit(solution)/shard_map/ppermute | solution.py:541
  59.7 8.7 %in_product.6.refs_3_ = f32[256,1024]{1,0:T(8,128)} custom-call(s32[2]{0:T(128)} %pad_add_fusion.2.which, bf16[128,1024]{1,0:T(8,128)(2,1)} %collective-permute-done.refs_0_, bf16[128,1024]{1,0:T(8,128)(2,1)} %collective-permute-done.4.refs_1_, bf16[8192,2,1024]{2,1,0:T(2,128)(2,1)} %refs_1_.3, ...), custom_call_target="tpu_custom_call", output_to_operand_aliasing={{}: (4, {})} | custom-call | flops 2147483648 | bytes 16777216 | tf_op jit(solution)/shard_map/in_product/pallas_call | solution.py:166
  68.4 3.9 %collective-permute-done.10 = f32[64,640]{1,0:T(8,128)S(1)} collective-permute-done((f32[64,640]{1,0:T(8,128)S(1)}, f32[64,640]{1,0:T(8,128)S(1)}, u32[]{:S(2)}, u32[]{:S(2)}) %collective-permute-start.10) | collective-permute-done | bytes 163872 | tf_op jit(solution)/shard_map/ppermute | solution.py:109
  75.8 8.7 %in_product.7.refs_3_ = f32[256,1024]{1,0:T(8,128)} custom-call(s32[2]{0:T(128)} %pad_add_fusion.1.which, bf16[128,1024]{1,0:T(8,128)(2,1)} %copy-done.10, bf16[128,1024]{1,0:T(8,128)(2,1)} %copy-done.11, bf16[8192,2,1024]{2,1,0:T(2,128)(2,1)} %refs_1_.3, f32[256,1024]{1,0:T(8,128)} %in_product.6.refs_3_), custom_call_target="tpu_custom_call", output_to_operand_aliasing={{}: (4, {})} | custom-call | flops 2147483648 | bytes 16777216 | tf_op jit(solution)/shard_map/in_product/pallas_call | solution.py:166
  89.3 8.7 %in_product.8.refs_2_ = f32[256,1024]{1,0:T(8,128)} custom-call(s32[2]{0:T(128)} %pad_add_fusion.which, bf16[128,1024]{1,0:T(8,128)(2,1)} %copy-done.8, bf16[128,1024]{1,0:T(8,128)(2,1)} %copy-done.7, bf16[8192,2,1024]{2,1,0:T(2,128)(2,1)} %refs_1_.3, f32[256,1024]{1,0:T(8,128)} %in_product.7.refs_3_), custom_call_target="tpu_custom_call", output_to_operand_aliasing={{}: (4, {})} | custom-call | flops 2147483648 | bytes 16777216 | tf_op jit(solution)/shard_map/in_product/pallas_call | solution.py:166
  101.5 5.8 %in_product.9.x_ref.z_ref = f32[256,1024]{1,0:T(8,128)} custom-call(s32[1]{0:T(128)} %bitcast.1.which, bf16[128,1024]{1,0:T(8,128)(2,1)} %pad_maximum_fusion.refs_0_, bf16[8192,2,1024]{2,1,0:T(2,128)(2,1)} %refs_1_.3, f32[256,1024]{1,0:T(8,128)} %in_product.8.refs_2_), custom_call_target="tpu_custom_call", output_to_operand_aliasing={{}: (3, {})} | custom-call | flops 1073741824 | bytes 8388608 | tf_op jit(solution)/shard_map/in_product/pallas_call | solution.py:166
  107.3 8.9 %state_pass.1 = (bf16[128,1024]{1,0:T(8,128)(2,1)}, f32[128,1]{1,0:T(8,128)}, f32[4,1024,256]{2,1,0:T(8,128)}) custom-call(s32[4]{0:T(128)} %get-tuple-element.48.own_id, s32[4]{0:T(128)} %get-tuple-element.47.far_id, s32[4]{0:T(128)} %and_convert_fusion.is_own, f32[256,1024]{1,0:T(8,128)} %in_product.9.x_ref.z_ref, f32[256,1024]{1,0:T(8,128)} %in_product.9.x_ref.z_ref, ...), custom_call_target="tpu_custom_call" | custom-call | flops 201326592 | bytes 10485760 | tf_op jit(solution)/shard_map/state_pass/pallas_call | solution.py:339
  125.9 6.1 %collective-permute-done.13 = bf16[64,1024]{1,0:T(8,128)(2,1)S(1)} collective-permute-done((bf16[64,1024]{1,0:T(8,128)(2,1)S(1)}, bf16[64,1024]{1,0:T(8,128)(2,1)S(1)}, u32[]{:S(2)}, u32[]{:S(2)}) %collective-permute-start.13) | collective-permute-done | bytes 131104 | tf_op jit(solution)/shard_map/ppermute | solution.py:53
  134.1 6.6 %collective-permute-done.18 = bf16[128,1024]{1,0:T(8,128)(2,1)S(1)} collective-permute-done((bf16[128,1024]{1,0:T(8,128)(2,1)S(1)}, bf16[128,1024]{1,0:T(8,128)(2,1)S(1)}, u32[]{:S(2)}, u32[]{:S(2)}) %collective-permute-start.18) | collective-permute-done | bytes 262176 | tf_op jit(solution)/shard_map/ppermute | solution.py:56
  147.9 3.7 %collective-permute-done.19 = bf16[128,1024]{1,0:T(8,128)(2,1)S(1)} collective-permute-done((bf16[128,1024]{1,0:T(8,128)(2,1)S(1)}, bf16[128,1024]{1,0:T(8,128)(2,1)S(1)}, u32[]{:S(2)}, u32[]{:S(2)}) %collective-permute-start.19) | collective-permute-done | bytes 262176 | tf_op jit(solution)/shard_map/ppermute | solution.py:56
  159.4 4.5 %collective-permute-done.23 = f32[128,1]{1,0:T(8,128)S(1)} collective-permute-done((f32[128,1]{1,0:T(8,128)S(1)}, f32[128,1]{1,0:T(8,128)S(1)}, u32[]{:S(2)}, u32[]{:S(2)}) %collective-permute-start.23) | collective-permute-done | bytes 544 | tf_op jit(solution)/shard_map/ppermute | solution.py:97
  166.4 3.1 %collective-permute-start.25 = (bf16[128,1024]{1,0:T(8,128)(2,1)S(1)}, bf16[128,1024]{1,0:T(8,128)(2,1)}, u32[]{:S(2)}, u32[]{:S(2)}) collective-permute-start(bf16[128,1024]{1,0:T(8,128)(2,1)S(1)} %get-tuple-element.34), channel_id=1, source_target_pairs={{0,2},{4,0},{8,4},{12,8},{14,12},{10,14},{6,10},{2,6},{1,3},{5,1},... | collective-permute-start | bytes 786440 | tf_op jit(solution)/shard_map/ppermute | solution.py:56
  174.1 2.9 %fusion.214 = f32[128,2048]{1,0:T(8,128)S(1)} fusion(bf16[128,1024]{1,0:T(8,128)(2,1)S(1)} %get-tuple-element.34, bf16[1024,2048]{1,0:T(8,128)(2,1)} %param.44), kind=kOutput, calls=%fused_computation.237 | convolution fusion | flops 536870912 | bytes 5505024 | tf_op jit(solution)/shard_map/dot_general | solution.py:601
  177.3 4.1 %collective-permute-done.39 = bf16[64,256]{1,0:T(8,128)(2,1)S(1)} collective-permute-done((bf16[64,256]{1,0:T(8,128)(2,1)S(1)}, bf16[64,256]{1,0:T(8,128)(2,1)S(1)}, u32[]{:S(2)}, u32[]{:S(2)}) %collective-permute-start.39) | collective-permute-done | bytes 32800 | tf_op jit(solution)/shard_map/ppermute | solution.py:56
  181.4 3.9 %collective-permute-done.35 = bf16[64,256]{1,0:T(8,128)(2,1)S(1)} collective-permute-done((bf16[64,256]{1,0:T(8,128)(2,1)S(1)}, bf16[64,256]{1,0:T(8,128)(2,1)S(1)}, u32[]{:S(2)}, u32[]{:S(2)}) %collective-permute-start.35) | collective-permute-done | bytes 32800 | tf_op jit(solution)/shard_map/ppermute | solution.py:53
  194.7 3.7 %collective-permute-done.34 = f32[128,65]{1,0:T(8,128)S(1)} collective-permute-done((f32[128,65]{1,0:T(8,128)S(1)}, f32[128,65]{1,0:T(8,128)S(1)}, u32[]{:S(2)}, u32[]{:S(2)}) %collective-permute-start.34) | collective-permute-done | bytes 33312 | tf_op jit(solution)/shard_map/ppermute | solution.py:97
  200.6 2.9 %collective-permute-done.37 = bf16[128,256]{1,0:T(8,128)(2,1)S(1)} collective-permute-done((bf16[128,256]{1,0:T(8,128)(2,1)S(1)}, bf16[128,256]{1,0:T(8,128)(2,1)S(1)}, u32[]{:S(2)}, u32[]{:S(2)}) %collective-permute-start.37) | collective-permute-done | bytes 65568 | tf_op jit(solution)/shard_map/ppermute | solution.py:53
  204.8 3.7 %collective-permute-done.38 = bf16[128,256]{1,0:T(8,128)(2,1)S(1)} collective-permute-done((bf16[128,256]{1,0:T(8,128)(2,1)S(1)}, bf16[128,256]{1,0:T(8,128)(2,1)S(1)}, u32[]{:S(2)}, u32[]{:S(2)}) %collective-permute-start.38) | collective-permute-done | bytes 65568 | tf_op jit(solution)/shard_map/ppermute | solution.py:53
  231.6 2.9 %fusion.96.q_ref = f32[128,1024]{1,0:T(8,128)} fusion(f32[128,1024]{1,0:T(8,128)S(1)} %fusion.16, f32[128,1024]{1,0:T(8,128)S(1)} %fusion.18, f32[128,1024]{1,0:T(8,128)S(1)} %fusion.99, bf16[128,1024]{1,0:T(8,128)(2,1)S(1)} %collective-permute-done.28, bf16[8192,1024]{1,0:T(8,128)(2,1)} %param.40, s32[]{:T(128)S(6)} %select_n.268), kind=kOutput, calls=%fused_computation.65 | convolution fusion | flops 268828672 | bytes 4456452 | tf_op jit(solution)/shard_map/dot_general | solution.py:614
  234.5 6.4 %attend.1 = bf16[128,1024]{1,0:T(8,128)(2,1)} custom-call(s32[4,8]{1,0:T(4,128)} %fusion.206.table, s32[4]{0:T(128)} %limit.1, s32[4]{0:T(128)} %adapter.1, s32[1]{0:T(128)} %bitcast.21.core, f32[128,1024]{1,0:T(8,128)} %fusion.96.q_ref, f32[128,64]{1,0:T(8,128)} %bitcast.96, f32[128,256]{1,0:T(8,128)} %fusion.163.fresh_ref, f32[128,1]{1,0:T(8,128)} %fusion.174.norm_ref, ...), custom_call_target="tpu_custom_call" | custom-call | flops 150994944 | bytes 2883584 | tf_op jit(solution)/shard_map/attend/pallas_call | solution.py:441
  (263 shorter events, 147.8 us)
Async XLA Ops:
  0.6 54.3 %collective-permute-start.4 = (bf16[128,1024]{1,0:T(8,128)(2,1)}, bf16[128,1024]{1,0:T(8,128)(2,1)}, u32[]{:S(2)}, u32[]{:S(2)}) collective-permute-start(bf16[128,1024]{1,0:T(8,128)(2,1)} %bitcast.88), channel_id=1, source_target_pairs={{0,2},{4,0},{8,4},{12,8},{14,12},{10,14},{6,10},{2,6},{1,3},{5,1},... | collective-permute-start | bytes 786440 | tf_op jit(solution)/shard_map/ppermute | solution.py:56
  3.7 52.9 %collective-permute-start = (bf16[128,1024]{1,0:T(8,128)(2,1)}, bf16[128,1024]{1,0:T(8,128)(2,1)}, u32[]{:S(2)}, u32[]{:S(2)}) collective-permute-start(bf16[128,1024]{1,0:T(8,128)(2,1)} %bitcast.89), channel_id=1, source_target_pairs={{0,4},{4,8},{8,12},{12,14},{14,10},{10,6},{6,2},{2,0},{1,5},{5,9},... | collective-permute-start | bytes 786440 | tf_op jit(solution)/shard_map/ppermute | solution.py:53
  6.3 39.8 %collective-permute-start.8 = (f32[64,640]{1,0:T(8,128)}, f32[64,640]{1,0:T(8,128)}, u32[]{:S(2)}, u32[]{:S(2)}) collective-permute-start(f32[64,640]{1,0:T(8,128)} %slice_select_fusion), channel_id=1, source_target_pairs={{0,2},{2,0},{4,6},{6,4},{8,10},{10,8},{12,14},{14,12},{1,3},{3,1},... | collective-permute-start | bytes 491528 | tf_op jit(solution)/shard_map/ppermute | solution.py:107
  12.9 94.4 %collective-permute-start.12 = (bf16[6,1024,256]{2,1,0:T(8,128)(2,1)}, bf16[6,1024,256]{2,1,0:T(8,128)(2,1)}, u32[]{:S(2)}, u32[]{:S(2)}) collective-permute-start(bf16[6,1024,256]{2,1,0:T(8,128)(2,1)} %bitcast_convert_fusion), channel_id=1, source_target_pairs={{0,1},{1,0},{2,3},{3,2},{4,5},{5,4},{6,7},{7,6},{8,9},{9,8},{10,11... | collective-permute-start | bytes 9437192 | tf_op jit(solution)/shard_map/ppermute | solution.py:518
  15.0 29.1 %collective-permute-start.43 = (bf16[8,16,256]{2,1,0:T(8,128)(2,1)}, bf16[8,16,256]{2,1,0:T(8,128)(2,1)S(1)}, u32[]{:S(2)}, u32[]{:S(2)}) collective-permute-start(bf16[8,16,256]{2,1,0:T(8,128)(2,1)} %get-tuple-element.30), channel_id=1, source_target_pairs={{0,2},{2,4},{4,6},{6,8},{8,10},{10,12},{12,14},{14,0},{1,3},{3,5},... | collective-permute-start | bytes 196616 | tf_op jit(solution)/shard_map/ppermute | solution.py:541
  54.7 78.0 %collective-permute-start.46 = (bf16[8,16,256]{2,1,0:T(8,128)(2,1)}, bf16[8,16,256]{2,1,0:T(8,128)(2,1)S(1)}, u32[]{:S(2)}, u32[]{:S(2)}) collective-permute-start(bf16[8,16,256]{2,1,0:T(8,128)(2,1)} %get-tuple-element.27), channel_id=1, source_target_pairs={{0,8},{2,10},{4,12},{6,14},{8,0},{10,2},{12,4},{14,6},{1,9},{3,11}... | collective-permute-start | bytes 196616 | tf_op jit(solution)/shard_map/ppermute | solution.py:541
  55.0 18.7 %collective-permute-start.5 = (bf16[128,1024]{1,0:T(8,128)(2,1)}, bf16[128,1024]{1,0:T(8,128)(2,1)S(1)}, u32[]{:S(2)}, u32[]{:S(2)}) collective-permute-start(bf16[128,1024]{1,0:T(8,128)(2,1)} %collective-permute-done.4.refs_1_), channel_id=1, source_target_pairs={{0,2},{4,0},{8,4},{12,8},{14,12},{10,14},{6,10},{2,6},{1,3},{5,1},... | collective-permute-start | bytes 786440 | tf_op jit(solution)/shard_map/ppermute | solution.py:56
  56.5 17.9 %collective-permute-start.1 = (bf16[128,1024]{1,0:T(8,128)(2,1)}, bf16[128,1024]{1,0:T(8,128)(2,1)S(1)}, u32[]{:S(2)}, u32[]{:S(2)}) collective-permute-start(bf16[128,1024]{1,0:T(8,128)(2,1)} %collective-permute-done.refs_0_), channel_id=1, source_target_pairs={{0,4},{4,8},{8,12},{12,14},{14,10},{10,6},{6,2},{2,0},{1,5},{5,9},... | collective-permute-start | bytes 786440 | tf_op jit(solution)/shard_map/ppermute | solution.py:53
  58.9 13.5 %collective-permute-start.10 = (f32[64,640]{1,0:T(8,128)S(1)}, f32[64,640]{1,0:T(8,128)S(1)}, u32[]{:S(2)}, u32[]{:S(2)}) collective-permute-start(f32[64,640]{1,0:T(8,128)S(1)} %add.366), channel_id=1, source_target_pairs={{0,8},{2,10},{4,12},{6,14},{8,0},{10,2},{12,4},{14,6},{1,9},{3,11}... | collective-permute-start | bytes 491528 | tf_op jit(solution)/shard_map/ppermute | solution.py:109
  72.3 12.1 %collective-permute-start.11 = (f32[64,640]{1,0:T(8,128)S(1)}, f32[64,640]{1,0:T(8,128)S(1)}, u32[]{:S(2)}, u32[]{:S(2)}) collective-permute-start(f32[64,640]{1,0:T(8,128)S(1)} %add.367), channel_id=1, source_target_pairs={{0,2},{2,0},{4,6},{6,4},{8,10},{10,8},{12,14},{14,12},{1,3},{3,1},... | collective-permute-start | bytes 491528 | tf_op jit(solution)/shard_map/ppermute | solution.py:110
  73.7 13.4 %collective-permute-start.6 = (bf16[128,1024]{1,0:T(8,128)(2,1)S(1)}, bf16[128,1024]{1,0:T(8,128)(2,1)S(1)}, u32[]{:S(2)}, u32[]{:S(2)}) collective-permute-start(bf16[128,1024]{1,0:T(8,128)(2,1)S(1)} %collective-permute-done.5.refs_1_), channel_id=1, source_target_pairs={{0,2},{4,0},{8,4},{12,8},{14,12},{10,14},{6,10},{2,6},{1,3},{5,1},... | collective-permute-start | bytes 786440 | tf_op jit(solution)/shard_map/ppermute | solution.py:56
  74.4 13.6 %collective-permute-start.2 = (bf16[128,1024]{1,0:T(8,128)(2,1)S(1)}, bf16[128,1024]{1,0:T(8,128)(2,1)S(1)}, u32[]{:S(2)}, u32[]{:S(2)}) collective-permute-start(bf16[128,1024]{1,0:T(8,128)(2,1)S(1)} %collective-permute-done.1.refs_0_), channel_id=1, source_target_pairs={{0,4},{4,8},{8,12},{12,14},{14,10},{10,6},{6,2},{2,0},{1,5},{5,9},... | collective-permute-start | bytes 786440 | tf_op jit(solution)/shard_map/ppermute | solution.py:53
  84.5 62.4 %collective-permute-start.47 = (bf16[8,16,256]{2,1,0:T(8,128)(2,1)S(1)}, bf16[8,16,256]{2,1,0:T(8,128)(2,1)S(1)}, u32[]{:S(2)}, u32[]{:S(2)}) collective-permute-start(bf16[8,16,256]{2,1,0:T(8,128)(2,1)S(1)} %copy-done.16), channel_id=1, source_target_pairs={{0,10},{2,12},{4,14},{6,0},{8,2},{10,4},{12,6},{14,8},{1,11},{3,13... | collective-permute-start | bytes 196616 | tf_op jit(solution)/shard_map/ppermute | solution.py:541
  87.1 10.9 %collective-permute-start.7 = (bf16[64,1024]{1,0:T(8,128)(2,1)S(1)}, bf16[64,1024]{1,0:T(8,128)(2,1)S(1)}, u32[]{:S(2)}, u32[]{:S(2)}) collective-permute-start(bf16[64,1024]{1,0:T(8,128)(2,1)S(1)} %slice.211), channel_id=1, source_target_pairs={{0,2},{4,0},{8,4},{12,8},{14,12},{10,14},{6,10},{2,6},{1,3},{5,1},... | collective-permute-start | bytes 393224 | tf_op jit(solution)/shard_map/ppermute | solution.py:56
  88.1 11.4 %collective-permute-start.3 = (bf16[64,1024]{1,0:T(8,128)(2,1)S(1)}, bf16[64,1024]{1,0:T(8,128)(2,1)S(1)}, u32[]{:S(2)}, u32[]{:S(2)}) collective-permute-start(bf16[64,1024]{1,0:T(8,128)(2,1)S(1)} %slice.210), channel_id=1, source_target_pairs={{0,4},{4,8},{8,12},{12,14},{14,10},{10,6},{6,2},{2,0},{1,5},{5,9},... | collective-permute-start | bytes 393224 | tf_op jit(solution)/shard_map/ppermute | solution.py:53
  98.0 59.9 %collective-permute-start.48 = (bf16[8,16,256]{2,1,0:T(8,128)(2,1)S(1)}, bf16[8,16,256]{2,1,0:T(8,128)(2,1)S(1)}, u32[]{:S(2)}, u32[]{:S(2)}) collective-permute-start(bf16[8,16,256]{2,1,0:T(8,128)(2,1)S(1)} %copy-done.15), channel_id=1, source_target_pairs={{0,12},{2,14},{4,0},{6,2},{8,4},{10,6},{12,8},{14,10},{1,13},{3,15... | collective-permute-start | bytes 196616 | tf_op jit(solution)/shard_map/ppermute | solution.py:541
  99.4 59.9 %collective-permute-start.49 = (bf16[8,16,256]{2,1,0:T(8,128)(2,1)S(1)}, bf16[8,16,256]{2,1,0:T(8,128)(2,1)S(1)}, u32[]{:S(2)}, u32[]{:S(2)}) collective-permute-start(bf16[8,16,256]{2,1,0:T(8,128)(2,1)S(1)} %copy-done.14), channel_id=1, source_target_pairs={{0,14},{2,0},{4,2},{6,4},{8,6},{10,8},{12,10},{14,12},{1,15},{3,1}... | collective-permute-start | bytes 196616 | tf_op jit(solution)/shard_map/ppermute | solution.py:541
  132.7 10.9 %collective-permute-start.14 = (bf16[128,1024]{1,0:T(8,128)(2,1)S(1)}, bf16[128,1024]{1,0:T(8,128)(2,1)S(1)}, u32[]{:S(2)}, u32[]{:S(2)}) collective-permute-start(bf16[128,1024]{1,0:T(8,128)(2,1)S(1)} %pad_maximum_fusion.1), channel_id=1, source_target_pairs={{0,4},{4,8},{8,12},{12,14},{14,10},{10,6},{6,2},{2,0},{1,5},{5,9},... | collective-permute-start | bytes 786440 | tf_op jit(solution)/shard_map/ppermute | solution.py:53
  147.8 10.1 %collective-permute-start.22 = (f32[128,1]{1,0:T(8,128)S(1)}, f32[128,1]{1,0:T(8,128)S(1)}, u32[]{:S(2)}, u32[]{:S(2)}) collective-permute-start(f32[128,1]{1,0:T(8,128)S(1)} %add.385), channel_id=1, source_target_pairs={{0,4},{2,6},{4,0},{6,2},{8,12},{10,14},{12,8},{14,10},{1,5},{3,7},... | collective-permute-start | bytes 1544 | tf_op jit(solution)/shard_map/ppermute | solution.py:97
  153.7 10.3 %collective-permute-start.20 = (bf16[128,1024]{1,0:T(8,128)(2,1)S(1)}, bf16[128,1024]{1,0:T(8,128)(2,1)S(1)}, u32[]{:S(2)}, u32[]{:S(2)}) collective-permute-start(bf16[128,1024]{1,0:T(8,128)(2,1)S(1)} %fusion.135), channel_id=1, source_target_pairs={{0,2},{4,0},{8,4},{12,8},{14,12},{10,14},{6,10},{2,6},{1,3},{5,1},... | collective-permute-start | bytes 786440 | tf_op jit(solution)/shard_map/ppermute | solution.py:56
  159.4 75.1 %collective-permute-start.50 = (bf16[64,16,256]{2,1,0:T(8,128)(2,1)S(1)}, bf16[64,16,256]{2,1,0:T(8,128)(2,1)}, u32[]{:S(2)}, u32[]{:S(2)}) collective-permute-start(bf16[64,16,256]{2,1,0:T(8,128)(2,1)S(1)} %constant_dynamic-update-slice_fusion.near_ref), channel_id=1, source_target_pairs={{0,1},{1,0},{2,3},{3,2},{4,5},{5,4},{6,7},{7,6},{8,9},{9,8},{10,11... | collective-permute-start | bytes 1572872 | tf_op jit(solution)/shard_map/ppermute | solution.py:553
  166.4 42.8 %collective-permute-start.25 = (bf16[128,1024]{1,0:T(8,128)(2,1)S(1)}, bf16[128,1024]{1,0:T(8,128)(2,1)}, u32[]{:S(2)}, u32[]{:S(2)}) collective-permute-start(bf16[128,1024]{1,0:T(8,128)(2,1)S(1)} %get-tuple-element.34), channel_id=1, source_target_pairs={{0,2},{4,0},{8,4},{12,8},{14,12},{10,14},{6,10},{2,6},{1,3},{5,1},... | collective-permute-start | bytes 786440 | tf_op jit(solution)/shard_map/ppermute | solution.py:56
  169.4 41.9 %collective-permute-start.24 = (bf16[128,1024]{1,0:T(8,128)(2,1)S(1)}, bf16[128,1024]{1,0:T(8,128)(2,1)}, u32[]{:S(2)}, u32[]{:S(2)}) collective-permute-start(bf16[128,1024]{1,0:T(8,128)(2,1)S(1)} %get-tuple-element.34), channel_id=1, source_target_pairs={{0,4},{4,8},{8,12},{12,14},{14,10},{10,6},{6,2},{2,0},{1,5},{5,9},... | collective-permute-start | bytes 786440 | tf_op jit(solution)/shard_map/ppermute | solution.py:53
  172.0 13.3 %collective-permute-start.32 = (f32[128,65]{1,0:T(8,128)S(1)}, f32[128,65]{1,0:T(8,128)S(1)}, u32[]{:S(2)}, u32[]{:S(2)}) collective-permute-start(f32[128,65]{1,0:T(8,128)S(1)} %pad_maximum_fusion.7), channel_id=1, source_target_pairs={{0,2},{2,0},{4,6},{6,4},{8,10},{10,8},{12,14},{14,12},{1,3},{3,1},... | collective-permute-start | bytes 99848 | tf_op jit(solution)/shard_map/ppermute | solution.py:97
  (62 other events, 577.7 us)

commit v2 on v1

v2 whole, which is shorter than its diff:
```python
import functools

import jax
import jax.numpy as jnp
from jax import lax
from jax.experimental import pallas as pl
from jax.experimental.pallas import tpu as pltpu
from jax.sharding import PartitionSpec as P

HDIM = 64
STATE = 256
QUERY_HEADS = 64
KEY_HEADS = 8
HEAD_SIZE = 128

epsilon = 1e-05
adapter_scale = 2.0
highest = lax.Precision.HIGHEST
f32 = jnp.float32
bf16 = jnp.bfloat16
VMEM_BYTES = 56 << 20


def ring_order(n):
    cols = 1
    for c in range(2, n):
        if n % c == 0 and (n // c) % 2 == 0 and c <= n // c:
            cols = c
    if cols == 1:
        return list(range(n))
    rows = n // cols
    order = [r * cols for r in range(rows)]
    for k, r in enumerate(reversed(range(rows))):
        across = list(range(1, cols))
        order += [r * cols + c for c in (across if k % 2 == 0 else across[::-1])]
    return order


class Ring:
    def __init__(self, n, pools):
        self.n = n
        self.half = n // 2
        self.pools = pools
        order = ring_order(n)
        place = {d: i for i, d in enumerate(order)}
        self.table = [
            [order[(place[d] + s) % n] for s in range(n)] + [d, c] for d in range(n) for c in range(pools)
        ]
        self.cw = [(order[i], order[(i + 1) % n]) for i in range(n)]
        self.ccw = [(order[i], order[(i - 1) % n]) for i in range(n)]

    def info(self):
        at = lax.axis_index("tensor") * self.pools + lax.axis_index("pool")
        return lax.dynamic_slice_in_dim(jnp.array(self.table, jnp.int32), at, 1, 0)[0]

    def right(self, x):
        return lax.ppermute(x, "tensor", self.cw)

    def left(self, x):
        return lax.ppermute(x, "tensor", self.ccw)

    def gather(self, x):
        n, half = self.n, self.half
        h = x.shape[0] // 2
        stages = [([0], [x])]
        a = b = x
        for s in range(1, half):
            a, b = self.right(a), self.left(b)
            stages.append(([n - s, s], [a, b]))
        stages.append(([half], [self.right(a[:h]), self.left(b[h:])]))
        return stages


def split(x):
    high = x.astype(bf16)
    return high, (x - high.astype(f32)).astype(bf16)


def in_kernel(offsets, count, first_call, info, *refs):
    blocks = refs[:count]
    w_ref = refs[count]
    o_ref, p_ref, spread = refs[-3:]
    j = pl.program_id(0)
    depth = w_ref.shape[0]
    rows = o_ref.shape[0] // 2

    @pl.when(j == 0)
    def _():
        if first_call:
            o_ref[...] = jnp.zeros_like(o_ref)
            p_ref[...] = jnp.zeros_like(p_ref)
        else:
            o_ref[...] = refs[count + 1][...]
            p_ref[...] = refs[count + 2][...]

    lane = lax.broadcasted_iota(jnp.int32, (128, 512), 1)
    sub = lax.broadcasted_iota(jnp.int32, (128, 512), 0)
    target = jnp.where(lane < 256, 2 * sub, 2 * sub + 257)
    widen = jnp.where(lane == target, 1.0, 0.0).astype(bf16)

    for b in range(len(offsets)):

        @pl.when(j == b)
        def _():
            base = 0
            for block in [blocks[b]] if count == len(offsets) else blocks:
                r = block.shape[0]
                for p in range(depth // 128):
                    piece = block[:, p * 128 : (p + 1) * 128]
                    both = jnp.dot(piece, widen, preferred_element_type=f32).astype(bf16)
                    spread[base : base + r, p * 256 : (p + 1) * 256] = both[:, :256]
                    spread[rows + base : rows + base + r, p * 256 : (p + 1) * 256] = both[:, 256:]
                p_ref[base : base + r] += block[:, depth:].astype(f32)
                base += r

    w = w_ref[...].reshape(2 * depth, w_ref.shape[2])
    o_ref[...] += jnp.dot(spread[...], w, preferred_element_type=f32)


def in_product(info, offsets, blocks, weight, depth, accs):
    count = len(blocks)
    rows = sum(b.shape[0] for b in blocks) // len(offsets)
    cols = weight.shape[2]
    extra = blocks[0].shape[1] - depth

    def row_block(j, info):
        at = info[offsets[0]]
        for b in range(1, len(offsets)):
            at = jnp.where(j == b, info[offsets[b]], at)
        return (at, 0, 0)

    def fixed(shape):
        return pl.BlockSpec(shape, lambda j, info: (0, 0))

    in_specs = [fixed(b.shape) for b in blocks]
    in_specs.append(pl.BlockSpec((depth, 2, cols), row_block))
    operands = [info, *blocks, weight]
    aliases = {}
    shapes = [(2 * rows, cols), (rows, extra)]
    if accs is not None:
        in_specs += [fixed(s) for s in shapes]
        aliases = {len(operands): 0, len(operands) + 1: 1}
        operands += accs
    return pl.pallas_call(
        functools.partial(in_kernel, offsets, count, accs is None),
        grid_spec=pltpu.PrefetchScalarGridSpec(
            num_scalar_prefetch=1,
            grid=(len(offsets),),
            in_specs=in_specs,
            out_specs=[fixed(s) for s in shapes],
            scratch_shapes=[pltpu.VMEM((2 * rows, 2 * depth), bf16)],
        ),
        out_shape=[jax.ShapeDtypeStruct(s, f32) for s in shapes],
        input_output_aliases=aliases,
        compiler_params=pltpu.CompilerParams(vmem_limit_bytes=VMEM_BYTES),
        cost_estimate=pl.CostEstimate(
            flops=len(offsets) * 8 * rows * depth * cols,
            bytes_accessed=len(offsets) * depth * cols * 8,
            transcendentals=0,
        ),
        name="in_product",
    )(*operands)


def lanes_of(columns, rows):
    lane = lax.broadcasted_iota(jnp.int32, (rows, 128), 1)
    out = jnp.zeros((rows, 128), f32)
    for at, value in columns:
        out = jnp.where(lane == at, value.astype(f32), out)
    return out.astype(bf16)


def energy_lanes(energy):
    high, low = split(energy)
    return lanes_of([(0, high), (1, low)], energy.shape[0])


def energy_of(lanes):
    wide = lanes.astype(f32)
    return wide[:, 0:1] + wide[:, 1:2]


def send_kernel(kind, dests, steps, with_energy, info, lhs_ref, w_ref, *refs):
    refs = list(refs)
    e_ref = refs.pop(0) if with_energy else None
    outs = refs[-2:]
    got = refs[:-2]
    j, c = pl.program_id(0), pl.program_id(1)
    ct = w_ref.shape[1]
    rows = lhs_ref.shape[0]
    h = rows // 2
    depth = steps * ct
    term = jnp.dot(lhs_ref[...], w_ref[...], preferred_element_type=f32)
    sides = [slice(0, h), slice(h, rows)]
    tail = slice(depth, depth + 128)

    for jj in range(dests):
        for cc in range(steps):

            @pl.when((j == jj) & (c == cc))
            def _():
                at = slice(cc * ct, (cc + 1) * ct)
                if kind == "first":
                    for out, side in zip(outs, sides):
                        out[:, at] = term[side].astype(bf16)
                elif kind == "second":
                    mine, other = sides[jj], sides[1 - jj]
                    outs[jj][mine, at] = (term[mine] + got[jj][:, at].astype(f32)).astype(bf16)
                    outs[jj][other, at] = term[other].astype(bf16)
                else:
                    outs[jj][:, at] = (term + got[jj][:, at].astype(f32)).astype(bf16)
                if with_energy and cc == 0:
                    e = e_ref[...]
                    if kind == "first":
                        for out, side in zip(outs, sides):
                            out[:, tail] = energy_lanes(e[side])
                    elif kind == "second":
                        came = e[mine] + energy_of(got[jj][:, tail])
                        outs[jj][mine, tail] = energy_lanes(came)
                        outs[jj][other, tail] = energy_lanes(e[other])
                    else:
                        outs[jj][:, tail] = energy_lanes(e + energy_of(got[jj][:, tail]))


def tile_of(depth):
    return min(512, depth)


def column_block(offsets, steps):
    def at(j, c, info, *more):
        device = info[offsets[0]]
        for b in range(1, len(offsets)):
            device = jnp.where(j == b, info[offsets[b]], device)
        return (0, device * steps + c)

    return at


def fixed_block(shape):
    return pl.BlockSpec(shape, lambda j, c, *s: (0,) * len(shape))


def send_step(info, kind, offsets, lhs, weight, depth, energy, got):
    rows = lhs.shape[0]
    ct = tile_of(depth)
    steps = depth // ct
    wide = depth + (0 if energy is None else 128)
    high = rows // 2 if kind == "first" else rows
    operands = [lhs, weight] + ([] if energy is None else [energy]) + got
    in_specs = [fixed_block(a.shape) for a in operands]
    in_specs[1] = pl.BlockSpec((weight.shape[0], ct), column_block(offsets, steps))
    return pl.pallas_call(
        functools.partial(send_kernel, kind, len(offsets), steps, energy is not None),
        grid_spec=pltpu.PrefetchScalarGridSpec(
            num_scalar_prefetch=1,
            grid=(len(offsets), steps),
            in_specs=in_specs,
            out_specs=[fixed_block((high, wide))] * 2,
        ),
        out_shape=[jax.ShapeDtypeStruct((high, wide), bf16)] * 2,
        compiler_params=pltpu.CompilerParams(vmem_limit_bytes=VMEM_BYTES),
        cost_estimate=pl.CostEstimate(
            flops=len(offsets) * 2 * rows * depth * weight.shape[0],
            bytes_accessed=len(offsets) * depth * weight.shape[0] * 2,
            transcendentals=0,
        ),
        name="send_step",
    )(info, *operands)


def ring_sum(ring, info, lhs, weight, depth, energy=None):
    n, half = ring.n, ring.half
    a, b = send_step(info, "first", [half], lhs, weight, depth, energy, [])
    a, b = ring.right(a), ring.left(b)
    for d in range(half - 1, 0, -1):
        kind = "second" if d == half - 1 else "later"
        a, b = send_step(info, kind, [d, n - d], lhs, weight, depth, energy, [a, b])
        a, b = ring.right(a), ring.left(b)
    return [a, b] if half > 1 else [jnp.concatenate([a, b], axis=0)]


def mixer_kernel(arrived, steps, tenants, inner_size, info, adapter, lhs_ref, w_ref, *refs):
    got = refs[:arrived]
    e_ref, tok_ref, gain_ref = refs[arrived : arrived + 3]
    downs = refs[arrived + 3 : arrived + 3 + tenants]
    first_ref, message_ref, square = refs[-3:]
    c = pl.program_id(1)
    ct = w_ref.shape[1]
    rows = lhs_ref.shape[0]
    depth = steps * ct
    length = rows // tenants
    tail = slice(depth, depth + 128)
    energy = e_ref[...]
    for g in got:
        energy = energy + energy_of(g[:, tail])
    scale = lax.rsqrt(energy / inner_size + epsilon)
    term = jnp.dot(lhs_ref[...], w_ref[...], preferred_element_type=f32)

    @pl.when(c == 0)
    def _():
        square[...] = jnp.zeros_like(square)

    for cc in range(steps):

        @pl.when(c == cc)
        def _():
            at = slice(cc * ct, (cc + 1) * ct)
            total = term
            for g in got:
                total = total + g[:, at].astype(f32)
            first = (tok_ref[:, at].astype(f32) + total * scale).astype(bf16)
            wide = first.astype(f32)
            square[...] += jnp.sum(wide * wide, axis=1, keepdims=True)
            first_ref[:, at] = first
            message_ref[:, at] = (wide * gain_ref[:, at]).astype(bf16)

    @pl.when(c == steps - 1)
    def _():
        high, low = split(square[...])
        rank = downs[0].shape[1]
        parts = []
        for i in range(tenants):
            x = message_ref[i * length : (i + 1) * length, :depth]
            parts.append(
                lax.dot_general(x, downs[i][0], (((1,), (1,)), ((), ())), preferred_element_type=f32)
            )
        small = jnp.concatenate(parts, axis=0).astype(bf16)
        message_ref[:, tail] = lanes_of([(rank, high), (rank + 1, low)], rows)
        message_ref[:, depth : depth + rank] = small


def mixer_step(info, adapter, lhs, weight, depth, energy, got, own_tokens, gain, down, inner_size):
    rows = lhs.shape[0]
    tenants = adapter.shape[0]
    ct = tile_of(depth)
    steps = depth // ct
    operands = [lhs, weight, *got, energy, own_tokens, gain] + [down] * tenants
    in_specs = [fixed_block(a.shape) for a in operands]
    in_specs[1] = pl.BlockSpec((weight.shape[0], ct), column_block([0], steps))
    in_specs[4 + len(got)] = pl.BlockSpec(
        (1, depth), lambda j, c, info, adapter: (0, info[info.shape[0] - 2])
    )
    for i in range(tenants):
        in_specs[5 + len(got) + i] = pl.BlockSpec(
            (1, *down.shape[1:]), functools.partial(lambda i, j, c, info, adapter: (adapter[i], 0, 0), i)
        )
    shapes = [(rows, depth), (rows, depth + 128)]
    return pl.pallas_call(
        functools.partial(mixer_kernel, len(got), steps, tenants, inner_size),
        grid_spec=pltpu.PrefetchScalarGridSpec(
            num_scalar_prefetch=2,
            grid=(1, steps),
            in_specs=in_specs,
            out_specs=[fixed_block(s) for s in shapes],
            scratch_shapes=[pltpu.VMEM((rows, 1), f32)],
        ),
        out_shape=[jax.ShapeDtypeStruct(s, bf16) for s in shapes],
        compiler_params=pltpu.CompilerParams(vmem_limit_bytes=VMEM_BYTES),
        cost_estimate=pl.CostEstimate(
            flops=2 * rows * depth * weight.shape[0],
            bytes_accessed=depth * weight.shape[0] * 2,
            transcendentals=0,
        ),
        name="mixer_step",
    )(info, adapter, *operands)


def final_kernel(arrived, info, lhs_ref, w_ref, *refs):
    total = jnp.dot(lhs_ref[...], w_ref[...], preferred_element_type=f32)
    for g in refs[:arrived]:
        total = total + g[...].astype(f32)
    refs[-1][...] = (refs[arrived][...].astype(f32) + total).astype(bf16)


def final_step(info, lhs, weight, depth, got, first):
    rows = lhs.shape[0]
    ct = tile_of(depth)
    steps = depth // ct
    operands = [lhs, weight, *got, first]
    tiles = pl.BlockSpec((rows, ct), lambda j, c, info: (0, c))
    return pl.pallas_call(
        functools.partial(final_kernel, len(got)),
        grid_spec=pltpu.PrefetchScalarGridSpec(
            num_scalar_prefetch=1,
            grid=(1, steps),
            in_specs=[
                fixed_block(lhs.shape),
                pl.BlockSpec((weight.shape[0], ct), column_block([0], steps)),
            ]
            + [tiles] * (len(got) + 1),
            out_specs=tiles,
        ),
        out_shape=jax.ShapeDtypeStruct((rows, depth), bf16),
        compiler_params=pltpu.CompilerParams(vmem_limit_bytes=VMEM_BYTES),
        name="final_step",
    )(info, *operands)


def query_kernel(offsets, count, first_call, info, *refs):
    blocks = refs[:count]
    w_ref = refs[count]
    q_ref, l_ref = refs[-2:]
    j, k = pl.program_id(0), pl.program_id(1)
    kb = w_ref.shape[0]
    steps = pl.num_programs(1)
    depth = blocks[0].shape[1] - 128

    @pl.when((j == 0) & (k == 0))
    def _():
        if first_call:
            q_ref[...] = jnp.zeros_like(q_ref)
            l_ref[...] = jnp.zeros_like(l_ref)
        else:
            q_ref[...] = refs[count + 1][...]
            l_ref[...] = refs[count + 2][...]

    for b in range(len(offsets)):
        for kk in range(depth // kb):

            @pl.when((j == b) & (k == kk))
            def _():
                pieces = [blocks[b]] if count == len(offsets) else blocks
                base = 0
                for block in pieces:
                    at = slice(base, base + block.shape[0])
                    q_ref[at] += jnp.dot(
                        block[:, kk * kb : (kk + 1) * kb], w_ref[...], preferred_element_type=f32
                    )
                    if kk == 0:
                        l_ref[at] += block[:, depth:].astype(f32)
                    base += block.shape[0]


def query_step(info, offsets, blocks, weight, depth, accs):
    count = len(blocks)
    rows = sum(b.shape[0] for b in blocks) // len(offsets)
    cols = weight.shape[1]
    kb = tile_of(depth)
    steps = depth // kb

    def row_block(j, k, info):
        at = info[offsets[0]]
        for b in range(1, len(offsets)):
            at = jnp.where(j == b, info[offsets[b]], at)
        return (at * steps + k, 0)

    shapes = [(rows, cols), (rows, 128)]
    in_specs = [fixed_block(b.shape) for b in blocks] + [pl.BlockSpec((kb, cols), row_block)]
    operands = [info, *blocks, weight]
    aliases = {}
    if accs is not None:
        in_specs += [fixed_block(s) for s in shapes]
        aliases = {len(operands): 0, len(operands) + 1: 1}
        operands += accs
    return pl.pallas_call(
        functools.partial(query_kernel, offsets, count, accs is None),
        grid_spec=pltpu.PrefetchScalarGridSpec(
            num_scalar_prefetch=1,
            grid=(len(offsets), steps),
            in_specs=in_specs,
            out_specs=[fixed_block(s) for s in shapes],
        ),
        out_shape=[jax.ShapeDtypeStruct(s, f32) for s in shapes],
        input_output_aliases=aliases,
        compiler_params=pltpu.CompilerParams(vmem_limit_bytes=VMEM_BYTES),
        cost_estimate=pl.CostEstimate(
            flops=len(offsets) * 2 * rows * depth * cols,
            bytes_accessed=len(offsets) * depth * cols * 2,
            transcendentals=0,
        ),
        name="query_step",
    )(*operands)


def shifted(history, x, k):
    if k == 3:
        return x
    return jnp.concatenate([history[k:3], x[: x.shape[0] - 3 + k]], axis=0)


def conv_silu(history, x, taps):
    total = taps[0:1] * shifted(history, x, 0)
    for k in range(1, 4):
        total = total + taps[k : k + 1] * shifted(history, x, k)
    return total * jax.nn.sigmoid(total)


def spans(heads, width):
    lane = lax.broadcasted_iota(jnp.int32, (heads, heads * width), 1)
    row = lax.broadcasted_iota(jnp.int32, (heads, heads * width), 0)
    return jnp.where(lane // width == row, 1.0, 0.0).astype(f32)


def state_kernel(
    slot,
    info,
    x_ref,
    z_ref,
    bc_ref,
    hx_ref,
    hbc_ref,
    tx_ref,
    tbc_ref,
    bias_ref,
    rate_ref,
    skip_ref,
    gain_ref,
    own_ref,
    far_ref,
    gated_ref,
    energy_ref,
    final_ref,
    initial,
    *,
    slots,
):
    i = pl.program_id(0)
    count = info.shape[0]
    is_own = slot[i] // slots == info[count - 1]

    @pl.when(is_own)
    def _():
        initial[...] = own_ref[0]

    @pl.when(jnp.logical_not(is_own))
    def _():
        initial[...] = far_ref[0].astype(f32)

    length = x_ref.shape[0]
    heads = bias_ref.shape[1]
    values = conv_silu(hx_ref[0], x_ref[...].astype(bf16).astype(f32), tx_ref[...])
    bc = conv_silu(hbc_ref[0], bc_ref[:, : 2 * STATE], tbc_ref[...])
    all_raw = bc_ref[:, 2 * STATE :]
    pick = (all_raw.shape[1], heads)
    chosen = lax.broadcasted_iota(jnp.int32, pick, 0) == (
        lax.broadcasted_iota(jnp.int32, pick, 1) + info[count - 2] * heads
    )
    chosen = jnp.where(chosen, 1.0, 0.0).astype(f32)
    in_state = bc[:, :STATE].astype(bf16)
    out_state = bc[:, STATE:].astype(bf16)
    raw = jnp.dot(all_raw, chosen, precision=highest, preferred_element_type=f32) + bias_ref[...]
    steps = jnp.maximum(raw, 0.0) + jnp.log1p(jnp.exp(-jnp.abs(raw)))
    log_decay = -steps * jnp.exp(rate_ref[...])
    row = lax.broadcasted_iota(jnp.int32, (length, length), 0)
    col = lax.broadcasted_iota(jnp.int32, (length, length), 1)
    lower = jnp.where(row >= col, 1.0, 0.0).astype(f32)
    running = jnp.dot(lower, log_decay, precision=highest, preferred_element_type=f32)
    last = running[length - 1 : length]

    wide = spans(heads, length)
    both = jnp.dot(
        jnp.concatenate([running, steps], axis=0), wide, precision=highest, preferred_element_type=f32
    )
    run_t, step_t = both[:length], both[length:]
    lane = lax.broadcasted_iota(jnp.int32, (length, heads * length), 1) % length
    place = lax.broadcasted_iota(jnp.int32, (length, heads * length), 0)
    diagonal = lane == place
    run_s = jnp.sum(jnp.where(diagonal, run_t, 0.0), axis=0, keepdims=True)
    step_s = jnp.sum(jnp.where(diagonal, step_t, 0.0), axis=0, keepdims=True)
    seen = place >= lane
    decays = jnp.where(seen, jnp.exp(jnp.where(seen, run_t - run_s, 0.0)), 0.0)
    overlap = lax.dot_general(
        out_state,
        jnp.concatenate([in_state] * heads, axis=0),
        (((1,), (1,)), ((), ())),
        preferred_element_type=f32,
    )
    mixing = (overlap * decays * step_s).astype(bf16)
    short = values.astype(bf16)
    group = min(4, heads)
    gl, gw = group * length, group * HDIM
    own_block = (
        lax.broadcasted_iota(jnp.int32, (gl, gw), 0) // length
        == lax.broadcasted_iota(jnp.int32, (gl, gw), 1) // HDIM
    )
    within = []
    for g in range(heads // group):
        v = jnp.concatenate([values[:, g * gw : (g + 1) * gw]] * group, axis=0)
        v = jnp.where(own_block, v, 0.0).astype(bf16)
        within.append(jnp.dot(mixing[:, g * gl : (g + 1) * gl], v, preferred_element_type=f32))
    within = within[0] if len(within) == 1 else jnp.concatenate(within, axis=1)

    narrow = spans(heads, HDIM)
    scales = jnp.dot(
        jnp.concatenate(
            [
                jnp.exp(running),
                jnp.exp(last - running) * steps,
                jnp.broadcast_to(skip_ref[...], (8, heads)),
            ],
            axis=0,
        ),
        narrow,
        precision=highest,
        preferred_element_type=f32,
    )
    start = initial[...]
    carried = lax.dot_general(
        out_state, start.astype(bf16), (((1,), (1,)), ((), ())), preferred_element_type=f32
    )
    result = within + carried * scales[:length] + scales[2 * length : 2 * length + 1] * values
    z = z_ref[...].astype(bf16).astype(f32)
    gated = result * (z * jax.nn.sigmoid(z))
    energy_ref[...] = jnp.sum(gated * gated, axis=1, keepdims=True)
    gated_ref[...] = (gated * gain_ref[...]).astype(bf16)

    kept = jnp.exp(
        lax.dot_general(
            log_decay,
            jnp.ones((length, STATE), f32),
            (((0,), (0,)), ((), ())),
            precision=highest,
            preferred_element_type=f32,
        )
    )
    update = lax.dot_general(
        (values * scales[length : 2 * length]).astype(bf16),
        in_state,
        (((0,), (0,)), ((), ())),
        preferred_element_type=f32,
    )
    for h in range(heads):
        at = slice(h * HDIM, (h + 1) * HDIM)
        final_ref[0, at, :] = update[at] + start[at] * kept[h : h + 1]


def state_pass(
    info, slot, inner, projected, hx, hbc, tx, tbc, bias, rate, skip, gain, own_pool, far_pool
):
    tenants = slot.shape[0]
    length = projected.shape[0] // tenants
    cols = inner.shape[1]
    slots = own_pool.shape[0]

    def rows(width):
        return pl.BlockSpec((length, width), lambda i, *s: (i, 0))

    def whole(a):
        return pl.BlockSpec(a.shape, lambda i, *s: (0,) * a.ndim)

    def own_slot(i, slot, info):
        return (jnp.clip(slot[i] - info[info.shape[0] - 1] * slots, 0, slots - 1), 0, 0)

    def far_slot(i, slot, info):
        return (jnp.clip(slot[i] - (1 - info[info.shape[0] - 1]) * slots, 0, slots - 1), 0, 0)

    pooled = (1, cols, STATE)
    return pl.pallas_call(
        functools.partial(state_kernel, slots=slots),
        grid_spec=pltpu.PrefetchScalarGridSpec(
            num_scalar_prefetch=2,
            grid=(tenants,),
            in_specs=[
                rows(cols),
                pl.BlockSpec((length, cols), lambda i, *s: (tenants + i, 0)),
                rows(projected.shape[1]),
                pl.BlockSpec((1, 3, cols), lambda i, *s: (i, 0, 0)),
                pl.BlockSpec((1, 3, 2 * STATE), lambda i, *s: (i, 0, 0)),
                whole(tx),
                whole(tbc),
                whole(bias),
                whole(rate),
                whole(skip),
                whole(gain),
                pl.BlockSpec(pooled, own_slot),
                pl.BlockSpec(pooled, far_slot),
            ],
            out_specs=[
                rows(cols),
                rows(1),
                pl.BlockSpec(pooled, lambda i, *s: (i, 0, 0)),
            ],
            scratch_shapes=[pltpu.VMEM((cols, STATE), f32)],
        ),
        out_shape=[
            jax.ShapeDtypeStruct((tenants * length, cols), bf16),
            jax.ShapeDtypeStruct((tenants * length, 1), f32),
            jax.ShapeDtypeStruct((tenants, cols, STATE), f32),
        ],
        compiler_params=pltpu.CompilerParams(vmem_limit_bytes=VMEM_BYTES),
        cost_estimate=pl.CostEstimate(
            flops=tenants * 6 * length * cols * STATE,
            bytes_accessed=tenants * cols * STATE * 10,
            transcendentals=0,
        ),
        name="state_pass",
    )(slot, info, inner, inner, projected, hx, hbc, tx, tbc, bias, rate, skip, gain, own_pool, far_pool)


def attend_kernel(
    size, width, table, limit, adapter, info, q_ref, low_ref, up_ref, near_ref, far_ref, *refs
):
    o_ref = refs[-1]
    i = pl.program_id(0)
    length = q_ref.shape[0]
    heads = q_ref.shape[1] // HEAD_SIZE
    blocks = table.shape[1]
    part = near_ref.shape[1]
    me, core = info[info.shape[0] - 2], info[info.shape[0] - 1]
    count = near_ref.shape[0] // size
    rank = up_ref.shape[1]
    square = low_ref[:, rank : rank + 1] + low_ref[:, rank + 1 : rank + 2]
    norm = lax.rsqrt(square / width + epsilon)
    low = (low_ref[:, :rank] * norm).astype(bf16)
    raised = jnp.dot(low, up_ref[0], preferred_element_type=f32)
    q = (q_ref[...] * norm + adapter_scale * raised).astype(bf16)
    q = jnp.concatenate([q[:, h * HEAD_SIZE : (h + 1) * HEAD_SIZE] for h in range(heads)], axis=0)
    fresh = jnp.concatenate([refs[0][...], refs[1][...]], axis=1)
    for came in refs[2:-1]:
        fresh = fresh + came[...].astype(f32)
    fresh = (fresh * norm).astype(bf16)
    pieces = []
    for j in range(blocks):
        owner = table[i, j] // count
        if size <= 8:
            owner = lax.rem(me - owner + size, size)
        at = owner * count + lax.rem(table[i, j], count)
        pieces += [near_ref[at], far_ref[at]]
    cached = jnp.concatenate(pieces, axis=0)
    context = cached.shape[0]
    nt = (((1,), (1,)), ((), ()))
    scale = HEAD_SIZE ** (-0.5)
    old = lax.dot_general(q, cached[:, :HEAD_SIZE], nt, preferred_element_type=f32) * scale
    new = lax.dot_general(q, fresh[:, :HEAD_SIZE], nt, preferred_element_type=f32) * scale
    lane = lax.broadcasted_iota(jnp.int32, old.shape, 1)
    inside = lane % (2 * part)
    far_side = jnp.where(inside >= part, 1, 0)
    half = jnp.where(core == 0, far_side, 1 - far_side)
    place = (lane // (2 * part)) * (2 * part) + half * part + inside % part
    old_seen = place < limit[i]
    token = lax.broadcasted_iota(jnp.int32, new.shape, 0) % length
    new_seen = lax.broadcasted_iota(jnp.int32, new.shape, 1) <= token
    old = jnp.where(old_seen, old, -jnp.inf)
    new = jnp.where(new_seen, new, -jnp.inf)
    top = jnp.maximum(jnp.max(old, axis=1, keepdims=True), jnp.max(new, axis=1, keepdims=True))
    old = jnp.where(old_seen, jnp.exp(old - top), 0.0)
    new = jnp.where(new_seen, jnp.exp(new - top), 0.0)
    share = 1.0 / (jnp.sum(old, axis=1, keepdims=True) + jnp.sum(new, axis=1, keepdims=True))
    out = jnp.dot((old * share).astype(bf16), cached[:, HEAD_SIZE:], preferred_element_type=f32)
    out += jnp.dot((new * share).astype(bf16), fresh[:, HEAD_SIZE:], preferred_element_type=f32)
    out = out.astype(bf16)
    for h in range(heads):
        o_ref[:, h * HEAD_SIZE : (h + 1) * HEAD_SIZE] = out[h * length : (h + 1) * length]


def attend(ring, width, table, limit, adapter, info, q, low, up, near, far, kv, kv_came, head_of):
    tenants = table.shape[0]
    length = q.shape[0] // tenants

    def rows(a):
        return pl.BlockSpec((length, a.shape[1]), lambda i, *s: (i, 0))

    def whole(a):
        return pl.BlockSpec(a.shape, lambda i, *s: (0,) * a.ndim)

    def own(base):
        return pl.BlockSpec(
            (length, HEAD_SIZE), lambda i, t, n, a, info: (i, base + head_of(info[info.shape[0] - 2]))
        )

    return pl.pallas_call(
        functools.partial(attend_kernel, ring.n, width),
        grid_spec=pltpu.PrefetchScalarGridSpec(
            num_scalar_prefetch=4,
            grid=(tenants,),
            in_specs=[
                rows(q),
                rows(low),
                pl.BlockSpec((1, *up.shape[1:]), lambda i, t, n, a, info: (a[i], 0, 0)),
                whole(near),
                whole(far),
                own(0),
                own(KEY_HEADS),
            ]
            + [rows(a) for a in kv_came],
            out_specs=rows(q),
        ),
        out_shape=jax.ShapeDtypeStruct(q.shape, bf16),
        compiler_params=pltpu.CompilerParams(vmem_limit_bytes=VMEM_BYTES),
        cost_estimate=pl.CostEstimate(
            flops=tenants * 4 * length * q.shape[1] * 288,
            bytes_accessed=near.size * 4 + q.size * 6 + up.size,
            transcendentals=0,
        ),
        name="attend",
    )(table, limit, adapter, info, q, low, up, near, far, kv, kv, *kv_came)


def per_device(
    ring,
    tokens,
    mamba_in_weight,
    state_projection,
    inner_taps,
    state_taps,
    inner_history,
    state_history,
    step_size_bias,
    log_decay_rate,
    skip_factor,
    gated_norm_gain,
    mamba_out_weight,
    saved_state_pool,
    tenant_state_slot,
    attention_gain,
    query_matrix,
    adapter_down,
    adapter_up,
    tenant_adapter,
    key_value_weight,
    key_value_pool,
    tenant_blocks,
    cached_length,
    attention_out_weight,
):
    n, half, pools = ring.n, ring.half, ring.pools
    tenants, length, depth = tokens.shape
    rows = tenants * length
    width = depth * n
    info = ring.info()
    me, core = info[n], info[n + 1]
    own_tokens = tokens.reshape(rows, depth)
    heads = step_size_bias.shape[0]
    cols = mamba_in_weight.shape[2]
    swap = [(i, (i + 1) % pools) for i in range(pools)]

    partial = jnp.dot(own_tokens, state_projection, preferred_element_type=f32)
    stages = ring.gather(jnp.concatenate([own_tokens, partial.astype(bf16)], axis=1))
    accs = None
    for offsets, blocks in stages:
        accs = in_product(info, offsets, blocks, mamba_in_weight, depth, accs)
    inner, projected = accs

    slots = saved_state_pool.shape[0]
    flat_pool = saved_state_pool.reshape(slots, heads * HDIM, STATE)
    far_pool = lax.ppermute(flat_pool.astype(bf16), "pool", swap)

    local_heads = query_matrix.shape[1] // HEAD_SIZE
    group_size = QUERY_HEADS // KEY_HEADS

    def head_of(device):
        return device * local_heads // group_size

    count, block_len, _ = key_value_pool.shape
    part = block_len // pools
    mine = lax.dynamic_slice_in_dim(key_value_pool, core * part, part, 1)
    mine = mine.reshape(count, part, 2, KEY_HEADS, HEAD_SIZE).transpose(3, 0, 1, 2, 4)
    mine = mine.reshape(KEY_HEADS, count, part, 2 * HEAD_SIZE)
    mine, _ = lax.optimization_barrier((mine, stages[-1][1]))

    if n <= 8:
        got = []
        for s in range(n):
            block = lax.dynamic_index_in_dim(mine, head_of((me + s) % n), 0, keepdims=False)
            if s > 0:
                block = lax.ppermute(block, "tensor", [(i, (i + s) % n) for i in range(n)])
            got.append(block)
        cache = jnp.concatenate(got, axis=0)
    else:
        every = jnp.stack([mine[head_of(d)] for d in range(n)])
        cache = lax.all_to_all(every, "tensor", 0, 0, tiled=True)
        cache = cache.reshape(n * count, part, 2 * HEAD_SIZE)
    far_cache = lax.ppermute(cache, "pool", swap)

    gated, energy, final_state = state_pass(
        info,
        tenant_state_slot,
        inner,
        projected,
        inner_history.astype(f32),
        state_history,
        inner_taps.astype(f32),
        state_taps.astype(f32),
        step_size_bias[None],
        log_decay_rate[None],
        skip_factor[None],
        gated_norm_gain[None],
        flat_pool,
        far_pool,
    )
    got = ring_sum(ring, info, gated, mamba_out_weight, depth, energy)
    first, message = mixer_step(
        info,
        tenant_adapter,
        gated,
        mamba_out_weight,
        depth,
        energy,
        got,
        own_tokens,
        attention_gain[None],
        adapter_down.transpose(0, 2, 1),
        cols * n,
    )

    kv = jnp.dot(message[:, :depth], key_value_weight, preferred_element_type=f32)

    def kv_part(s):
        head = head_of(info[s])
        key = lax.dynamic_slice_in_dim(kv, head * HEAD_SIZE, HEAD_SIZE, 1)
        value = lax.dynamic_slice_in_dim(kv, (KEY_HEADS + head) * HEAD_SIZE, HEAD_SIZE, 1)
        return jnp.concatenate([key, value], axis=1)

    h = rows // 2
    stages = [([0], [message])]
    a, b = message, message
    ka, kb = kv_part(half)[:h].astype(bf16), kv_part(half)[h:].astype(bf16)
    for s in range(1, half):
        a, b, ka, kb = ring.right(a), ring.left(b), ring.right(ka), ring.left(kb)
        a, b, ka, kb = lax.optimization_barrier((a, b, ka, kb))
        stages.append(([n - s, s], [a, b]))
        pa, pb = kv_part(half - s), kv_part(n - half + s)
        if s == 1:
            pa = jnp.concatenate([pa[:h] + ka.astype(f32), pa[h:]], axis=0)
            pb = jnp.concatenate([pb[:h], pb[h:] + kb.astype(f32)], axis=0)
        else:
            pa, pb = pa + ka.astype(f32), pb + kb.astype(f32)
        ka, kb = pa.astype(bf16), pb.astype(bf16)
    stages.append(([half], [ring.right(a[:h]), ring.left(b[h:])]))
    ka, kb = ring.right(ka), ring.left(kb)
    kv_came = [ka, kb] if half > 1 else [jnp.concatenate([ka, kb], axis=0)]
    accs = None
    for offsets, blocks in stages:
        accs = query_step(info, offsets, blocks, query_matrix, depth, accs)
    query, low = accs
    heads_out = attend(
        ring,
        width,
        tenant_blocks,
        cached_length,
        tenant_adapter,
        info,
        query,
        low,
        adapter_up,
        cache,
        far_cache,
        kv,
        kv_came,
        head_of,
    )
    got = ring_sum(ring, info, heads_out, attention_out_weight, depth)
    second = final_step(info, heads_out, attention_out_weight, depth, got, first)
    return (
        second.reshape(tenants, length, depth),
        final_state.reshape(tenants, heads, HDIM, STATE),
    )


def solution(mesh):
    in_specs = (
        P(("groups", "pool"), None, "tensor"),
        P(None, None, "tensor"),
        P("tensor", None),
        P(None, "tensor"),
        P(),
        P(("groups", "pool"), None, "tensor"),
        P(("groups", "pool"), None, None),
        P("tensor"),
        P("tensor"),
        P("tensor"),
        P("tensor"),
        P("tensor", None),
        P(("groups", "pool"), "tensor", None, None),
        P(("groups", "pool")),
        P(),
        P(None, "tensor"),
        P(None, "tensor", None),
        P(None, None, "tensor"),
        P(("groups", "pool")),
        P("tensor", None),
        P(("groups", "tensor"), None, None),
        P(("groups", "pool"), None),
        P(("groups", "pool")),
        P("tensor", None),
    )
    out_specs = (P(("groups", "pool"), None, "tensor"), P(("groups", "pool"), "tensor", None, None))
    ring = Ring(mesh.shape["tensor"], mesh.shape["pool"])
    return jax.shard_map(
        functools.partial(per_device, ring),
        mesh=mesh,
        in_specs=in_specs,
        out_specs=out_specs,
        check_vma=False,
    )
```

time: 281 us -> 269 us (0.957)
  Pallas kernels: 52.7 us -> 124 us
  matrix products: 56.4 us -> 2.07 us
  waiting for transfers between devices: 73 us -> 56.5 us
  other arithmetic: 18.5 us -> 6.22 us
  starting transfers between devices: 59.9 us -> 54.1 us
  local copies, waits for them, and re-layouts: 6.98 us -> 12.2 us
    pallas_call x7 -> x22, Pallas kernels: 52.7 us -> 124 us  [the longest x8 39.2 us: send_step(): pl.pallas_call(functools.partial(send_kernel, kind, len(offsets), steps,...]
    dot_general x27 -> x2, matrix products: 56.4 us -> 2.07 us  [the longest x1 1.69 us: per_device(): jnp.dot(message[:, :depth], key_value_weight, preferred_element_type=f32)]
    ppermute x20, waiting for transfers between devices: 26.7 us -> 49 us  [right(): return lax.ppermute(x, 'tensor', self.cw)]
    ppermute x19 -> x9, waiting for transfers between devices: 19.8 us -> 0.02 us  [the longest x7 0.02 us: per_device(): block = lax.ppermute(block, 'tensor', [(i, (i + s) % n) for i in range(n)])]
    ppermute x20, waiting for transfers between devices: 26.5 us -> 7.52 us  [left(): return lax.ppermute(x, 'tensor', self.ccw)]
    ppermute x19 -> x9, starting transfers between devices: 21.8 us -> 12.1 us  [the longest x7 11.6 us: per_device(): block = lax.ppermute(block, 'tensor', [(i, (i + s) % n) for i in range(n)])]
    unnamed x61 -> x103, local copies, waits for them, and re-layouts: 0.9 us -> 8.64 us
    another operation x11 -> x5, other arithmetic: 5.79 us -> 0.04 us  [the longest x3 5.64 us: per_device(): ids = jnp.stack([near[s] for s, _ in stage])]
  transfers between devices with their start and end apart: 59 -> 49, of which waited for: 29 -> 18; matrix products, arithmetic and copies ran while one was open for 27% -> 3% of each run, Pallas kernels for 17% -> 28%
where the time goes in v2:
time: 269 us; the launch traced here: 268 us
  Pallas kernels  124 us (46%)
  waiting for transfers between devices  56.5 us (21%)
  starting transfers between devices  54.1 us (20%)
  between operations  13.1 us (5%)
  local copies, waits for them, and re-layouts  12.2 us (5%)
  other arithmetic  6.22 us (2%)
    ppermute x20, waiting for transfers between devices, right(): return lax.ppermute(x, 'tensor', self.cw)  49 us
    pallas_call x8, Pallas kernels, send_step(): pl.pallas_call(functools.partial(send_kernel, kind, len(offsets), steps,...  39.2 us
    pallas_call x5, Pallas kernels, in_product(): pl.pallas_call(functools.partial(in_kernel, offsets, count, accs is None)...  35.9 us
    ppermute x20, starting transfers between devices, right(): return lax.ppermute(x, 'tensor', self.cw)  25.4 us
    pallas_call x5, Pallas kernels, query_step(): pl.pallas_call(functools.partial(query_kernel, offsets, count, accs is No...  23.6 us
    ppermute x20, starting transfers between devices, left(): return lax.ppermute(x, 'tensor', self.ccw)  16.6 us
    ppermute x7, starting transfers between devices, per_device(): block = lax.ppermute(block, 'tensor', [(i, (i + s) % n) for i in range(n)])  11.6 us
    pallas_call x1, Pallas kernels, state_pass(): pl.pallas_call(functools.partial(state_kernel, slots=slots), grid_spec=pl...  9.7 us
  transfers between devices with their start and end apart: 49, of which 18 were waited for; matrix products, arithmetic and copies ran while one was open for 3% of the time, Pallas kernels for 28%

profile of v2, /device:TPU:0, one launch (start us, length us, event | category | flops | bytes accessed | tf_op | source)
XLA Modules:
  0.0 268.0 jit_solution(12879985093865170860)
XLA Ops:
  0.7 4.9 %bitcast_convert_fusion = bf16[6,1024,256]{2,1,0:T(8,128)(2,1)} fusion(f32[6,16,64,256]{3,2,1,0:T(8,128)} %param.37), kind=kLoop, calls=%fused_computation.60 | loop fusion | flops 1572864 | bytes 9437184 | tf_op jit(solution)/shard_map/convert_element_type | solution.py:836
  9.1 10.4 %collective-permute-done.refs_0_ = bf16[128,1664]{1,0:T(8,128)(2,1)S(1)} collective-permute-done((bf16[128,1664]{1,0:T(8,128)(2,1)S(1)}, bf16[128,1664]{1,0:T(8,128)(2,1)S(1)}, u32[]{:S(2)}, u32[]{:S(2)}) %collective-permute-start) | collective-permute-done | bytes 426016 | tf_op jit(solution)/shard_map/ppermute | solution.py:57
  21.6 9.6 %collective-permute-done.1.refs_0_ = bf16[128,1664]{1,0:T(8,128)(2,1)S(1)} collective-permute-done((bf16[128,1664]{1,0:T(8,128)(2,1)S(1)}, bf16[128,1664]{1,0:T(8,128)(2,1)S(1)}, u32[]{:S(2)}, u32[]{:S(2)}) %collective-permute-start.1) | collective-permute-done | bytes 426016 | tf_op jit(solution)/shard_map/ppermute | solution.py:57
  36.9 5.6 %in_product.5 = (f32[256,1024]{1,0:T(8,128)}, f32[128,640]{1,0:T(8,128)}) custom-call(s32[10]{0:T(128)} %get-tuple-element.134.info, bf16[128,1664]{1,0:T(8,128)(2,1)} %copy-done.5, bf16[8192,2,1024]{2,1,0:T(2,128)(2,1)} %refs_2_.11), custom_call_target="tpu_custom_call" | custom-call | flops 1073741824 | bytes 8388608 | tf_op jit(solution)/shard_map/in_product/pallas_call | solution.py:144
  42.5 8.1 %in_product.6 = (f32[256,1024]{1,0:T(8,128)}, f32[128,640]{1,0:T(8,128)}) custom-call(s32[10]{0:T(128)} %get-tuple-element.134.info, bf16[128,1664]{1,0:T(8,128)(2,1)} %copy-done.14, bf16[128,1664]{1,0:T(8,128)(2,1)} %copy-done.15, bf16[8192,2,1024]{2,1,0:T(2,128)(2,1)} %refs_2_.11, ...), custom_call_target="tpu_custom_call", output_to_operand_aliasing={{0}: (4, {}), {1}: (5, {})} | custom-call | flops 2147483648 | bytes 16777216 | tf_op jit(solution)/shard_map/in_product/pallas_call | solution.py:144
  53.0 8.1 %in_product.7 = (f32[256,1024]{1,0:T(8,128)}, f32[128,640]{1,0:T(8,128)}) custom-call(s32[10]{0:T(128)} %get-tuple-element.134.info, bf16[128,1664]{1,0:T(8,128)(2,1)} %copy-done.12, bf16[128,1664]{1,0:T(8,128)(2,1)} %copy-done.13, bf16[8192,2,1024]{2,1,0:T(2,128)(2,1)} %refs_2_.11, ...), custom_call_target="tpu_custom_call", output_to_operand_aliasing={{0}: (4, {}), {1}: (5, {})} | custom-call | flops 2147483648 | bytes 16777216 | tf_op jit(solution)/shard_map/in_product/pallas_call | solution.py:144
  61.0 8.1 %in_product.8 = (f32[256,1024]{1,0:T(8,128)}, f32[128,640]{1,0:T(8,128)}) custom-call(s32[10]{0:T(128)} %get-tuple-element.134.info, bf16[128,1664]{1,0:T(8,128)(2,1)} %copy-done.6, bf16[128,1664]{1,0:T(8,128)(2,1)} %copy-done.7, bf16[8192,2,1024]{2,1,0:T(2,128)(2,1)} %refs_2_.11, ...), custom_call_target="tpu_custom_call", output_to_operand_aliasing={{0}: (4, {}), {1}: (5, {})} | custom-call | flops 2147483648 | bytes 16777216 | tf_op jit(solution)/shard_map/in_product/pallas_call | solution.py:144
  69.8 6.1 %in_product.9 = (f32[256,1024]{1,0:T(8,128)}, f32[128,640]{1,0:T(8,128)}) custom-call(s32[10]{0:T(128)} %get-tuple-element.134.info, bf16[64,1664]{1,0:T(8,128)(2,1)} %copy-done.33, bf16[64,1664]{1,0:T(8,128)(2,1)} %copy-done.34, bf16[8192,2,1024]{2,1,0:T(2,128)(2,1)} %refs_2_.11, ...), custom_call_target="tpu_custom_call", output_to_operand_aliasing={{0}: (4, {}), {1}: (5, {})} | custom-call | flops 1073741824 | bytes 8388608 | tf_op jit(solution)/shard_map/in_product/pallas_call | solution.py:144
  75.9 9.7 %state_pass.1 = (bf16[128,1024]{1,0:T(8,128)(2,1)}, f32[128,1]{1,0:T(8,128)}, f32[4,1024,256]{2,1,0:T(8,128)}) custom-call(s32[4]{0:T(128)} %slot.1, s32[10]{0:T(128)} %get-tuple-element.134.info, f32[256,1024]{1,0:T(8,128)} %get-tuple-element.64.x_ref.z_ref, f32[256,1024]{1,0:T(8,128)} %get-tuple-element.64.x_ref.z_ref, ...), custom_call_target="tpu_custom_call" | custom-call | flops 201326592 | bytes 10485760 | tf_op jit(solution)/shard_map/state_pass/pallas_call | solution.py:648
  96.7 5.5 %send_step.9 = (bf16[128,1152]{1,0:T(8,128)(2,1)}, bf16[128,1152]{1,0:T(8,128)(2,1)}) custom-call(s32[10]{0:T(128)} %get-tuple-element.134.info, bf16[128,1024]{1,0:T(8,128)(2,1)} %get-tuple-element.66.lhs_ref, bf16[1024,8192]{1,0:T(8,128)(2,1)} %w_ref.14, f32[128,1]{1,0:T(8,128)} %get-tuple-element.67.refs_0_.refs_2_, bf16[64,1152]{1,0:T(8,128)(2,1)} %copy-done.36, ...), custom_call_target="tpu_custom_call" | custom-call | flops 536870912 | bytes 4194304 | tf_op jit(solution)/shard_map/send_step/pallas_call | solution.py:252
  124.1 5.6 %send_step.10 = (bf16[128,1152]{1,0:T(8,128)(2,1)}, bf16[128,1152]{1,0:T(8,128)(2,1)}) custom-call(s32[10]{0:T(128)} %get-tuple-element.134.info, bf16[128,1024]{1,0:T(8,128)(2,1)} %get-tuple-element.66.lhs_ref, bf16[1024,8192]{1,0:T(8,128)(2,1)} %w_ref.14, f32[128,1]{1,0:T(8,128)} %get-tuple-element.67.refs_0_.refs_2_, bf16[128,1152]{1,0:T(8,128)(2,1)} %copy-done.16, ...), custom_call_target="tpu_custom_call" | custom-call | flops 536870912 | bytes 4194304 | tf_op jit(solution)/shard_map/send_step/pallas_call | solution.py:252
  139.6 5.6 %send_step.11 = (bf16[128,1152]{1,0:T(8,128)(2,1)}, bf16[128,1152]{1,0:T(8,128)(2,1)}) custom-call(s32[10]{0:T(128)} %get-tuple-element.134.info, bf16[128,1024]{1,0:T(8,128)(2,1)} %get-tuple-element.66.lhs_ref, bf16[1024,8192]{1,0:T(8,128)(2,1)} %w_ref.14, f32[128,1]{1,0:T(8,128)} %get-tuple-element.67.refs_0_.refs_2_, bf16[128,1152]{1,0:T(8,128)(2,1)} %copy-done.18, ...), custom_call_target="tpu_custom_call" | custom-call | flops 536870912 | bytes 4194304 | tf_op jit(solution)/shard_map/send_step/pallas_call | solution.py:252
  147.2 4.9 %collective-permute-done.15.refs_0_ = bf16[128,1152]{1,0:T(8,128)(2,1)S(1)} collective-permute-done((bf16[128,1152]{1,0:T(8,128)(2,1)}, bf16[128,1152]{1,0:T(8,128)(2,1)S(1)}, u32[]{:S(2)}, u32[]{:S(2)}) %collective-permute-start.15) | collective-permute-done | bytes 294944 | tf_op jit(solution)/shard_map/ppermute | solution.py:57
  153.1 5.1 %mixer_step.1 = (bf16[128,1024]{1,0:T(8,128)(2,1)}, bf16[128,1152]{1,0:T(8,128)(2,1)}) custom-call(s32[10]{0:T(128)} %get-tuple-element.134.info, s32[4]{0:T(128)} %adapter.3, bf16[128,1024]{1,0:T(8,128)(2,1)} %get-tuple-element.66.lhs_ref, bf16[1024,8192]{1,0:T(8,128)(2,1)} %w_ref.14, bf16[128,1152]{1,0:T(8,128)(2,1)} %copy-done.20, ...), custom_call_target="tpu_custom_call" | custom-call | flops 268435456 | bytes 2097152 | tf_op jit(solution)/shard_map/mixer_step/pallas_call | solution.py:348
  180.8 5.4 %query_step.6 = (f32[128,1024]{1,0:T(8,128)}, f32[128,128]{1,0:T(8,128)}) custom-call(s32[10]{0:T(128)} %get-tuple-element.134.info, bf16[128,1152]{1,0:T(8,128)(2,1)} %copy-done.22, bf16[128,1152]{1,0:T(8,128)(2,1)} %copy-done.23, bf16[8192,1024]{1,0:T(8,128)(2,1)} %refs_2_.15, ...), custom_call_target="tpu_custom_call", output_to_operand_aliasing={{0}: (4, {}), {1}: (5, {})} | custom-call | flops 536870912 | bytes 4194304 | tf_op jit(solution)/shard_map/query_step/pallas_call | solution.py:455
  186.2 5.4 %query_step.7 = (f32[128,1024]{1,0:T(8,128)}, f32[128,128]{1,0:T(8,128)}) custom-call(s32[10]{0:T(128)} %get-tuple-element.134.info, bf16[128,1152]{1,0:T(8,128)(2,1)} %copy-done.24, bf16[128,1152]{1,0:T(8,128)(2,1)} %copy-done.25, bf16[8192,1024]{1,0:T(8,128)(2,1)} %refs_2_.15, ...), custom_call_target="tpu_custom_call", output_to_operand_aliasing={{0}: (4, {}), {1}: (5, {})} | custom-call | flops 536870912 | bytes 4194304 | tf_op jit(solution)/shard_map/query_step/pallas_call | solution.py:455
  195.9 5.4 %query_step.8 = (f32[128,1024]{1,0:T(8,128)}, f32[128,128]{1,0:T(8,128)}) custom-call(s32[10]{0:T(128)} %get-tuple-element.134.info, bf16[128,1152]{1,0:T(8,128)(2,1)} %copy-done.9, bf16[128,1152]{1,0:T(8,128)(2,1)} %copy-done.10, bf16[8192,1024]{1,0:T(8,128)(2,1)} %refs_2_.15, ...), custom_call_target="tpu_custom_call", output_to_operand_aliasing={{0}: (4, {}), {1}: (5, {})} | custom-call | flops 536870912 | bytes 4194304 | tf_op jit(solution)/shard_map/query_step/pallas_call | solution.py:455
  206.8 6.7 %attend.1.lhs_ref = bf16[128,1024]{1,0:T(8,128)(2,1)} custom-call(s32[4,8]{1,0:T(4,128)} %table.1, s32[4]{0:T(128)} %limit.1, s32[4]{0:T(128)} %adapter.3, s32[10]{0:T(128)} %get-tuple-element.134.info, f32[128,1024]{1,0:T(8,128)} %get-tuple-element.95.q_ref, f32[128,128]{1,0:T(8,128)} %get-tuple-element.96.low_ref, bf16[16,64,1024]{2,1,0:T(8,128)(2,1)} %up_ref.1, ...), custom_call_target="tpu_custom_call" | custom-call | flops 150994944 | bytes 2883584 | tf_op jit(solution)/shard_map/attend/pallas_call | solution.py:761
  223.6 5.2 %send_step.13 = (bf16[128,1024]{1,0:T(8,128)(2,1)}, bf16[128,1024]{1,0:T(8,128)(2,1)}) custom-call(s32[10]{0:T(128)} %get-tuple-element.134.info, bf16[128,1024]{1,0:T(8,128)(2,1)} %attend.1.lhs_ref, bf16[1024,8192]{1,0:T(8,128)(2,1)} %w_ref.19, bf16[64,1024]{1,0:T(8,128)(2,1)} %copy-done.39, bf16[64,1024]{1,0:T(8,128)(2,1)} %copy-done.40), custom_call_target="tpu_custom_call" | custom-call | flops 536870912 | bytes 4194304 | tf_op jit(solution)/shard_map/send_step/pallas_call | solution.py:252
  230.8 4.6 %collective-permute-done.43.refs_0_ = bf16[128,1024]{1,0:T(8,128)(2,1)S(1)} collective-permute-done((bf16[128,1024]{1,0:T(8,128)(2,1)}, bf16[128,1024]{1,0:T(8,128)(2,1)S(1)}, u32[]{:S(2)}, u32[]{:S(2)}) %collective-permute-start.43) | collective-permute-done | bytes 262176 | tf_op jit(solution)/shard_map/ppermute | solution.py:57
  236.8 5.3 %send_step.14 = (bf16[128,1024]{1,0:T(8,128)(2,1)}, bf16[128,1024]{1,0:T(8,128)(2,1)}) custom-call(s32[10]{0:T(128)} %get-tuple-element.134.info, bf16[128,1024]{1,0:T(8,128)(2,1)} %attend.1.lhs_ref, bf16[1024,8192]{1,0:T(8,128)(2,1)} %w_ref.19, bf16[128,1024]{1,0:T(8,128)(2,1)} %copy-done.26, bf16[128,1024]{1,0:T(8,128)(2,1)} %copy-done.28), custom_call_target="tpu_custom_call" | custom-call | flops 536870912 | bytes 4194304 | tf_op jit(solution)/shard_map/send_step/pallas_call | solution.py:252
  244.2 4.6 %collective-permute-done.45.refs_0_ = bf16[128,1024]{1,0:T(8,128)(2,1)S(1)} collective-permute-done((bf16[128,1024]{1,0:T(8,128)(2,1)}, bf16[128,1024]{1,0:T(8,128)(2,1)S(1)}, u32[]{:S(2)}, u32[]{:S(2)}) %collective-permute-start.45) | collective-permute-done | bytes 262176 | tf_op jit(solution)/shard_map/ppermute | solution.py:57
  250.2 5.3 %send_step.15 = (bf16[128,1024]{1,0:T(8,128)(2,1)}, bf16[128,1024]{1,0:T(8,128)(2,1)}) custom-call(s32[10]{0:T(128)} %get-tuple-element.134.info, bf16[128,1024]{1,0:T(8,128)(2,1)} %attend.1.lhs_ref, bf16[1024,8192]{1,0:T(8,128)(2,1)} %w_ref.19, bf16[128,1024]{1,0:T(8,128)(2,1)} %copy-done.27, bf16[128,1024]{1,0:T(8,128)(2,1)} %copy-done.29), custom_call_target="tpu_custom_call" | custom-call | flops 536870912 | bytes 4194304 | tf_op jit(solution)/shard_map/send_step/pallas_call | solution.py:252
  257.5 4.6 %collective-permute-done.47.refs_0_ = bf16[128,1024]{1,0:T(8,128)(2,1)S(1)} collective-permute-done((bf16[128,1024]{1,0:T(8,128)(2,1)}, bf16[128,1024]{1,0:T(8,128)(2,1)S(1)}, u32[]{:S(2)}, u32[]{:S(2)}) %collective-permute-start.47) | collective-permute-done | bytes 262176 | tf_op jit(solution)/shard_map/ppermute | solution.py:57
  (231 shorter events, 105.5 us)
Async XLA Ops:
  5.6 70.3 %collective-permute-start.8 = (bf16[6,1024,256]{2,1,0:T(8,128)(2,1)}, bf16[6,1024,256]{2,1,0:T(8,128)(2,1)}, u32[]{:S(2)}, u32[]{:S(2)}) collective-permute-start(bf16[6,1024,256]{2,1,0:T(8,128)(2,1)} %bitcast_convert_fusion), channel_id=1, source_target_pairs={{0,1},{1,0},{2,3},{3,2},{4,5},{5,4},{6,7},{7,6},{8,9},{9,8},{10,11... | collective-permute-start | bytes 9437192 | tf_op jit(solution)/shard_map/ppermute | solution.py:836
  6.5 13.1 %collective-permute-start = (bf16[128,1664]{1,0:T(8,128)(2,1)S(1)}, bf16[128,1664]{1,0:T(8,128)(2,1)S(1)}, u32[]{:S(2)}, u32[]{:S(2)}) collective-permute-start(bf16[128,1664]{1,0:T(8,128)(2,1)S(1)} %pad_maximum_fusion.refs_0_), channel_id=1, source_target_pairs={{0,4},{4,8},{8,12},{12,14},{14,10},{10,6},{6,2},{2,0},{1,5},{5,9},... | collective-permute-start | bytes 1277960 | tf_op jit(solution)/shard_map/ppermute | solution.py:57
  9.1 12.2 %collective-permute-start.4 = (bf16[128,1664]{1,0:T(8,128)(2,1)S(1)}, bf16[128,1664]{1,0:T(8,128)(2,1)S(1)}, u32[]{:S(2)}, u32[]{:S(2)}) collective-permute-start(bf16[128,1664]{1,0:T(8,128)(2,1)S(1)} %pad_maximum_fusion.refs_0_), channel_id=1, source_target_pairs={{0,2},{4,0},{8,4},{12,8},{14,12},{10,14},{6,10},{2,6},{1,3},{5,1},... | collective-permute-start | bytes 1277960 | tf_op jit(solution)/shard_map/ppermute | solution.py:60
  19.5 11.6 %collective-permute-start.1 = (bf16[128,1664]{1,0:T(8,128)(2,1)S(1)}, bf16[128,1664]{1,0:T(8,128)(2,1)S(1)}, u32[]{:S(2)}, u32[]{:S(2)}) collective-permute-start(bf16[128,1664]{1,0:T(8,128)(2,1)S(1)} %collective-permute-done.refs_0_), channel_id=1, source_target_pairs={{0,4},{4,8},{8,12},{12,14},{14,10},{10,6},{6,2},{2,0},{1,5},{5,9},... | collective-permute-start | bytes 1277960 | tf_op jit(solution)/shard_map/ppermute | solution.py:57
  21.3 11.4 %collective-permute-start.5 = (bf16[128,1664]{1,0:T(8,128)(2,1)S(1)}, bf16[128,1664]{1,0:T(8,128)(2,1)S(1)}, u32[]{:S(2)}, u32[]{:S(2)}) collective-permute-start(bf16[128,1664]{1,0:T(8,128)(2,1)S(1)} %collective-permute-done.4.refs_1_), channel_id=1, source_target_pairs={{0,2},{4,0},{8,4},{12,8},{14,12},{10,14},{6,10},{2,6},{1,3},{5,1},... | collective-permute-start | bytes 1277960 | tf_op jit(solution)/shard_map/ppermute | solution.py:60
  31.2 19.4 %collective-permute-start.2 = (bf16[128,1664]{1,0:T(8,128)(2,1)S(1)}, bf16[128,1664]{1,0:T(8,128)(2,1)S(1)}, u32[]{:S(2)}, u32[]{:S(2)}) collective-permute-start(bf16[128,1664]{1,0:T(8,128)(2,1)S(1)} %collective-permute-done.1.refs_0_), channel_id=1, source_target_pairs={{0,4},{4,8},{8,12},{12,14},{14,10},{10,6},{6,2},{2,0},{1,5},{5,9},... | collective-permute-start | bytes 1277960 | tf_op jit(solution)/shard_map/ppermute | solution.py:57
  32.8 19.5 %collective-permute-start.6 = (bf16[128,1664]{1,0:T(8,128)(2,1)S(1)}, bf16[128,1664]{1,0:T(8,128)(2,1)S(1)}, u32[]{:S(2)}, u32[]{:S(2)}) collective-permute-start(bf16[128,1664]{1,0:T(8,128)(2,1)S(1)} %collective-permute-done.5.refs_1_), channel_id=1, source_target_pairs={{0,2},{4,0},{8,4},{12,8},{14,12},{10,14},{6,10},{2,6},{1,3},{5,1},... | collective-permute-start | bytes 1277960 | tf_op jit(solution)/shard_map/ppermute | solution.py:60
  50.6 18.5 %collective-permute-start.3 = (bf16[64,1664]{1,0:T(8,128)(2,1)S(1)}, bf16[64,1664]{1,0:T(8,128)(2,1)S(1)}, u32[]{:S(2)}, u32[]{:S(2)}) collective-permute-start(bf16[64,1664]{1,0:T(8,128)(2,1)S(1)} %slice.94), channel_id=1, source_target_pairs={{0,4},{4,8},{8,12},{12,14},{14,10},{10,6},{6,2},{2,0},{1,5},{5,9},... | collective-permute-start | bytes 638984 | tf_op jit(solution)/shard_map/ppermute | solution.py:57
  52.3 16.8 %collective-permute-start.7 = (bf16[64,1664]{1,0:T(8,128)(2,1)S(1)}, bf16[64,1664]{1,0:T(8,128)(2,1)S(1)}, u32[]{:S(2)}, u32[]{:S(2)}) collective-permute-start(bf16[64,1664]{1,0:T(8,128)(2,1)S(1)} %slice.95), channel_id=1, source_target_pairs={{0,2},{4,0},{8,4},{12,8},{14,12},{10,14},{6,10},{2,6},{1,3},{5,1},... | collective-permute-start | bytes 638984 | tf_op jit(solution)/shard_map/ppermute | solution.py:60
  102.1 20.0 %collective-permute-start.11 = (bf16[128,1152]{1,0:T(8,128)(2,1)}, bf16[128,1152]{1,0:T(8,128)(2,1)S(1)}, u32[]{:S(2)}, u32[]{:S(2)}) collective-permute-start(bf16[128,1152]{1,0:T(8,128)(2,1)} %get-tuple-element.70), channel_id=1, source_target_pairs={{0,4},{4,8},{8,12},{12,14},{14,10},{10,6},{6,2},{2,0},{1,5},{5,9},... | collective-permute-start | bytes 884744 | tf_op jit(solution)/shard_map/ppermute | solution.py:57
  103.7 19.7 %collective-permute-start.12 = (bf16[128,1152]{1,0:T(8,128)(2,1)}, bf16[128,1152]{1,0:T(8,128)(2,1)S(1)}, u32[]{:S(2)}, u32[]{:S(2)}) collective-permute-start(bf16[128,1152]{1,0:T(8,128)(2,1)} %get-tuple-element.71), channel_id=1, source_target_pairs={{0,2},{4,0},{8,4},{12,8},{14,12},{10,14},{6,10},{2,6},{1,3},{5,1},... | collective-permute-start | bytes 884744 | tf_op jit(solution)/shard_map/ppermute | solution.py:60
  116.4 14.8 %collective-permute-start.31 = (bf16[8,16,256]{2,1,0:T(8,128)(2,1)S(1)}, bf16[8,16,256]{2,1,0:T(8,128)(2,1)S(1)}, u32[]{:S(2)}, u32[]{:S(2)}) collective-permute-start(bf16[8,16,256]{2,1,0:T(8,128)(2,1)S(1)} %get-tuple-element.130), channel_id=1, source_target_pairs={{0,2},{2,4},{4,6},{6,8},{8,10},{10,12},{12,14},{14,0},{1,3},{3,5},... | collective-permute-start | bytes 196616 | tf_op jit(solution)/shard_map/ppermute | solution.py:856
  117.0 14.7 %collective-permute-start.32 = (bf16[8,16,256]{2,1,0:T(8,128)(2,1)S(1)}, bf16[8,16,256]{2,1,0:T(8,128)(2,1)S(1)}, u32[]{:S(2)}, u32[]{:S(2)}) collective-permute-start(bf16[8,16,256]{2,1,0:T(8,128)(2,1)S(1)} %get-tuple-element.129), channel_id=1, source_target_pairs={{0,4},{2,6},{4,8},{6,10},{8,12},{10,14},{12,0},{14,2},{1,5},{3,7},... | collective-permute-start | bytes 196616 | tf_op jit(solution)/shard_map/ppermute | solution.py:856
  118.6 14.9 %collective-permute-start.33 = (bf16[8,16,256]{2,1,0:T(8,128)(2,1)S(1)}, bf16[8,16,256]{2,1,0:T(8,128)(2,1)S(1)}, u32[]{:S(2)}, u32[]{:S(2)}) collective-permute-start(bf16[8,16,256]{2,1,0:T(8,128)(2,1)S(1)} %get-tuple-element.128), channel_id=1, source_target_pairs={{0,6},{2,8},{4,10},{6,12},{8,14},{10,0},{12,2},{14,4},{1,7},{3,9},... | collective-permute-start | bytes 196616 | tf_op jit(solution)/shard_map/ppermute | solution.py:856
  122.1 23.3 %collective-permute-start.34 = (bf16[8,16,256]{2,1,0:T(8,128)(2,1)S(1)}, bf16[8,16,256]{2,1,0:T(8,128)(2,1)S(1)}, u32[]{:S(2)}, u32[]{:S(2)}) collective-permute-start(bf16[8,16,256]{2,1,0:T(8,128)(2,1)S(1)} %get-tuple-element.127), channel_id=1, source_target_pairs={{0,8},{2,10},{4,12},{6,14},{8,0},{10,2},{12,4},{14,6},{1,9},{3,11}... | collective-permute-start | bytes 196616 | tf_op jit(solution)/shard_map/ppermute | solution.py:856
  131.7 15.5 %collective-permute-start.35 = (bf16[8,16,256]{2,1,0:T(8,128)(2,1)S(1)}, bf16[8,16,256]{2,1,0:T(8,128)(2,1)S(1)}, u32[]{:S(2)}, u32[]{:S(2)}) collective-permute-start(bf16[8,16,256]{2,1,0:T(8,128)(2,1)S(1)} %get-tuple-element.126), channel_id=1, source_target_pairs={{0,10},{2,12},{4,14},{6,0},{8,2},{10,4},{12,6},{14,8},{1,11},{3,13... | collective-permute-start | bytes 196616 | tf_op jit(solution)/shard_map/ppermute | solution.py:856
  133.5 13.7 %collective-permute-start.36 = (bf16[8,16,256]{2,1,0:T(8,128)(2,1)S(1)}, bf16[8,16,256]{2,1,0:T(8,128)(2,1)S(1)}, u32[]{:S(2)}, u32[]{:S(2)}) collective-permute-start(bf16[8,16,256]{2,1,0:T(8,128)(2,1)S(1)} %get-tuple-element.125), channel_id=1, source_target_pairs={{0,12},{2,14},{4,0},{6,2},{8,4},{10,6},{12,8},{14,10},{1,13},{3,15... | collective-permute-start | bytes 196616 | tf_op jit(solution)/shard_map/ppermute | solution.py:856
  137.3 34.8 %collective-permute-start.37 = (bf16[8,16,256]{2,1,0:T(8,128)(2,1)S(1)}, bf16[8,16,256]{2,1,0:T(8,128)(2,1)S(1)}, u32[]{:S(2)}, u32[]{:S(2)}) collective-permute-start(bf16[8,16,256]{2,1,0:T(8,128)(2,1)S(1)} %get-tuple-element.124), channel_id=1, source_target_pairs={{0,14},{2,0},{4,2},{6,4},{8,6},{10,8},{12,10},{14,12},{1,15},{3,1}... | collective-permute-start | bytes 196616 | tf_op jit(solution)/shard_map/ppermute | solution.py:856
  172.1 33.9 %collective-permute-start.38 = (bf16[64,16,256]{2,1,0:T(8,128)(2,1)S(1)}, bf16[64,16,256]{2,1,0:T(8,128)(2,1)S(1)}, u32[]{:S(2)}, u32[]{:S(2)}) collective-permute-start(bf16[64,16,256]{2,1,0:T(8,128)(2,1)S(1)} %constant_dynamic-update-slice_fusion.near_ref), channel_id=1, source_target_pairs={{0,1},{1,0},{2,3},{3,2},{4,5},{5,4},{6,7},{7,6},{8,9},{9,8},{10,11... | collective-permute-start | bytes 1572872 | tf_op jit(solution)/shard_map/ppermute | solution.py:863
  176.5 15.0 %collective-permute-start.25 = (bf16[128,1152]{1,0:T(8,128)(2,1)S(1)}, bf16[128,1152]{1,0:T(8,128)(2,1)S(1)}, u32[]{:S(2)}, u32[]{:S(2)}) collective-permute-start(bf16[128,1152]{1,0:T(8,128)(2,1)S(1)} %collective-permute-done.21.refs_0_), channel_id=1, source_target_pairs={{0,4},{4,8},{8,12},{12,14},{14,10},{10,6},{6,2},{2,0},{1,5},{5,9},... | collective-permute-start | bytes 884744 | tf_op jit(solution)/shard_map/ppermute | solution.py:57
  177.5 14.1 %collective-permute-start.26 = (bf16[128,1152]{1,0:T(8,128)(2,1)S(1)}, bf16[128,1152]{1,0:T(8,128)(2,1)S(1)}, u32[]{:S(2)}, u32[]{:S(2)}) collective-permute-start(bf16[128,1152]{1,0:T(8,128)(2,1)S(1)} %collective-permute-done.22.refs_1_), channel_id=1, source_target_pairs={{0,2},{4,0},{8,4},{12,8},{14,12},{10,14},{6,10},{2,6},{1,3},{5,1},... | collective-permute-start | bytes 884744 | tf_op jit(solution)/shard_map/ppermute | solution.py:60
  178.6 12.9 %collective-permute-start.27 = (bf16[128,256]{1,0:T(8,128)(2,1)S(1)}, bf16[128,256]{1,0:T(8,128)(2,1)S(1)}, u32[]{:S(2)}, u32[]{:S(2)}) collective-permute-start(bf16[128,256]{1,0:T(8,128)(2,1)S(1)} %fusion.2), channel_id=1, source_target_pairs={{0,4},{4,8},{8,12},{12,14},{14,10},{10,6},{6,2},{2,0},{1,5},{5,9},... | collective-permute-start | bytes 196616 | tf_op jit(solution)/shard_map/ppermute | solution.py:57
  179.6 11.9 %collective-permute-start.28 = (bf16[128,256]{1,0:T(8,128)(2,1)S(1)}, bf16[128,256]{1,0:T(8,128)(2,1)S(1)}, u32[]{:S(2)}, u32[]{:S(2)}) collective-permute-start(bf16[128,256]{1,0:T(8,128)(2,1)S(1)} %fusion.3), channel_id=1, source_target_pairs={{0,2},{4,0},{8,4},{12,8},{14,12},{10,14},{6,10},{2,6},{1,3},{5,1},... | collective-permute-start | bytes 196616 | tf_op jit(solution)/shard_map/ppermute | solution.py:60
  193.8 12.2 %collective-permute-start.39 = (bf16[128,256]{1,0:T(8,128)(2,1)S(1)}, bf16[128,256]{1,0:T(8,128)(2,1)S(1)}, u32[]{:S(2)}, u32[]{:S(2)}) collective-permute-start(bf16[128,256]{1,0:T(8,128)(2,1)S(1)} %fusion.4), channel_id=1, source_target_pairs={{0,4},{4,8},{8,12},{12,14},{14,10},{10,6},{6,2},{2,0},{1,5},{5,9},... | collective-permute-start | bytes 196616 | tf_op jit(solution)/shard_map/ppermute | solution.py:57
  (72 other events, 537.4 us)

commit v3 on v2

v3 whole, which is shorter than its diff:
```python
import functools

import jax
import jax.numpy as jnp
from jax import lax
from jax.experimental import pallas as pl
from jax.experimental.pallas import tpu as pltpu
from jax.sharding import PartitionSpec as P

HDIM = 64
STATE = 256
QUERY_HEADS = 64
KEY_HEADS = 8
HEAD_SIZE = 128

epsilon = 1e-05
adapter_scale = 2.0
highest = lax.Precision.HIGHEST
f32 = jnp.float32
bf16 = jnp.bfloat16


def ring_order(n):
    cols = 1
    for c in range(2, n):
        if n % c == 0 and (n // c) % 2 == 0 and c <= n // c:
            cols = c
    if cols == 1:
        return list(range(n))
    rows = n // cols
    order = [r * cols for r in range(rows)]
    for k, r in enumerate(reversed(range(rows))):
        across = list(range(1, cols))
        order += [r * cols + c for c in (across if k % 2 == 0 else across[::-1])]
    return order


class Ring:
    def __init__(self, n, pools):
        self.n = n
        heads = [d * QUERY_HEADS // n // (QUERY_HEADS // KEY_HEADS) for d in range(n)]
        self.half = n // 2
        self.pools = pools
        order = ring_order(n)
        place = {d: i for i, d in enumerate(order)}
        self.table = [
            [order[(place[d] + s) % n] for s in range(n)]
            + [heads[order[(place[d] + s) % n]] for s in range(n)]
            + [d, c]
            for d in range(n)
            for c in range(pools)
        ]
        self.cw = [(order[i], order[(i + 1) % n]) for i in range(n)]
        self.ccw = [(order[i], order[(i - 1) % n]) for i in range(n)]

    def info(self):
        at = lax.axis_index("tensor") * self.pools + lax.axis_index("pool")
        return lax.dynamic_slice_in_dim(jnp.array(self.table, jnp.int32), at, 1, 0)[0]

    def right(self, x):
        return lax.ppermute(x, "tensor", self.cw)

    def left(self, x):
        return lax.ppermute(x, "tensor", self.ccw)

    def masks(self):
        found, m = [], 1
        while m < self.n:
            found.append([(i, i ^ m) for i in range(self.n)])
            m *= 2
        return found

    def gather(self, x, weigh, keep, give):
        n, half = self.n, self.half
        h = x.shape[0] // 2
        pairs = self.masks()
        exchange = pairs + pairs[:1]
        sums, ready = None, ([0], [x])
        a = b = x
        for s in range(1, max(half, len(exchange)) + 1):
            if s == half:
                a, b = a[:h], b[h:]
            if s <= half:
                a, b = self.right(a), self.left(b)
            if s <= len(exchange):
                came = lax.ppermute(give, "tensor", exchange[s - 1])
            if s <= half:
                sums = weigh(*ready, sums)
            if s <= len(exchange):
                a, b, sums, came = lax.optimization_barrier((a, b, sums, came))
            else:
                a, b, sums = lax.optimization_barrier((a, b, sums))
            if s < len(exchange):
                keep = keep + came.astype(f32)
                give = keep.astype(bf16)
            if s <= half:
                ready = ([n - s, s], [a, b]) if s < half else ([half], [a, b])
        return weigh(*ready, sums), keep, came


def split(x):
    high = x.astype(bf16)
    return high, (x - high.astype(f32)).astype(bf16)


def partial_kernel(info, x_ref, w_ref, keep_ref, give_ref, whole):
    whole[...] = jnp.dot(x_ref[...], w_ref[...], preferred_element_type=f32)
    h = keep_ref.shape[0]
    odd = lax.rem(info[info.shape[0] - 2], 2)
    keep_ref[...] = whole[pl.ds(pl.multiple_of(odd * h, 8), h), :]
    give_ref[...] = whole[pl.ds(pl.multiple_of((1 - odd) * h, 8), h), :].astype(bf16)


def partial_product(info, x, weight):
    shape = (x.shape[0] // 2, weight.shape[1])
    return pl.pallas_call(
        partial_kernel,
        grid_spec=pltpu.PrefetchScalarGridSpec(
            num_scalar_prefetch=1,
            grid=(1,),
            in_specs=[
                pl.BlockSpec(x.shape, lambda j, info: (0, 0)),
                pl.BlockSpec(weight.shape, lambda j, info: (0, 0)),
            ],
            out_specs=[pl.BlockSpec(shape, lambda j, info: (0, 0))] * 2,
            scratch_shapes=[pltpu.VMEM((x.shape[0], weight.shape[1]), f32)],
        ),
        out_shape=[jax.ShapeDtypeStruct(shape, f32), jax.ShapeDtypeStruct(shape, bf16)],
        compiler_params=pltpu.CompilerParams(vmem_limit_bytes=12 << 20),
        name="partial_product",
    )(info, x, weight)


def in_kernel(offsets, count, chunks, first_call, info, *refs):
    blocks = refs[:count]
    w_ref = refs[count]
    o_ref, spread, held, arrived = refs[-4:]
    depth = held.shape[1] * chunks
    rows = o_ref.shape[0] // 2
    part = depth // chunks
    copies = []
    for b, offset in enumerate(offsets):
        for c in range(chunks):
            at = pl.multiple_of(info[offset] * depth + c * part, part)
            slot = b * chunks + c
            copies.append(
                pltpu.make_async_copy(w_ref.at[pl.ds(at, part)], held.at[slot], arrived.at[slot])
            )
    for copy in copies:
        copy.start()

    lane = lax.broadcasted_iota(jnp.int32, (128, 512), 1)
    sub = lax.broadcasted_iota(jnp.int32, (128, 512), 0)
    target = jnp.where(lane < 256, 2 * sub, 2 * sub + 257)
    widen = jnp.where(lane == target, 1.0, 0.0).astype(bf16)
    for b in range(len(offsets)):
        base = 0
        for block in [blocks[b]] if count == len(offsets) else blocks:
            r = block.shape[0]
            for p in range(depth // 128):
                piece = block[:, p * 128 : (p + 1) * 128]
                both = jnp.dot(piece, widen, preferred_element_type=f32).astype(bf16)
                spread[b, base : base + r, p * 256 : (p + 1) * 256] = both[:, :256]
                spread[b, rows + base : rows + base + r, p * 256 : (p + 1) * 256] = both[:, 256:]
            base += r

    for slot, copy in enumerate(copies):
        b, c = slot // chunks, slot % chunks
        copy.wait()
        w = held[slot].reshape(2 * part, held.shape[3])
        x = spread[b, :, c * 2 * part : (c + 1) * 2 * part]
        term = jnp.dot(x, w, preferred_element_type=f32)
        if slot == 0:
            o_ref[...] = term if first_call else refs[count + 1][...] + term
        else:
            o_ref[...] += term


def in_product(info, offsets, blocks, weight, depth, acc):
    count = len(blocks)
    rows = sum(b.shape[0] for b in blocks) // len(offsets)
    cols = weight.shape[2]
    chunks = 2 if depth % 512 == 0 else 1
    slots = chunks * len(offsets)

    def fixed(shape):
        return pl.BlockSpec(shape, lambda j, info: (0, 0))

    in_specs = [fixed(b.shape) for b in blocks]
    in_specs.append(pl.BlockSpec(memory_space=pl.ANY))
    operands = [info, *blocks, weight]
    aliases = {}
    shape = (2 * rows, cols)
    if acc is not None:
        in_specs.append(fixed(shape))
        aliases = {len(operands): 0}
        operands.append(acc)
    return pl.pallas_call(
        functools.partial(in_kernel, offsets, count, chunks, acc is None),
        grid_spec=pltpu.PrefetchScalarGridSpec(
            num_scalar_prefetch=1,
            grid=(1,),
            in_specs=in_specs,
            out_specs=fixed(shape),
            scratch_shapes=[
                pltpu.VMEM((len(offsets), 2 * rows, 2 * depth), bf16),
                pltpu.VMEM((slots, depth // chunks, 2, cols), bf16),
                pltpu.SemaphoreType.DMA((slots,)),
            ],
        ),
        out_shape=jax.ShapeDtypeStruct(shape, f32),
        input_output_aliases=aliases,
        compiler_params=pltpu.CompilerParams(vmem_limit_bytes=30 << 20),
        cost_estimate=pl.CostEstimate(
            flops=len(offsets) * 8 * rows * depth * cols,
            bytes_accessed=len(offsets) * depth * cols * 8,
            transcendentals=0,
        ),
        name="in_product",
    )(*operands)


def lanes_of(columns, rows):
    lane = lax.broadcasted_iota(jnp.int32, (rows, 128), 1)
    out = jnp.zeros((rows, 128), f32)
    for at, value in columns:
        out = jnp.where(lane == at, value.astype(f32), out)
    return out.astype(bf16)


def energy_lanes(energy):
    high, low = split(energy)
    return lanes_of([(0, high), (1, low)], energy.shape[0])


def energy_of(lanes):
    wide = lanes.astype(f32)
    return wide[:, 0:1] + wide[:, 1:2]


def join_kernel(kind, depth, with_energy, *refs):
    refs = list(refs)
    e_ref = refs.pop(0) if with_energy else None
    term_ref = refs.pop(0)
    outs = refs[-2:]
    got = refs[:-2]
    rows = term_ref.shape[0] if kind == "first" else term_ref.shape[0] // 2
    h = rows // 2
    sides = [slice(0, h), slice(h, rows)]
    main, tail = slice(0, depth), slice(depth, depth + 128)
    for j in range(2):
        mine, other = sides[j], sides[1 - j]
        out = outs[j]
        if kind == "first":
            out[:, main] = term_ref[mine].astype(bf16)
            if with_energy:
                out[:, tail] = energy_lanes(e_ref[mine])
            continue
        base = j * rows
        if kind == "second":
            own = slice(base + mine.start, base + mine.stop)
            rest = slice(base + other.start, base + other.stop)
            out[mine, main] = (term_ref[own] + got[j][:, main].astype(f32)).astype(bf16)
            out[other, main] = term_ref[rest].astype(bf16)
            if with_energy:
                out[mine, tail] = energy_lanes(e_ref[mine] + energy_of(got[j][:, tail]))
                out[other, tail] = energy_lanes(e_ref[other])
        else:
            whole = slice(base, base + rows)
            out[:, main] = (term_ref[whole] + got[j][:, main].astype(f32)).astype(bf16)
            if with_energy:
                out[:, tail] = energy_lanes(e_ref[...] + energy_of(got[j][:, tail]))


def join(kind, rows, depth, energy, terms, got):
    wide = depth + (0 if energy is None else 128)
    high = rows // 2 if kind == "first" else rows
    operands = ([] if energy is None else [energy]) + [terms] + got
    return pl.pallas_call(
        functools.partial(join_kernel, kind, depth, energy is not None),
        out_shape=[jax.ShapeDtypeStruct((high, wide), bf16)] * 2,
        compiler_params=pltpu.CompilerParams(vmem_limit_bytes=12 << 20),
        cost_estimate=pl.CostEstimate(flops=0, bytes_accessed=rows * wide * 8, transcendentals=0),
        name="join",
    )(*operands)


def term_kernel(info, lhs_ref, w_ref, o_ref):
    o_ref[...] = jnp.dot(lhs_ref[...], w_ref[...], preferred_element_type=f32)


def terms_of(info, offsets, lhs, weight, depth):
    rows = lhs.shape[0]
    return pl.pallas_call(
        term_kernel,
        grid_spec=pltpu.PrefetchScalarGridSpec(
            num_scalar_prefetch=1,
            grid=(len(offsets), 1),
            in_specs=[
                fixed_block(lhs.shape),
                pl.BlockSpec((weight.shape[0], depth), column_block(offsets, 1)),
            ],
            out_specs=pl.BlockSpec((rows, depth), lambda j, c, info: (j, 0)),
        ),
        out_shape=jax.ShapeDtypeStruct((len(offsets) * rows, depth), f32),
        compiler_params=pltpu.CompilerParams(vmem_limit_bytes=46 << 20),
        cost_estimate=pl.CostEstimate(
            flops=len(offsets) * 2 * rows * depth * weight.shape[0],
            bytes_accessed=len(offsets) * depth * weight.shape[0] * 2,
            transcendentals=0,
        ),
        name="terms",
    )(info, lhs, weight)


def tile_of(depth):
    return min(1024, depth)


def column_block(offsets, steps):
    def at(j, c, info, *more):
        device = info[offsets[0]]
        for b in range(1, len(offsets)):
            device = jnp.where(j == b, info[offsets[b]], device)
        return (0, device * steps + c)

    return at


def fixed_block(shape):
    return pl.BlockSpec(shape, lambda j, c, *s: (0,) * len(shape))


def ring_sum(ring, info, lhs, weight, depth, energy=None):
    n, half = ring.n, ring.half
    rows = lhs.shape[0]
    terms = terms_of(info, [half], lhs, weight, depth)
    a, b = join("first", rows, depth, energy, terms, [])
    for d in range(half - 1, -1, -1):
        lhs, a, b = lax.optimization_barrier((lhs, a, b))
        a, b = ring.right(a), ring.left(b)
        terms = terms_of(info, [d, n - d] if d > 0 else [0], lhs, weight, depth)
        terms, a, b = lax.optimization_barrier((terms, a, b))
        if d > 0:
            kind = "second" if d == half - 1 else "later"
            a, b = join(kind, rows, depth, energy, terms, [a, b])
    return terms, ([a, b] if half > 1 else [jnp.concatenate([a, b], axis=0)])


def mixer_kernel(arrived, tenants, inner_size, info, adapter, term_ref, *refs):
    got = refs[:arrived]
    e_ref, tok_ref, gain_ref = refs[arrived : arrived + 3]
    downs = refs[arrived + 3 : arrived + 3 + tenants]
    first_ref, message_ref = refs[-2:]
    rows, depth = term_ref.shape
    length = rows // tenants
    tail = slice(depth, depth + 128)
    energy = e_ref[...]
    total = term_ref[...]
    for g in got:
        energy = energy + energy_of(g[:, tail])
        total = total + g[:, :depth].astype(f32)
    scale = lax.rsqrt(energy / inner_size + epsilon)
    first = (tok_ref[...].astype(f32) + total * scale).astype(bf16)
    wide = first.astype(f32)
    high, low = split(jnp.sum(wide * wide, axis=1, keepdims=True))
    first_ref[...] = first
    attn = (wide * gain_ref[...]).astype(bf16)
    message_ref[:, :depth] = attn
    rank = downs[0].shape[1]
    parts = []
    for i in range(tenants):
        x = attn[i * length : (i + 1) * length]
        parts.append(
            lax.dot_general(x, downs[i][0], (((1,), (1,)), ((), ())), preferred_element_type=f32)
        )
    small = jnp.concatenate(parts, axis=0).astype(bf16)
    message_ref[:, tail] = lanes_of([(rank, high), (rank + 1, low)], rows)
    message_ref[:, depth : depth + rank] = small


def mixer_step(info, adapter, terms, got, energy, own_tokens, gain, down, inner_size):
    rows, depth = terms.shape
    tenants = adapter.shape[0]
    operands = [terms, *got, energy, own_tokens, gain] + [down] * tenants

    def whole(a):
        return pl.BlockSpec(a.shape, lambda j, *s: (0,) * a.ndim)

    in_specs = [whole(a) for a in operands]
    in_specs[3 + len(got)] = pl.BlockSpec(
        (1, depth), lambda j, info, adapter: (0, info[info.shape[0] - 2])
    )
    for i in range(tenants):
        in_specs[4 + len(got) + i] = pl.BlockSpec(
            (1, *down.shape[1:]), functools.partial(lambda i, j, info, adapter: (adapter[i], 0, 0), i)
        )
    shapes = [jax.ShapeDtypeStruct((rows, depth), bf16), jax.ShapeDtypeStruct((rows, depth + 128), bf16)]
    return pl.pallas_call(
        functools.partial(mixer_kernel, len(got), tenants, inner_size),
        grid_spec=pltpu.PrefetchScalarGridSpec(
            num_scalar_prefetch=2,
            grid=(1,),
            in_specs=in_specs,
            out_specs=[whole(s) for s in shapes],
        ),
        out_shape=shapes,
        compiler_params=pltpu.CompilerParams(vmem_limit_bytes=16 << 20),
        cost_estimate=pl.CostEstimate(
            flops=2 * rows * depth * 64, bytes_accessed=rows * depth * 16, transcendentals=0
        ),
        name="mixer_step",
    )(info, adapter, *operands)


def query_kernel(offsets, count, first_call, info, *refs):
    blocks = refs[:count]
    w_ref = refs[count]
    q_ref, l_ref = refs[-2:]
    j, k = pl.program_id(0), pl.program_id(1)
    kb = w_ref.shape[0]
    steps = pl.num_programs(1)
    depth = blocks[0].shape[1] - 128

    @pl.when((j == 0) & (k == 0))
    def _():
        if first_call:
            q_ref[...] = jnp.zeros_like(q_ref)
            l_ref[...] = jnp.zeros_like(l_ref)
        else:
            q_ref[...] = refs[count + 1][...]
            l_ref[...] = refs[count + 2][...]

    for b in range(len(offsets)):
        for kk in range(depth // kb):

            @pl.when((j == b) & (k == kk))
            def _():
                pieces = [blocks[b]] if count == len(offsets) else blocks
                base = 0
                for block in pieces:
                    at = slice(base, base + block.shape[0])
                    q_ref[at] += jnp.dot(
                        block[:, kk * kb : (kk + 1) * kb], w_ref[...], preferred_element_type=f32
                    )
                    if kk == 0:
                        l_ref[at] += block[:, depth:].astype(f32)
                    base += block.shape[0]


def query_step(info, offsets, blocks, weight, depth, accs):
    count = len(blocks)
    rows = sum(b.shape[0] for b in blocks) // len(offsets)
    cols = weight.shape[1]
    kb = tile_of(depth)
    steps = depth // kb

    def row_block(j, k, info):
        at = info[offsets[0]]
        for b in range(1, len(offsets)):
            at = jnp.where(j == b, info[offsets[b]], at)
        return (at * steps + k, 0)

    shapes = [(rows, cols), (rows, 128)]
    in_specs = [fixed_block(b.shape) for b in blocks] + [pl.BlockSpec((kb, cols), row_block)]
    operands = [info, *blocks, weight]
    aliases = {}
    if accs is not None:
        in_specs += [fixed_block(s) for s in shapes]
        aliases = {len(operands): 0, len(operands) + 1: 1}
        operands += accs
    return pl.pallas_call(
        functools.partial(query_kernel, offsets, count, accs is None),
        grid_spec=pltpu.PrefetchScalarGridSpec(
            num_scalar_prefetch=1,
            grid=(len(offsets), steps),
            in_specs=in_specs,
            out_specs=[fixed_block(s) for s in shapes],
        ),
        out_shape=[jax.ShapeDtypeStruct(s, f32) for s in shapes],
        input_output_aliases=aliases,
        compiler_params=pltpu.CompilerParams(vmem_limit_bytes=16 << 20),
        cost_estimate=pl.CostEstimate(
            flops=len(offsets) * 2 * rows * depth * cols,
            bytes_accessed=len(offsets) * depth * cols * 2,
            transcendentals=0,
        ),
        name="query_step",
    )(*operands)


def shifted(history, x, k):
    if k == 3:
        return x
    return jnp.concatenate([history[k:3], x[: x.shape[0] - 3 + k]], axis=0)


def conv_silu(history, x, taps):
    total = taps[0:1] * shifted(history, x, 0)
    for k in range(1, 4):
        total = total + taps[k : k + 1] * shifted(history, x, k)
    return total * jax.nn.sigmoid(total)


def spans(heads, width):
    lane = lax.broadcasted_iota(jnp.int32, (heads, heads * width), 1)
    row = lax.broadcasted_iota(jnp.int32, (heads, heads * width), 0)
    return jnp.where(lane // width == row, 1.0, 0.0).astype(f32)


def state_kernel(
    slot,
    info,
    x_ref,
    z_ref,
    kept_ref,
    came_ref,
    hx_ref,
    hbc_ref,
    tx_ref,
    tbc_ref,
    bias_ref,
    rate_ref,
    skip_ref,
    gain_ref,
    own_ref,
    far_ref,
    gated_ref,
    energy_ref,
    final_ref,
    initial,
    *,
    slots,
):
    i = pl.program_id(0)
    count = info.shape[0]
    is_own = slot[i] // slots == info[count - 1]

    @pl.when(is_own)
    def _():
        initial[...] = own_ref[0]

    @pl.when(jnp.logical_not(is_own))
    def _():
        initial[...] = far_ref[0]

    length = x_ref.shape[0]
    heads = bias_ref.shape[1]
    values = conv_silu(hx_ref[0], x_ref[...].astype(bf16).astype(f32), tx_ref[...])
    shared = i // (pl.num_programs(0) // 2) == lax.rem(info[count - 2], 2)
    projected = jnp.where(shared, kept_ref[...], came_ref[...].astype(f32))
    bc = conv_silu(hbc_ref[0], projected[:, : 2 * STATE], tbc_ref[...])
    all_raw = projected[:, 2 * STATE :]
    pick = (all_raw.shape[1], heads)
    chosen = lax.broadcasted_iota(jnp.int32, pick, 0) == (
        lax.broadcasted_iota(jnp.int32, pick, 1) + info[count - 2] * heads
    )
    chosen = jnp.where(chosen, 1.0, 0.0).astype(f32)
    in_state = bc[:, :STATE].astype(bf16)
    out_state = bc[:, STATE:].astype(bf16)
    raw = jnp.dot(all_raw, chosen, precision=highest, preferred_element_type=f32) + bias_ref[...]
    steps = jnp.maximum(raw, 0.0) + jnp.log1p(jnp.exp(-jnp.abs(raw)))
    log_decay = -steps * jnp.exp(rate_ref[...])
    row = lax.broadcasted_iota(jnp.int32, (length, length), 0)
    col = lax.broadcasted_iota(jnp.int32, (length, length), 1)
    lower = jnp.where(row >= col, 1.0, 0.0).astype(f32)
    running = jnp.dot(lower, log_decay, precision=highest, preferred_element_type=f32)
    last = running[length - 1 : length]

    wide = spans(heads, length)
    both = jnp.dot(
        jnp.concatenate([running, steps], axis=0), wide, precision=highest, preferred_element_type=f32
    )
    run_t, step_t = both[:length], both[length:]
    lane = lax.broadcasted_iota(jnp.int32, (length, heads * length), 1) % length
    place = lax.broadcasted_iota(jnp.int32, (length, heads * length), 0)
    diagonal = lane == place
    run_s = jnp.sum(jnp.where(diagonal, run_t, 0.0), axis=0, keepdims=True)
    step_s = jnp.sum(jnp.where(diagonal, step_t, 0.0), axis=0, keepdims=True)
    seen = place >= lane
    decays = jnp.where(seen, jnp.exp(jnp.where(seen, run_t - run_s, 0.0)), 0.0)
    overlap = lax.dot_general(
        out_state,
        jnp.concatenate([in_state] * heads, axis=0),
        (((1,), (1,)), ((), ())),
        preferred_element_type=f32,
    )
    mixing = (overlap * decays * step_s).astype(bf16)
    short = values.astype(bf16)
    group = min(4, heads)
    gl, gw = group * length, group * HDIM
    own_block = (
        lax.broadcasted_iota(jnp.int32, (gl, gw), 0) // length
        == lax.broadcasted_iota(jnp.int32, (gl, gw), 1) // HDIM
    )
    within = []
    for g in range(heads // group):
        v = jnp.concatenate([values[:, g * gw : (g + 1) * gw]] * group, axis=0)
        v = jnp.where(own_block, v, 0.0).astype(bf16)
        within.append(jnp.dot(mixing[:, g * gl : (g + 1) * gl], v, preferred_element_type=f32))
    within = within[0] if len(within) == 1 else jnp.concatenate(within, axis=1)

    narrow = spans(heads, HDIM)
    scales = jnp.dot(
        jnp.concatenate(
            [
                jnp.exp(running),
                jnp.exp(last - running) * steps,
                jnp.broadcast_to(skip_ref[...], (8, heads)),
            ],
            axis=0,
        ),
        narrow,
        precision=highest,
        preferred_element_type=f32,
    )
    start = initial[...]
    carried = lax.dot_general(
        out_state, start.astype(bf16), (((1,), (1,)), ((), ())), preferred_element_type=f32
    )
    result = within + carried * scales[:length] + scales[2 * length : 2 * length + 1] * values
    z = z_ref[...].astype(bf16).astype(f32)
    gated = result * (z * jax.nn.sigmoid(z))
    energy_ref[...] = jnp.sum(gated * gated, axis=1, keepdims=True)
    gated_ref[...] = (gated * gain_ref[...]).astype(bf16)

    kept = jnp.exp(
        lax.dot_general(
            log_decay,
            jnp.ones((length, STATE), f32),
            (((0,), (0,)), ((), ())),
            precision=highest,
            preferred_element_type=f32,
        )
    )
    update = lax.dot_general(
        (values * scales[length : 2 * length]).astype(bf16),
        in_state,
        (((0,), (0,)), ((), ())),
        preferred_element_type=f32,
    )
    for h in range(heads):
        at = slice(h * HDIM, (h + 1) * HDIM)
        final_ref[0, at, :] = update[at] + start[at] * kept[h : h + 1]


def state_pass(
    info, slot, inner, kept, came, hx, hbc, tx, tbc, bias, rate, skip, gain, own_pool, far_pool
):
    tenants = slot.shape[0]
    length = inner.shape[0] // 2 // tenants
    cols = inner.shape[1]
    slots = own_pool.shape[0]

    def rows(width):
        return pl.BlockSpec((length, width), lambda i, *s: (i, 0))

    def whole(a):
        return pl.BlockSpec(a.shape, lambda i, *s: (0,) * a.ndim)

    def own_slot(i, slot, info):
        return (jnp.clip(slot[i] - info[info.shape[0] - 1] * slots, 0, slots - 1), 0, 0)

    def far_slot(i, slot, info):
        return (jnp.clip(slot[i] - (1 - info[info.shape[0] - 1]) * slots, 0, slots - 1), 0, 0)

    pooled = (1, cols, STATE)
    return pl.pallas_call(
        functools.partial(state_kernel, slots=slots),
        grid_spec=pltpu.PrefetchScalarGridSpec(
            num_scalar_prefetch=2,
            grid=(tenants,),
            in_specs=[
                rows(cols),
                pl.BlockSpec((length, cols), lambda i, *s: (tenants + i, 0)),
                pl.BlockSpec((length, kept.shape[1]), lambda i, *s: (i % (tenants // 2), 0)),
                pl.BlockSpec((length, kept.shape[1]), lambda i, *s: (i % (tenants // 2), 0)),
                pl.BlockSpec((1, 3, cols), lambda i, *s: (i, 0, 0)),
                pl.BlockSpec((1, 3, 2 * STATE), lambda i, *s: (i, 0, 0)),
                whole(tx),
                whole(tbc),
                whole(bias),
                whole(rate),
                whole(skip),
                whole(gain),
                pl.BlockSpec(pooled, own_slot),
                pl.BlockSpec(pooled, far_slot),
            ],
            out_specs=[
                rows(cols),
                rows(1),
                pl.BlockSpec(pooled, lambda i, *s: (i, 0, 0)),
            ],
            scratch_shapes=[pltpu.VMEM((cols, STATE), f32)],
        ),
        out_shape=[
            jax.ShapeDtypeStruct((tenants * length, cols), bf16),
            jax.ShapeDtypeStruct((tenants * length, 1), f32),
            jax.ShapeDtypeStruct((tenants, cols, STATE), f32),
        ],
        compiler_params=pltpu.CompilerParams(vmem_limit_bytes=28 << 20),
        cost_estimate=pl.CostEstimate(
            flops=tenants * 6 * length * cols * STATE,
            bytes_accessed=tenants * cols * STATE * 10,
            transcendentals=0,
        ),
        name="state_pass",
    )(slot, info, inner, inner, kept, came, hx, hbc, tx, tbc, bias, rate, skip, gain, own_pool, far_pool)


def attend_kernel(
    width, table, limit, adapter, info, q_ref, low_ref, up_ref, near_ref, far_ref, *refs
):
    o_ref = refs[-1]
    i = pl.program_id(0)
    length = q_ref.shape[0]
    heads = q_ref.shape[1] // HEAD_SIZE
    blocks = table.shape[1]
    part = near_ref.shape[1]
    core = info[info.shape[0] - 1]
    rank = up_ref.shape[1]
    square = low_ref[:, rank : rank + 1] + low_ref[:, rank + 1 : rank + 2]
    norm = lax.rsqrt(square / width + epsilon)
    low = (low_ref[:, :rank] * norm).astype(bf16)
    raised = jnp.dot(low, up_ref[0], preferred_element_type=f32)
    q = (q_ref[...] * norm + adapter_scale * raised).astype(bf16)
    q = jnp.concatenate([q[:, h * HEAD_SIZE : (h + 1) * HEAD_SIZE] for h in range(heads)], axis=0)
    fresh = jnp.concatenate([refs[0][...], refs[1][...]], axis=1)
    for came in refs[2:-1]:
        fresh = fresh + came[...].astype(f32)
    fresh = (fresh * norm).astype(bf16)
    pieces = []
    for j in range(blocks):
        at = table[i, j]
        pieces += [near_ref[at], far_ref[at]]
    cached = jnp.concatenate(pieces, axis=0)
    context = cached.shape[0]
    nt = (((1,), (1,)), ((), ()))
    scale = HEAD_SIZE ** (-0.5)
    old = lax.dot_general(q, cached[:, :HEAD_SIZE], nt, preferred_element_type=f32) * scale
    new = lax.dot_general(q, fresh[:, :HEAD_SIZE], nt, preferred_element_type=f32) * scale
    lane = lax.broadcasted_iota(jnp.int32, old.shape, 1)
    inside = lane % (2 * part)
    far_side = jnp.where(inside >= part, 1, 0)
    half = jnp.where(core == 0, far_side, 1 - far_side)
    place = (lane // (2 * part)) * (2 * part) + half * part + inside % part
    old_seen = place < limit[i]
    token = lax.broadcasted_iota(jnp.int32, new.shape, 0) % length
    new_seen = lax.broadcasted_iota(jnp.int32, new.shape, 1) <= token
    old = jnp.where(old_seen, old, -jnp.inf)
    new = jnp.where(new_seen, new, -jnp.inf)
    top = jnp.maximum(jnp.max(old, axis=1, keepdims=True), jnp.max(new, axis=1, keepdims=True))
    old = jnp.where(old_seen, jnp.exp(old - top), 0.0)
    new = jnp.where(new_seen, jnp.exp(new - top), 0.0)
    share = 1.0 / (jnp.sum(old, axis=1, keepdims=True) + jnp.sum(new, axis=1, keepdims=True))
    out = jnp.dot((old * share).astype(bf16), cached[:, HEAD_SIZE:], preferred_element_type=f32)
    out += jnp.dot((new * share).astype(bf16), fresh[:, HEAD_SIZE:], preferred_element_type=f32)
    out = out.astype(bf16)
    for h in range(heads):
        o_ref[:, h * HEAD_SIZE : (h + 1) * HEAD_SIZE] = out[h * length : (h + 1) * length]


def attend(ring, width, table, limit, adapter, info, q, low, up, near, far, kv, kv_came):
    tenants = table.shape[0]
    length = q.shape[0] // tenants

    def rows(a):
        return pl.BlockSpec((length, a.shape[1]), lambda i, *s: (i, 0))

    def whole(a):
        return pl.BlockSpec(a.shape, lambda i, *s: (0,) * a.ndim)

    def own(base):
        return pl.BlockSpec(
            (length, HEAD_SIZE), lambda i, t, n, a, info: (i, base + info[ring.n])
        )

    return pl.pallas_call(
        functools.partial(attend_kernel, width),
        grid_spec=pltpu.PrefetchScalarGridSpec(
            num_scalar_prefetch=4,
            grid=(tenants,),
            in_specs=[
                rows(q),
                rows(low),
                pl.BlockSpec((1, *up.shape[1:]), lambda i, t, n, a, info: (a[i], 0, 0)),
                whole(near),
                whole(far),
                own(0),
                own(KEY_HEADS),
            ]
            + [rows(a) for a in kv_came],
            out_specs=rows(q),
        ),
        out_shape=jax.ShapeDtypeStruct(q.shape, bf16),
        compiler_params=pltpu.CompilerParams(vmem_limit_bytes=24 << 20),
        cost_estimate=pl.CostEstimate(
            flops=tenants * 4 * length * q.shape[1] * 288,
            bytes_accessed=near.size * 4 + q.size * 6 + up.size,
            transcendentals=0,
        ),
        name="attend",
    )(table, limit, adapter, info, q, low, up, near, far, kv, kv, *kv_came)


def pick_kernel(info, key_ref, value_ref, o_ref):
    o_ref[0, :, :, :HEAD_SIZE] = key_ref[...]
    o_ref[0, :, :, HEAD_SIZE:] = value_ref[...]


def pick_heads(info, pool, devices, pools):
    count, block_len, _ = pool.shape
    part = block_len // pools
    each = QUERY_HEADS // devices
    group = QUERY_HEADS // KEY_HEADS

    def lanes(base):
        return pl.BlockSpec(
            (count, part, HEAD_SIZE),
            lambda d, info: (0, info[info.shape[0] - 1], base + lax.div(d * each, group)),
        )

    shape = (devices, count, part, 2 * HEAD_SIZE)
    return pl.pallas_call(
        pick_kernel,
        grid_spec=pltpu.PrefetchScalarGridSpec(
            num_scalar_prefetch=1,
            grid=(devices,),
            in_specs=[lanes(0), lanes(KEY_HEADS)],
            out_specs=pl.BlockSpec((1, *shape[1:]), lambda d, info: (d, 0, 0, 0)),
        ),
        out_shape=jax.ShapeDtypeStruct(shape, bf16),
        compiler_params=pltpu.CompilerParams(vmem_limit_bytes=8 << 20),
        name="pick_heads",
    )(info, pool, pool)


def fresh_kernel(kind, offsets, heads_at, info, kv_ref, *refs):
    outs = refs[-2:]
    got = refs[:-2]
    rows = kv_ref.shape[0]
    h = rows // 2
    sides = [slice(0, h), slice(h, rows)]
    for j in range(2):
        offset = offsets[0] if kind == "first" else offsets[j]
        head = info[heads_at + offset]
        for k in range(2):
            at = pl.ds(pl.multiple_of((head + k * KEY_HEADS) * HEAD_SIZE, HEAD_SIZE), HEAD_SIZE)
            to = slice(k * HEAD_SIZE, (k + 1) * HEAD_SIZE)
            if kind == "first":
                outs[j][:, to] = kv_ref[sides[j], at].astype(bf16)
            elif kind == "second":
                mine, other = sides[j], sides[1 - j]
                outs[j][mine, to] = (kv_ref[mine, at] + got[j][:, to].astype(f32)).astype(bf16)
                outs[j][other, to] = kv_ref[other, at].astype(bf16)
            else:
                outs[j][:, to] = (kv_ref[:, at] + got[j][:, to].astype(f32)).astype(bf16)


def fresh_join(info, kind, offsets, heads_at, kv, got):
    rows = kv.shape[0]
    shape = (rows // 2 if kind == "first" else rows, 2 * HEAD_SIZE)
    operands = [kv, *got]
    return pl.pallas_call(
        functools.partial(fresh_kernel, kind, offsets, heads_at),
        grid_spec=pltpu.PrefetchScalarGridSpec(
            num_scalar_prefetch=1,
            grid=(1,),
            in_specs=[pl.BlockSpec(a.shape, lambda j, info: (0, 0)) for a in operands],
            out_specs=[pl.BlockSpec(shape, lambda j, info: (0, 0))] * 2,
        ),
        out_shape=[jax.ShapeDtypeStruct(shape, bf16)] * 2,
        compiler_params=pltpu.CompilerParams(vmem_limit_bytes=8 << 20),
        name="fresh_join",
    )(info, *operands)


def per_device(
    ring,
    tokens,
    mamba_in_weight,
    state_projection,
    inner_taps,
    state_taps,
    inner_history,
    state_history,
    step_size_bias,
    log_decay_rate,
    skip_factor,
    gated_norm_gain,
    mamba_out_weight,
    saved_state_pool,
    tenant_state_slot,
    attention_gain,
    query_matrix,
    adapter_down,
    adapter_up,
    tenant_adapter,
    key_value_weight,
    key_value_pool,
    tenant_blocks,
    cached_length,
    attention_out_weight,
):
    n, half, pools = ring.n, ring.half, ring.pools
    tenants, length, depth = tokens.shape
    rows = tenants * length
    width = depth * n
    info = ring.info()
    own_tokens = tokens.reshape(rows, depth)
    heads = step_size_bias.shape[0]
    cols = mamba_in_weight.shape[2]
    swap = [(i, (i + 1) % pools) for i in range(pools)]

    slots = saved_state_pool.shape[0]
    flat_pool = saved_state_pool.reshape(slots, heads * HDIM, STATE)
    far_pool = lax.ppermute(flat_pool, "pool", swap)

    keep, give = partial_product(info, own_tokens, state_projection)
    inner, kept, came = ring.gather(
        own_tokens,
        lambda offsets, blocks, acc: in_product(info, offsets, blocks, mamba_in_weight, depth, acc),
        keep,
        give,
    )

    mine = pick_heads(info, key_value_pool, n, pools)
    mine, inner = lax.optimization_barrier((mine, inner))
    cache = lax.all_to_all(mine, "tensor", 0, 0, tiled=True)
    cache = cache.reshape(-1, *cache.shape[2:])
    far_cache = lax.ppermute(cache, "pool", swap)

    gated, energy, final_state = state_pass(
        info,
        tenant_state_slot,
        inner,
        kept,
        came,
        inner_history.astype(f32),
        state_history,
        inner_taps.astype(f32),
        state_taps.astype(f32),
        step_size_bias[None],
        log_decay_rate[None],
        skip_factor[None],
        gated_norm_gain[None],
        flat_pool,
        far_pool,
    )
    terms, got = ring_sum(ring, info, gated, mamba_out_weight, depth, energy)
    first, message = mixer_step(
        info,
        tenant_adapter,
        terms,
        got,
        energy,
        own_tokens,
        attention_gain[None],
        adapter_down.transpose(0, 2, 1),
        cols * n,
    )

    kv = jnp.dot(message[:, :depth], key_value_weight, preferred_element_type=f32)

    h = rows // 2
    a, b = message, message
    ka, kb = fresh_join(info, "first", [half], n, kv, [])
    accs, ready = None, ([0], [message])
    for s in range(1, half + 1):
        if s == half:
            a, b = a[:h], b[h:]
        a, b, ka, kb = ring.right(a), ring.left(b), ring.right(ka), ring.left(kb)
        accs = query_step(info, *ready, query_matrix, depth, accs)
        a, b, ka, kb, accs = lax.optimization_barrier((a, b, ka, kb, accs))
        ready = ([n - s, s], [a, b]) if s < half else ([half], [a, b])
        if s < half:
            kind = "second" if s == 1 else "later"
            ka, kb = fresh_join(info, kind, [half - s, n - half + s], n, kv, [ka, kb])
    kv_came = [ka, kb] if half > 1 else [jnp.concatenate([ka, kb], axis=0)]
    query, low = query_step(info, *ready, query_matrix, depth, accs)
    heads_out = attend(
        ring,
        width,
        tenant_blocks,
        cached_length,
        tenant_adapter,
        info,
        query,
        low,
        adapter_up,
        cache,
        far_cache,
        kv,
        kv_came,
    )
    terms, got = ring_sum(ring, info, heads_out, attention_out_weight, depth)
    second = terms + first.astype(f32)
    for g in got:
        second = second + g.astype(f32)
    second = second.astype(bf16)
    return (
        second.reshape(tenants, length, depth),
        final_state.reshape(tenants, heads, HDIM, STATE),
    )


def solution(mesh):
    in_specs = (
        P(("groups", "pool"), None, "tensor"),
        P(None, None, "tensor"),
        P("tensor", None),
        P(None, "tensor"),
        P(),
        P(("groups", "pool"), None, "tensor"),
        P(("groups", "pool"), None, None),
        P("tensor"),
        P("tensor"),
        P("tensor"),
        P("tensor"),
        P("tensor", None),
        P(("groups", "pool"), "tensor", None, None),
        P(("groups", "pool")),
        P(),
        P(None, "tensor"),
        P(None, "tensor", None),
        P(None, None, "tensor"),
        P(("groups", "pool")),
        P("tensor", None),
        P(("groups", "tensor"), None, None),
        P(("groups", "pool"), None),
        P(("groups", "pool")),
        P("tensor", None),
    )
    out_specs = (P(("groups", "pool"), None, "tensor"), P(("groups", "pool"), "tensor", None, None))
    ring = Ring(mesh.shape["tensor"], mesh.shape["pool"])
    return jax.shard_map(
        functools.partial(per_device, ring),
        mesh=mesh,
        in_specs=in_specs,
        out_specs=out_specs,
        check_vma=False,
    )
```

time: 269 us -> 194 us (0.72)
  Pallas kernels: 124 us -> 84 us
  waiting for transfers between devices: 56.5 us -> 39 us
  between operations: 13.1 us -> 1.4 us
  other arithmetic: 6.22 us -> 0.97 us
    ppermute x20, waiting for transfers between devices: 49 us -> 21.1 us  [right(): return lax.ppermute(x, 'tensor', self.cw)]
    pallas_call x16 -> x31, Pallas kernels: 90.5 us -> 68.1 us  [the longest x10 30.2 us: terms_of(): pl.pallas_call(term_kernel, grid_spec=pltpu.PrefetchScalarGridSpec(num_sc...]
    pallas_call x5, Pallas kernels: 23.6 us -> 6.96 us  [query_step(): pl.pallas_call(functools.partial(query_kernel, offsets, count, accs is No...]
    ppermute x8 -> x5, waiting for transfers between devices: 0.02 us -> 5.2 us  [the longest x4 5.2 us: gather(): came = lax.ppermute(give, 'tensor', exchange[s - 1])]
    ppermute x20, waiting for transfers between devices: 7.52 us -> 12.7 us  [left(): return lax.ppermute(x, 'tensor', self.ccw)]
    ppermute x8 -> x5, starting transfers between devices: 12 us -> 6.89 us  [the longest x4 6.37 us: gather(): came = lax.ppermute(give, 'tensor', exchange[s - 1])]
    ppermute x20, starting transfers between devices: 25.4 us -> 30.2 us  [right(): return lax.ppermute(x, 'tensor', self.cw)]
    convert_element_type x5 -> x4, other arithmetic: 4.92 us -> 0.96 us  [the longest x1 0.85 us: per_device(): second = second.astype(bf16)]
  transfers between devices with their start and end apart: 49 -> 47, of which waited for: 18 -> 21; matrix products, arithmetic and copies ran while one was open for 3% -> 1% of each run, Pallas kernels for 28% -> 33%
where the time goes in v3:
time: 194 us
  Pallas kernels  84 us (43%)
  starting transfers between devices  56.6 us (29%)
  waiting for transfers between devices  39 us (20%)
  local copies, waits for them, and re-layouts  11 us (6%)
    pallas_call x10, Pallas kernels, terms_of(): pl.pallas_call(term_kernel, grid_spec=pltpu.PrefetchScalarGridSpec(num_sc...  30.2 us
    ppermute x20, starting transfers between devices, right(): return lax.ppermute(x, 'tensor', self.cw)  30.2 us
    pallas_call x5, Pallas kernels, in_product(): pl.pallas_call(functools.partial(in_kernel, offsets, count, chunks, acc i...  24.3 us
    ppermute x20, waiting for transfers between devices, right(): return lax.ppermute(x, 'tensor', self.cw)  21.1 us
    ppermute x20, starting transfers between devices, left(): return lax.ppermute(x, 'tensor', self.ccw)  16 us
    ppermute x20, waiting for transfers between devices, left(): return lax.ppermute(x, 'tensor', self.ccw)  12.7 us
    unnamed x59, local copies, waits for them, and re-layouts  10.2 us
    pallas_call x1, Pallas kernels, state_pass(): pl.pallas_call(functools.partial(state_kernel, slots=slots), grid_spec=pl...  8.97 us
  transfers between devices with their start and end apart: 47, of which 21 were waited for; matrix products, arithmetic and copies ran while one was open for 1% of the time, Pallas kernels for 33%

profile of v3, /device:TPU:0, one launch (start us, length us, event | category | flops | bytes accessed | tf_op | source)
XLA Modules:
  0.0 193.6 jit_solution(10057610095016598014)
XLA Ops:
  11.0 3.3 %pick_heads.1 = bf16[8,8,16,256]{3,2,1,0:T(8,128)(2,1)} custom-call(s32[18]{0:T(128)S(1)} %dynamic-slice_bitcast_fusion.info, bf16[8,32,2048]{2,1,0:T(8,128)(2,1)S(1)} %copy-done.2, bf16[8,32,2048]{2,1,0:T(8,128)(2,1)S(1)} %copy-done.2), custom_call_target="tpu_custom_call" | custom-call | tf_op jit(solution)/shard_map/pick_heads/pallas_call | solution.py:824
  14.4 3.8 %in_product.5.refs_3_ = f32[256,1024]{1,0:T(8,128)S(1)} custom-call(s32[18]{0:T(128)S(1)} %dynamic-slice_bitcast_fusion.info, bf16[128,1024]{1,0:T(8,128)(2,1)S(1)} %bitcast.27, bf16[8192,2,1024]{2,1,0:T(2,128)(2,1)} %refs_2_.11), custom_call_target="tpu_custom_call" | custom-call | flops 1073741824 | bytes 8388608 | tf_op jit(solution)/shard_map/in_product/pallas_call | solution.py:198
  22.0 5.5 %in_product.6.refs_3_ = f32[256,1024]{1,0:T(8,128)S(1)} custom-call(s32[18]{0:T(128)S(1)} %dynamic-slice_bitcast_fusion.info, bf16[128,1024]{1,0:T(8,128)(2,1)S(1)} %collective-permute-done.refs_0_, bf16[128,1024]{1,0:T(8,128)(2,1)S(1)} %collective-permute-done.1.refs_1_, bf16[8192,2,1024]{2,1,0:T(2,128)(2,1)} %refs_2_.11, ...), custom_call_target="tpu_custom_call", output_to_operand_aliasing={{}: (4, {})} | custom-call | flops 2147483648 | bytes 16777216 | tf_op jit(solution)/shard_map/in_product/pallas_call | solution.py:198
  33.9 5.6 %in_product.7.refs_3_ = f32[256,1024]{1,0:T(8,128)S(1)} custom-call(s32[18]{0:T(128)S(1)} %dynamic-slice_bitcast_fusion.info, bf16[128,1024]{1,0:T(8,128)(2,1)S(1)} %collective-permute-done.3.refs_0_, bf16[128,1024]{1,0:T(8,128)(2,1)S(1)} %collective-permute-done.4.refs_1_, bf16[8192,2,1024]{2,1,0:T(2,128)(2,1)} %refs_2_.11, ...), custom_call_target="tpu_custom_call", output_to_operand_aliasing={{}: (4, {})} | custom-call | flops 2147483648 | bytes 16777216 | tf_op jit(solution)/shard_map/in_product/pallas_call | solution.py:198
  39.5 3.5 %collective-permute-done.8 = bf16[64,640]{1,0:T(8,128)(2,1)S(1)} collective-permute-done((bf16[64,640]{1,0:T(8,128)(2,1)S(1)}, bf16[64,640]{1,0:T(8,128)(2,1)S(1)}, u32[]{:S(2)}, u32[]{:S(2)}) %collective-permute-start.8) | collective-permute-done | bytes 81952 | tf_op jit(solution)/shard_map/ppermute | solution.py:86
  45.5 5.5 %in_product.8.refs_3_ = f32[256,1024]{1,0:T(8,128)S(1)} custom-call(s32[18]{0:T(128)S(1)} %dynamic-slice_bitcast_fusion.info, bf16[128,1024]{1,0:T(8,128)(2,1)S(1)} %collective-permute-done.6.refs_0_, bf16[128,1024]{1,0:T(8,128)(2,1)S(1)} %collective-permute-done.7.refs_1_, bf16[8192,2,1024]{2,1,0:T(2,128)(2,1)} %refs_2_.11, ...), custom_call_target="tpu_custom_call", output_to_operand_aliasing={{}: (4, {})} | custom-call | flops 2147483648 | bytes 16777216 | tf_op jit(solution)/shard_map/in_product/pallas_call | solution.py:198
  51.0 3.9 %in_product.9.x_ref.z_ref = f32[256,1024]{1,0:T(8,128)S(1)} custom-call(s32[18]{0:T(128)S(1)} %dynamic-slice_bitcast_fusion.info, bf16[64,1024]{1,0:T(8,128)(2,1)S(1)} %collective-permute-done.9.refs_0_, bf16[64,1024]{1,0:T(8,128)(2,1)S(1)} %collective-permute-done.10.refs_1_, bf16[8192,2,1024]{2,1,0:T(2,128)(2,1)} %refs_2_.11, ...), custom_call_target="tpu_custom_call", output_to_operand_aliasing={{}: (4, {})} | custom-call | flops 1073741824 | bytes 8388608 | tf_op jit(solution)/shard_map/in_product/pallas_call | solution.py:198
  55.1 9.0 %state_pass.1 = (bf16[128,1024]{1,0:T(8,128)(2,1)S(1)}, f32[128,1]{1,0:T(8,128)S(1)}, f32[4,1024,256]{2,1,0:T(8,128)}) custom-call(s32[4]{0:T(128)S(1)} %copy-done.13, s32[18]{0:T(128)S(1)} %dynamic-slice_bitcast_fusion.info, f32[256,1024]{1,0:T(8,128)S(1)} %in_product.9.x_ref.z_ref, f32[256,1024]{1,0:T(8,128)S(1)} %in_product.9.x_ref.z_ref, ...), custom_call_target="tpu_custom_call" | custom-call | flops 201326592 | bytes 10485760 | tf_op jit(solution)/shard_map/state_pass/pallas_call | solution.py:668
  68.9 3.3 %terms.11.refs_1_ = f32[256,1024]{1,0:T(8,128)S(1)} custom-call(s32[18]{0:T(128)S(1)} %dynamic-slice_bitcast_fusion.info, bf16[128,1024]{1,0:T(8,128)(2,1)S(1)} %get-tuple-element.180.lhs_ref, bf16[1024,8192]{1,0:T(8,128)(2,1)} %w_ref.16), custom_call_target="tpu_custom_call" | custom-call | flops 536870912 | bytes 4194304 | tf_op jit(solution)/shard_map/terms/pallas_call | solution.py:294
  75.6 3.3 %terms.12.refs_1_ = f32[256,1024]{1,0:T(8,128)S(1)} custom-call(s32[18]{0:T(128)S(1)} %dynamic-slice_bitcast_fusion.info, bf16[128,1024]{1,0:T(8,128)(2,1)S(1)} %get-tuple-element.180.lhs_ref, bf16[1024,8192]{1,0:T(8,128)(2,1)} %w_ref.16), custom_call_target="tpu_custom_call" | custom-call | flops 536870912 | bytes 4194304 | tf_op jit(solution)/shard_map/terms/pallas_call | solution.py:294
  78.9 3.5 %collective-permute-done.15.refs_2_ = bf16[128,1152]{1,0:T(8,128)(2,1)S(1)} collective-permute-done((bf16[128,1152]{1,0:T(8,128)(2,1)S(1)}, bf16[128,1152]{1,0:T(8,128)(2,1)S(1)}, u32[]{:S(2)}, u32[]{:S(2)}) %collective-permute-start.15) | collective-permute-done | bytes 294944 | tf_op jit(solution)/shard_map/ppermute | solution.py:61
  85.7 3.3 %terms.13.refs_1_ = f32[256,1024]{1,0:T(8,128)S(1)} custom-call(s32[18]{0:T(128)S(1)} %dynamic-slice_bitcast_fusion.info, bf16[128,1024]{1,0:T(8,128)(2,1)S(1)} %get-tuple-element.180.lhs_ref, bf16[1024,8192]{1,0:T(8,128)(2,1)} %w_ref.16), custom_call_target="tpu_custom_call" | custom-call | flops 536870912 | bytes 4194304 | tf_op jit(solution)/shard_map/terms/pallas_call | solution.py:294
  89.0 4.0 %collective-permute-done.17.refs_2_ = bf16[128,1152]{1,0:T(8,128)(2,1)S(1)} collective-permute-done((bf16[128,1152]{1,0:T(8,128)(2,1)S(1)}, bf16[128,1152]{1,0:T(8,128)(2,1)S(1)}, u32[]{:S(2)}, u32[]{:S(2)}) %collective-permute-start.17) | collective-permute-done | bytes 294944 | tf_op jit(solution)/shard_map/ppermute | solution.py:61
  94.8 4.8 %collective-permute-start.19 = (bf16[128,1152]{1,0:T(8,128)(2,1)S(1)}, bf16[128,1152]{1,0:T(8,128)(2,1)S(1)}, u32[]{:S(2)}, u32[]{:S(2)}) collective-permute-start(bf16[128,1152]{1,0:T(8,128)(2,1)S(1)} %get-tuple-element.181), channel_id=1, source_target_pairs={{0,4},{4,8},{8,12},{12,14},{14,10},{10,6},{6,2},{2,0},{1,5},{5,9},... | collective-permute-start | bytes 884744 | tf_op jit(solution)/shard_map/ppermute | solution.py:61
  99.6 3.5 %all-to-all-start = ((bf16[8,8,16,256]{3,2,1,0:T(8,128)(2,1)}), bf16[8,8,16,256]{3,2,1,0:T(8,128)(2,1)S(1)}, u32[]{:S(2)}, u32[]{:S(2)}) async-start(bf16[8,8,16,256]{3,2,1,0:T(8,128)(2,1)} %pick_heads.1), calls=%async_computation | async-start | bytes 1048576 | tf_op jit(solution)/shard_map/all_to_all | solution.py:929
  103.2 2.9 %terms.14.term_ref = f32[128,1024]{1,0:T(8,128)S(1)} custom-call(s32[18]{0:T(128)S(1)} %dynamic-slice_bitcast_fusion.info, bf16[128,1024]{1,0:T(8,128)(2,1)S(1)} %get-tuple-element.180.lhs_ref, bf16[1024,8192]{1,0:T(8,128)(2,1)} %w_ref.16), custom_call_target="tpu_custom_call" | custom-call | flops 268435456 | bytes 2097152 | tf_op jit(solution)/shard_map/terms/pallas_call | solution.py:294
  118.4 2.9 %collective-permute-start.25 = (bf16[128,1152]{1,0:T(8,128)(2,1)S(1)}, bf16[128,1152]{1,0:T(8,128)(2,1)S(1)}, u32[]{:S(2)}, u32[]{:S(2)}) collective-permute-start(bf16[128,1152]{1,0:T(8,128)(2,1)S(1)} %collective-permute-done.21.refs_0_), channel_id=1, source_target_pairs={{0,4},{4,8},{8,12},{12,14},{14,10},{10,6},{6,2},{2,0},{1,5},{5,9},... | collective-permute-start | bytes 884744 | tf_op jit(solution)/shard_map/ppermute | solution.py:61
  124.5 5.8 %copy-done = bf16[8192,1024]{1,0:T(8,128)(2,1)S(1)} copy-done((bf16[8192,1024]{1,0:T(8,128)(2,1)S(1)}, bf16[8192,1024]{1,0:T(8,128)(2,1)}, u32[]{:S(2)}) %copy-start) | copy-done | bytes 16777240
  138.1 4.6 %collective-permute-done.31.refs_0_ = bf16[128,256]{1,0:T(8,128)(2,1)S(1)} collective-permute-done((bf16[128,256]{1,0:T(8,128)(2,1)S(1)}, bf16[128,256]{1,0:T(8,128)(2,1)S(1)}, u32[]{:S(2)}, u32[]{:S(2)}) %collective-permute-start.31) | collective-permute-done | bytes 65568 | tf_op jit(solution)/shard_map/ppermute | solution.py:61
  153.5 4.3 %attend.1.lhs_ref = bf16[128,1024]{1,0:T(8,128)(2,1)S(1)} custom-call(s32[4,8]{1,0:T(4,128)S(1)} %copy-done.11, s32[4]{0:T(128)S(1)} %copy-done.17, s32[4]{0:T(128)S(1)} %copy-done.12, s32[18]{0:T(128)S(1)} %dynamic-slice_bitcast_fusion.info, f32[128,1024]{1,0:T(8,128)S(1)} %get-tuple-element.225.q_ref, f32[128,128]{1,0:T(8,128)S(1)} %get-tuple-element.226.low_ref, ...), custom_call_target="tpu_custom_call" | custom-call | flops 150994944 | bytes 2883584 | tf_op jit(solution)/shard_map/attend/pallas_call | solution.py:778
  162.5 3.3 %terms.16.refs_0_ = f32[256,1024]{1,0:T(8,128)S(1)} custom-call(s32[18]{0:T(128)S(1)} %dynamic-slice_bitcast_fusion.info, bf16[128,1024]{1,0:T(8,128)(2,1)S(1)} %attend.1.lhs_ref, bf16[1024,8192]{1,0:T(8,128)(2,1)} %w_ref.21), custom_call_target="tpu_custom_call" | custom-call | flops 536870912 | bytes 4194304 | tf_op jit(solution)/shard_map/terms/pallas_call | solution.py:294
  167.9 3.3 %terms.17.refs_0_ = f32[256,1024]{1,0:T(8,128)S(1)} custom-call(s32[18]{0:T(128)S(1)} %dynamic-slice_bitcast_fusion.info, bf16[128,1024]{1,0:T(8,128)(2,1)S(1)} %attend.1.lhs_ref, bf16[1024,8192]{1,0:T(8,128)(2,1)} %w_ref.21), custom_call_target="tpu_custom_call" | custom-call | flops 536870912 | bytes 4194304 | tf_op jit(solution)/shard_map/terms/pallas_call | solution.py:294
  176.4 3.3 %terms.18.refs_0_ = f32[256,1024]{1,0:T(8,128)S(1)} custom-call(s32[18]{0:T(128)S(1)} %dynamic-slice_bitcast_fusion.info, bf16[128,1024]{1,0:T(8,128)(2,1)S(1)} %attend.1.lhs_ref, bf16[1024,8192]{1,0:T(8,128)(2,1)} %w_ref.21), custom_call_target="tpu_custom_call" | custom-call | flops 536870912 | bytes 4194304 | tf_op jit(solution)/shard_map/terms/pallas_call | solution.py:294
  182.0 2.8 %collective-permute-done.43.refs_2_ = bf16[128,1024]{1,0:T(8,128)(2,1)S(1)} collective-permute-done((bf16[128,1024]{1,0:T(8,128)(2,1)S(1)}, bf16[128,1024]{1,0:T(8,128)(2,1)S(1)}, u32[]{:S(2)}, u32[]{:S(2)}) %collective-permute-start.43) | collective-permute-done | bytes 262176 | tf_op jit(solution)/shard_map/ppermute | solution.py:64
  (181 shorter events, 93.6 us)
Async XLA Ops:
  0.6 54.3 %collective-permute-start.12 = (f32[6,1024,256]{2,1,0:T(8,128)}, f32[6,1024,256]{2,1,0:T(8,128)}, u32[]{:S(2)}, u32[]{:S(2)}) collective-permute-start(f32[6,1024,256]{2,1,0:T(8,128)} %bitcast.20), channel_id=1, source_target_pairs={{0,1},{1,0},{2,3},{3,2},{4,5},{5,4},{6,7},{7,6},{8,9},{9,8},{10,11... | collective-permute-start | bytes 18874376 | tf_op jit(solution)/shard_map/ppermute | solution.py:917
  1.2 17.0 %collective-permute-start = (bf16[128,1024]{1,0:T(8,128)(2,1)}, bf16[128,1024]{1,0:T(8,128)(2,1)S(1)}, u32[]{:S(2)}, u32[]{:S(2)}) collective-permute-start(bf16[128,1024]{1,0:T(8,128)(2,1)} %bitcast.24), channel_id=1, source_target_pairs={{0,4},{4,8},{8,12},{12,14},{14,10},{10,6},{6,2},{2,0},{1,5},{5,9},... | collective-permute-start | bytes 786440 | tf_op jit(solution)/shard_map/ppermute | solution.py:61
  3.8 14.4 %collective-permute-start.1 = (bf16[128,1024]{1,0:T(8,128)(2,1)}, bf16[128,1024]{1,0:T(8,128)(2,1)S(1)}, u32[]{:S(2)}, u32[]{:S(2)}) collective-permute-start(bf16[128,1024]{1,0:T(8,128)(2,1)} %bitcast.25), channel_id=1, source_target_pairs={{0,2},{4,0},{8,4},{12,8},{14,12},{10,14},{6,10},{2,6},{1,3},{5,1},... | collective-permute-start | bytes 786440 | tf_op jit(solution)/shard_map/ppermute | solution.py:64
  7.7 10.4 %collective-permute-start.2 = (bf16[64,640]{1,0:T(8,128)(2,1)S(1)}, bf16[64,640]{1,0:T(8,128)(2,1)S(1)}, u32[]{:S(2)}, u32[]{:S(2)}) collective-permute-start(bf16[64,640]{1,0:T(8,128)(2,1)S(1)} %get-tuple-element.133), channel_id=1, source_target_pairs={{0,2},{2,0},{4,6},{6,4},{8,10},{10,8},{12,14},{14,12},{1,3},{3,1},... | collective-permute-start | bytes 245768 | tf_op jit(solution)/shard_map/ppermute | solution.py:86
  18.2 10.9 %collective-permute-start.3 = (bf16[128,1024]{1,0:T(8,128)(2,1)S(1)}, bf16[128,1024]{1,0:T(8,128)(2,1)S(1)}, u32[]{:S(2)}, u32[]{:S(2)}) collective-permute-start(bf16[128,1024]{1,0:T(8,128)(2,1)S(1)} %collective-permute-done.refs_0_), channel_id=1, source_target_pairs={{0,4},{4,8},{8,12},{12,14},{14,10},{10,6},{6,2},{2,0},{1,5},{5,9},... | collective-permute-start | bytes 786440 | tf_op jit(solution)/shard_map/ppermute | solution.py:61
  19.8 9.3 %collective-permute-start.4 = (bf16[128,1024]{1,0:T(8,128)(2,1)S(1)}, bf16[128,1024]{1,0:T(8,128)(2,1)S(1)}, u32[]{:S(2)}, u32[]{:S(2)}) collective-permute-start(bf16[128,1024]{1,0:T(8,128)(2,1)S(1)} %collective-permute-done.1.refs_1_), channel_id=1, source_target_pairs={{0,2},{4,0},{8,4},{12,8},{14,12},{10,14},{6,10},{2,6},{1,3},{5,1},... | collective-permute-start | bytes 786440 | tf_op jit(solution)/shard_map/ppermute | solution.py:64
  20.3 8.8 %collective-permute-start.5 = (bf16[64,640]{1,0:T(8,128)(2,1)S(1)}, bf16[64,640]{1,0:T(8,128)(2,1)S(1)}, u32[]{:S(2)}, u32[]{:S(2)}) collective-permute-start(bf16[64,640]{1,0:T(8,128)(2,1)S(1)} %fusion.2), channel_id=1, source_target_pairs={{0,4},{2,6},{4,0},{6,2},{8,12},{10,14},{12,8},{14,10},{1,5},{3,7},... | collective-permute-start | bytes 245768 | tf_op jit(solution)/shard_map/ppermute | solution.py:86
  29.1 13.8 %collective-permute-start.6 = (bf16[128,1024]{1,0:T(8,128)(2,1)S(1)}, bf16[128,1024]{1,0:T(8,128)(2,1)S(1)}, u32[]{:S(2)}, u32[]{:S(2)}) collective-permute-start(bf16[128,1024]{1,0:T(8,128)(2,1)S(1)} %collective-permute-done.3.refs_0_), channel_id=1, source_target_pairs={{0,4},{4,8},{8,12},{12,14},{14,10},{10,6},{6,2},{2,0},{1,5},{5,9},... | collective-permute-start | bytes 786440 | tf_op jit(solution)/shard_map/ppermute | solution.py:61
  29.4 13.5 %collective-permute-start.7 = (bf16[128,1024]{1,0:T(8,128)(2,1)S(1)}, bf16[128,1024]{1,0:T(8,128)(2,1)S(1)}, u32[]{:S(2)}, u32[]{:S(2)}) collective-permute-start(bf16[128,1024]{1,0:T(8,128)(2,1)S(1)} %collective-permute-done.4.refs_1_), channel_id=1, source_target_pairs={{0,2},{4,0},{8,4},{12,8},{14,12},{10,14},{6,10},{2,6},{1,3},{5,1},... | collective-permute-start | bytes 786440 | tf_op jit(solution)/shard_map/ppermute | solution.py:64
  31.2 11.8 %collective-permute-start.8 = (bf16[64,640]{1,0:T(8,128)(2,1)S(1)}, bf16[64,640]{1,0:T(8,128)(2,1)S(1)}, u32[]{:S(2)}, u32[]{:S(2)}) collective-permute-start(bf16[64,640]{1,0:T(8,128)(2,1)S(1)} %fusion.3), channel_id=1, source_target_pairs={{0,8},{2,10},{4,12},{6,14},{8,0},{10,2},{12,4},{14,6},{1,9},{3,11}... | collective-permute-start | bytes 245768 | tf_op jit(solution)/shard_map/ppermute | solution.py:86
  73.6 8.9 %collective-permute-start.15 = (bf16[128,1152]{1,0:T(8,128)(2,1)S(1)}, bf16[128,1152]{1,0:T(8,128)(2,1)S(1)}, u32[]{:S(2)}, u32[]{:S(2)}) collective-permute-start(bf16[128,1152]{1,0:T(8,128)(2,1)S(1)} %get-tuple-element.165), channel_id=1, source_target_pairs={{0,4},{4,8},{8,12},{12,14},{14,10},{10,6},{6,2},{2,0},{1,5},{5,9},... | collective-permute-start | bytes 884744 | tf_op jit(solution)/shard_map/ppermute | solution.py:61
  73.8 9.5 %collective-permute-start.16 = (bf16[128,1152]{1,0:T(8,128)(2,1)S(1)}, bf16[128,1152]{1,0:T(8,128)(2,1)S(1)}, u32[]{:S(2)}, u32[]{:S(2)}) collective-permute-start(bf16[128,1152]{1,0:T(8,128)(2,1)S(1)} %get-tuple-element.166), channel_id=1, source_target_pairs={{0,2},{4,0},{8,4},{12,8},{14,12},{10,14},{6,10},{2,6},{1,3},{5,1},... | collective-permute-start | bytes 884744 | tf_op jit(solution)/shard_map/ppermute | solution.py:64
  83.6 9.4 %collective-permute-start.17 = (bf16[128,1152]{1,0:T(8,128)(2,1)S(1)}, bf16[128,1152]{1,0:T(8,128)(2,1)S(1)}, u32[]{:S(2)}, u32[]{:S(2)}) collective-permute-start(bf16[128,1152]{1,0:T(8,128)(2,1)S(1)} %get-tuple-element.173), channel_id=1, source_target_pairs={{0,4},{4,8},{8,12},{12,14},{14,10},{10,6},{6,2},{2,0},{1,5},{5,9},... | collective-permute-start | bytes 884744 | tf_op jit(solution)/shard_map/ppermute | solution.py:61
  84.6 9.9 %collective-permute-start.18 = (bf16[128,1152]{1,0:T(8,128)(2,1)S(1)}, bf16[128,1152]{1,0:T(8,128)(2,1)S(1)}, u32[]{:S(2)}, u32[]{:S(2)}) collective-permute-start(bf16[128,1152]{1,0:T(8,128)(2,1)S(1)} %get-tuple-element.174), channel_id=1, source_target_pairs={{0,2},{4,0},{8,4},{12,8},{14,12},{10,14},{6,10},{2,6},{1,3},{5,1},... | collective-permute-start | bytes 884744 | tf_op jit(solution)/shard_map/ppermute | solution.py:64
  94.8 11.2 %collective-permute-start.19 = (bf16[128,1152]{1,0:T(8,128)(2,1)S(1)}, bf16[128,1152]{1,0:T(8,128)(2,1)S(1)}, u32[]{:S(2)}, u32[]{:S(2)}) collective-permute-start(bf16[128,1152]{1,0:T(8,128)(2,1)S(1)} %get-tuple-element.181), channel_id=1, source_target_pairs={{0,4},{4,8},{8,12},{12,14},{14,10},{10,6},{6,2},{2,0},{1,5},{5,9},... | collective-permute-start | bytes 884744 | tf_op jit(solution)/shard_map/ppermute | solution.py:61
  99.6 24.9 %all-to-all-start = ((bf16[8,8,16,256]{3,2,1,0:T(8,128)(2,1)}), bf16[8,8,16,256]{3,2,1,0:T(8,128)(2,1)S(1)}, u32[]{:S(2)}, u32[]{:S(2)}) async-start(bf16[8,8,16,256]{3,2,1,0:T(8,128)(2,1)} %pick_heads.1), calls=%async_computation | async-start | bytes 1048576 | tf_op jit(solution)/shard_map/all_to_all | solution.py:929
  108.1 10.3 %collective-permute-start.21 = (bf16[128,1152]{1,0:T(8,128)(2,1)S(1)}, bf16[128,1152]{1,0:T(8,128)(2,1)S(1)}, u32[]{:S(2)}, u32[]{:S(2)}) collective-permute-start(bf16[128,1152]{1,0:T(8,128)(2,1)S(1)} %get-tuple-element.186.refs_0_), channel_id=1, source_target_pairs={{0,4},{4,8},{8,12},{12,14},{14,10},{10,6},{6,2},{2,0},{1,5},{5,9},... | collective-permute-start | bytes 884744 | tf_op jit(solution)/shard_map/ppermute | solution.py:61
  109.9 8.5 %collective-permute-start.22 = (bf16[128,1152]{1,0:T(8,128)(2,1)S(1)}, bf16[128,1152]{1,0:T(8,128)(2,1)S(1)}, u32[]{:S(2)}, u32[]{:S(2)}) collective-permute-start(bf16[128,1152]{1,0:T(8,128)(2,1)S(1)} %get-tuple-element.186.refs_0_), channel_id=1, source_target_pairs={{0,2},{4,0},{8,4},{12,8},{14,12},{10,14},{6,10},{2,6},{1,3},{5,1},... | collective-permute-start | bytes 884744 | tf_op jit(solution)/shard_map/ppermute | solution.py:64
  118.4 13.4 %collective-permute-start.25 = (bf16[128,1152]{1,0:T(8,128)(2,1)S(1)}, bf16[128,1152]{1,0:T(8,128)(2,1)S(1)}, u32[]{:S(2)}, u32[]{:S(2)}) collective-permute-start(bf16[128,1152]{1,0:T(8,128)(2,1)S(1)} %collective-permute-done.21.refs_0_), channel_id=1, source_target_pairs={{0,4},{4,8},{8,12},{12,14},{14,10},{10,6},{6,2},{2,0},{1,5},{5,9},... | collective-permute-start | bytes 884744 | tf_op jit(solution)/shard_map/ppermute | solution.py:61
  121.3 10.6 %collective-permute-start.26 = (bf16[128,1152]{1,0:T(8,128)(2,1)S(1)}, bf16[128,1152]{1,0:T(8,128)(2,1)S(1)}, u32[]{:S(2)}, u32[]{:S(2)}) collective-permute-start(bf16[128,1152]{1,0:T(8,128)(2,1)S(1)} %collective-permute-done.22.refs_1_), channel_id=1, source_target_pairs={{0,2},{4,0},{8,4},{12,8},{14,12},{10,14},{6,10},{2,6},{1,3},{5,1},... | collective-permute-start | bytes 884744 | tf_op jit(solution)/shard_map/ppermute | solution.py:64
  122.5 9.3 %collective-permute-start.27 = (bf16[128,256]{1,0:T(8,128)(2,1)}, bf16[128,256]{1,0:T(8,128)(2,1)S(1)}, u32[]{:S(2)}, u32[]{:S(2)}) collective-permute-start(bf16[128,256]{1,0:T(8,128)(2,1)} %get-tuple-element.195), channel_id=1, source_target_pairs={{0,4},{4,8},{8,12},{12,14},{14,10},{10,6},{6,2},{2,0},{1,5},{5,9},... | collective-permute-start | bytes 196616 | tf_op jit(solution)/shard_map/ppermute | solution.py:61
  124.5 28.8 %collective-permute-start.37 = (bf16[64,16,256]{2,1,0:T(8,128)(2,1)S(1)}, bf16[64,16,256]{2,1,0:T(8,128)(2,1)S(1)}, u32[]{:S(2)}, u32[]{:S(2)}) collective-permute-start(bf16[64,16,256]{2,1,0:T(8,128)(2,1)S(1)} %bitcast.29), channel_id=1, source_target_pairs={{0,1},{1,0},{2,3},{3,2},{4,5},{5,4},{6,7},{7,6},{8,9},{9,8},{10,11... | collective-permute-start | bytes 1572872 | tf_op jit(solution)/shard_map/ppermute | solution.py:931
  131.8 12.6 %collective-permute-start.29 = (bf16[128,1152]{1,0:T(8,128)(2,1)S(1)}, bf16[128,1152]{1,0:T(8,128)(2,1)S(1)}, u32[]{:S(2)}, u32[]{:S(2)}) collective-permute-start(bf16[128,1152]{1,0:T(8,128)(2,1)S(1)} %collective-permute-done.25.refs_0_), channel_id=1, source_target_pairs={{0,4},{4,8},{8,12},{12,14},{14,10},{10,6},{6,2},{2,0},{1,5},{5,9},... | collective-permute-start | bytes 884744 | tf_op jit(solution)/shard_map/ppermute | solution.py:61
  133.9 10.5 %collective-permute-start.30 = (bf16[128,1152]{1,0:T(8,128)(2,1)S(1)}, bf16[128,1152]{1,0:T(8,128)(2,1)S(1)}, u32[]{:S(2)}, u32[]{:S(2)}) collective-permute-start(bf16[128,1152]{1,0:T(8,128)(2,1)S(1)} %collective-permute-done.26.refs_1_), channel_id=1, source_target_pairs={{0,2},{4,0},{8,4},{12,8},{14,12},{10,14},{6,10},{2,6},{1,3},{5,1},... | collective-permute-start | bytes 884744 | tf_op jit(solution)/shard_map/ppermute | solution.py:64
  (52 other events, 319.7 us)

commit v4 on v3

--- a/solution.py
+++ b/solution.py
@@ -50,6 +50,7 @@
             for d in range(n)
             for c in range(pools)
         ]
+        self.heads = heads
         self.cw = [(order[i], order[(i + 1) % n]) for i in range(n)]
         self.ccw = [(order[i], order[(i - 1) % n]) for i in range(n)]
 
@@ -70,7 +71,7 @@
             m *= 2
         return found
 
-    def gather(self, x, weigh, keep, give):
+    def gather(self, x, weigh, project, aside):
         n, half = self.n, self.half
         h = x.shape[0] // 2
         pairs = self.masks()
@@ -79,12 +80,17 @@
         a = b = x
         for s in range(1, max(half, len(exchange)) + 1):
             if s == half:
-                a, b = a[:h], b[h:]
+                a, b, aside = lax.optimization_barrier((a[:h], b[h:], aside))
+                aside = lax.all_to_all(aside, "tensor", 0, 0, tiled=True)
             if s <= half:
                 a, b = self.right(a), self.left(b)
+            if s == 1:
+                sums = weigh(*ready, sums)
+                x, sums = lax.optimization_barrier((x, sums))
+                keep, give = project(x)
             if s <= len(exchange):
                 came = lax.ppermute(give, "tensor", exchange[s - 1])
-            if s <= half:
+            if 1 < s <= half:
                 sums = weigh(*ready, sums)
             if s <= len(exchange):
                 a, b, sums, came = lax.optimization_barrier((a, b, sums, came))
@@ -95,7 +101,7 @@
                 give = keep.astype(bf16)
             if s <= half:
                 ready = ([n - s, s], [a, b]) if s < half else ([half], [a, b])
-        return weigh(*ready, sums), keep, came
+        return weigh(*ready, sums), keep, came, aside
 
 
 def split(x):
@@ -244,18 +250,13 @@
     term_ref = refs.pop(0)
     outs = refs[-2:]
     got = refs[:-2]
-    rows = term_ref.shape[0] if kind == "first" else term_ref.shape[0] // 2
+    rows = term_ref.shape[0] // 2
     h = rows // 2
     sides = [slice(0, h), slice(h, rows)]
     main, tail = slice(0, depth), slice(depth, depth + 128)
     for j in range(2):
         mine, other = sides[j], sides[1 - j]
         out = outs[j]
-        if kind == "first":
-            out[:, main] = term_ref[mine].astype(bf16)
-            if with_energy:
-                out[:, tail] = energy_lanes(e_ref[mine])
-            continue
         base = j * rows
         if kind == "second":
             own = slice(base + mine.start, base + mine.stop)
@@ -274,11 +275,10 @@
 
 def join(kind, rows, depth, energy, terms, got):
     wide = depth + (0 if energy is None else 128)
-    high = rows // 2 if kind == "first" else rows
     operands = ([] if energy is None else [energy]) + [terms] + got
     return pl.pallas_call(
         functools.partial(join_kernel, kind, depth, energy is not None),
-        out_shape=[jax.ShapeDtypeStruct((high, wide), bf16)] * 2,
+        out_shape=[jax.ShapeDtypeStruct((rows, wide), bf16)] * 2,
         compiler_params=pltpu.CompilerParams(vmem_limit_bytes=12 << 20),
         cost_estimate=pl.CostEstimate(flops=0, bytes_accessed=rows * wide * 8, transcendentals=0),
         name="join",
@@ -331,20 +331,21 @@
     return pl.BlockSpec(shape, lambda j, c, *s: (0,) * len(shape))
 
 
-def ring_sum(ring, info, lhs, weight, depth, energy=None):
+def ring_sum(ring, info, a, b, lhs, weight, depth, energy=None, aside=None):
     n, half = ring.n, ring.half
     rows = lhs.shape[0]
-    terms = terms_of(info, [half], lhs, weight, depth)
-    a, b = join("first", rows, depth, energy, terms, [])
     for d in range(half - 1, -1, -1):
         lhs, a, b = lax.optimization_barrier((lhs, a, b))
         a, b = ring.right(a), ring.left(b)
         terms = terms_of(info, [d, n - d] if d > 0 else [0], lhs, weight, depth)
-        terms, a, b = lax.optimization_barrier((terms, a, b))
+        if d == max(half - 2, 0) and aside is not None:
+            terms, a, b, aside = lax.optimization_barrier((terms, a, b, aside))
+        else:
+            terms, a, b = lax.optimization_barrier((terms, a, b))
         if d > 0:
             kind = "second" if d == half - 1 else "later"
             a, b = join(kind, rows, depth, energy, terms, [a, b])
-    return terms, ([a, b] if half > 1 else [jnp.concatenate([a, b], axis=0)])
+    return terms, ([a, b] if half > 1 else [jnp.concatenate([a, b], axis=0)]), aside
 
 
 def mixer_kernel(arrived, tenants, inner_size, info, adapter, term_ref, *refs):
@@ -479,7 +480,7 @@
         ),
         out_shape=[jax.ShapeDtypeStruct(s, f32) for s in shapes],
         input_output_aliases=aliases,
-        compiler_params=pltpu.CompilerParams(vmem_limit_bytes=16 << 20),
+        compiler_params=pltpu.CompilerParams(vmem_limit_bytes=46 << 20),
         cost_estimate=pl.CostEstimate(
             flops=len(offsets) * 2 * rows * depth * cols,
             bytes_accessed=len(offsets) * depth * cols * 2,
@@ -506,6 +507,22 @@
     lane = lax.broadcasted_iota(jnp.int32, (heads, heads * width), 1)
     row = lax.broadcasted_iota(jnp.int32, (heads, heads * width), 0)
     return jnp.where(lane // width == row, 1.0, 0.0).astype(f32)
+
+
+def far_columns(info, half, w_ref, held, arrived):
+    depth = held.shape[1]
+    at = pl.multiple_of(info[half] * depth, 128)
+    return pltpu.make_async_copy(w_ref.at[:, pl.ds(at, depth)], held, arrived)
+
+
+def first_messages(lhs_ref, held, energy_ref, left_ref, right_ref):
+    term = jnp.dot(lhs_ref[...], held[...], preferred_element_type=f32)
+    h, depth = left_ref.shape[0], held.shape[1]
+    for j, out in enumerate((left_ref, right_ref)):
+        side = slice(j * h, (j + 1) * h)
+        out[:, :depth] = term[side].astype(bf16)
+        if energy_ref is not None:
+            out[:, depth : depth + 128] = energy_lanes(energy_ref[side])
 
 
 def state_kernel(
@@ -515,6 +532,7 @@
     z_ref,
     kept_ref,
     came_ref,
+    w_ref,
     hx_ref,
     hbc_ref,
     tx_ref,
@@ -528,12 +546,23 @@
     gated_ref,
     energy_ref,
     final_ref,
+    left_ref,
+    right_ref,
     initial,
+    held,
+    arrived,
     *,
     slots,
+    half,
 ):
     i = pl.program_id(0)
     count = info.shape[0]
+    copy = far_columns(info, half, w_ref, held, arrived)
+
+    @pl.when(i == 0)
+    def _():
+        copy.start()
+
     is_own = slot[i] // slots == info[count - 1]
 
     @pl.when(is_own)
@@ -621,8 +650,9 @@
     result = within + carried * scales[:length] + scales[2 * length : 2 * length + 1] * values
     z = z_ref[...].astype(bf16).astype(f32)
     gated = result * (z * jax.nn.sigmoid(z))
-    energy_ref[...] = jnp.sum(gated * gated, axis=1, keepdims=True)
-    gated_ref[...] = (gated * gain_ref[...]).astype(bf16)
+    at = pl.ds(pl.multiple_of(i * length, length), length)
+    energy_ref[at, :] = jnp.sum(gated * gated, axis=1, keepdims=True)
+    gated_ref[at, :] = (gated * gain_ref[...]).astype(bf16)
 
     kept = jnp.exp(
         lax.dot_general(
@@ -643,9 +673,14 @@
         at = slice(h * HDIM, (h + 1) * HDIM)
         final_ref[0, at, :] = update[at] + start[at] * kept[h : h + 1]
 
+    @pl.when(i == pl.num_programs(0) - 1)
+    def _():
+        copy.wait()
+        first_messages(gated_ref, held, energy_ref, left_ref, right_ref)
+
 
 def state_pass(
-    info, slot, inner, kept, came, hx, hbc, tx, tbc, bias, rate, skip, gain, own_pool, far_pool
+    half, info, slot, inner, kept, came, weight, hx, hbc, tx, tbc, bias, rate, skip, gain, own_pool, far_pool
 ):
     tenants = slot.shape[0]
     length = inner.shape[0] // 2 // tenants
@@ -665,8 +700,13 @@
         return (jnp.clip(slot[i] - (1 - info[info.shape[0] - 1]) * slots, 0, slots - 1), 0, 0)
 
     pooled = (1, cols, STATE)
+    message = (tenants * length // 2, weight.shape[1] // (2 * half) + 128)
+
+    def fixed(shape):
+        return pl.BlockSpec(shape, lambda i, *s: (0, 0))
+
     return pl.pallas_call(
-        functools.partial(state_kernel, slots=slots),
+        functools.partial(state_kernel, slots=slots, half=half),
         grid_spec=pltpu.PrefetchScalarGridSpec(
             num_scalar_prefetch=2,
             grid=(tenants,),
@@ -675,6 +715,7 @@
                 pl.BlockSpec((length, cols), lambda i, *s: (tenants + i, 0)),
                 pl.BlockSpec((length, kept.shape[1]), lambda i, *s: (i % (tenants // 2), 0)),
                 pl.BlockSpec((length, kept.shape[1]), lambda i, *s: (i % (tenants // 2), 0)),
+                pl.BlockSpec(memory_space=pl.ANY),
                 pl.BlockSpec((1, 3, cols), lambda i, *s: (i, 0, 0)),
                 pl.BlockSpec((1, 3, 2 * STATE), lambda i, *s: (i, 0, 0)),
                 whole(tx),
@@ -687,31 +728,45 @@
                 pl.BlockSpec(pooled, far_slot),
             ],
             out_specs=[
-                rows(cols),
-                rows(1),
+                fixed((tenants * length, cols)),
+                fixed((tenants * length, 1)),
                 pl.BlockSpec(pooled, lambda i, *s: (i, 0, 0)),
+                fixed(message),
+                fixed(message),
             ],
-            scratch_shapes=[pltpu.VMEM((cols, STATE), f32)],
+            scratch_shapes=[
+                pltpu.VMEM((cols, STATE), f32),
+                pltpu.VMEM((weight.shape[0], message[1] - 128), bf16),
+                pltpu.SemaphoreType.DMA,
+            ],
         ),
         out_shape=[
             jax.ShapeDtypeStruct((tenants * length, cols), bf16),
             jax.ShapeDtypeStruct((tenants * length, 1), f32),
             jax.ShapeDtypeStruct((tenants, cols, STATE), f32),
+            jax.ShapeDtypeStruct(message, bf16),
+            jax.ShapeDtypeStruct(message, bf16),
         ],
-        compiler_params=pltpu.CompilerParams(vmem_limit_bytes=28 << 20),
+        compiler_params=pltpu.CompilerParams(vmem_limit_bytes=48 << 20),
         cost_estimate=pl.CostEstimate(
             flops=tenants * 6 * length * cols * STATE,
             bytes_accessed=tenants * cols * STATE * 10,
             transcendentals=0,
         ),
         name="state_pass",
-    )(slot, info, inner, inner, kept, came, hx, hbc, tx, tbc, bias, rate, skip, gain, own_pool, far_pool)
+    )(slot, info, inner, inner, kept, came, weight, hx, hbc, tx, tbc, bias, rate, skip, gain, own_pool, far_pool)
 
 
 def attend_kernel(
-    width, table, limit, adapter, info, q_ref, low_ref, up_ref, near_ref, far_ref, *refs
+    half, width, table, limit, adapter, info, q_ref, low_ref, up_ref, near_ref, far_ref, w_ref, *refs
 ):
-    o_ref = refs[-1]
+    o_ref, left_ref, right_ref, held, arrived = refs[-5:]
+    copy = far_columns(info, half, w_ref, held, arrived)
+
+    @pl.when(pl.program_id(0) == 0)
+    def _():
+        copy.start()
+
     i = pl.program_id(0)
     length = q_ref.shape[0]
     heads = q_ref.shape[1] // HEAD_SIZE
@@ -726,7 +781,7 @@
     q = (q_ref[...] * norm + adapter_scale * raised).astype(bf16)
     q = jnp.concatenate([q[:, h * HEAD_SIZE : (h + 1) * HEAD_SIZE] for h in range(heads)], axis=0)
     fresh = jnp.concatenate([refs[0][...], refs[1][...]], axis=1)
-    for came in refs[2:-1]:
+    for came in refs[2:-5]:
         fresh = fresh + came[...].astype(f32)
     fresh = (fresh * norm).astype(bf16)
     pieces = []
@@ -756,11 +811,17 @@
     out = jnp.dot((old * share).astype(bf16), cached[:, HEAD_SIZE:], preferred_element_type=f32)
     out += jnp.dot((new * share).astype(bf16), fresh[:, HEAD_SIZE:], preferred_element_type=f32)
     out = out.astype(bf16)
+    own_rows = pl.ds(pl.multiple_of(i * length, length), length)
     for h in range(heads):
-        o_ref[:, h * HEAD_SIZE : (h + 1) * HEAD_SIZE] = out[h * length : (h + 1) * length]
-
-
-def attend(ring, width, table, limit, adapter, info, q, low, up, near, far, kv, kv_came):
+        o_ref[own_rows, h * HEAD_SIZE : (h + 1) * HEAD_SIZE] = out[h * length : (h + 1) * length]
+
+    @pl.when(i == pl.num_programs(0) - 1)
+    def _():
+        copy.wait()
+        first_messages(o_ref, held, None, left_ref, right_ref)
+
+
+def attend(ring, width, table, limit, adapter, info, q, low, up, near, far, weight, kv, came):
     tenants = table.shape[0]
     length = q.shape[0] // tenants
 
@@ -769,6 +830,11 @@
 
     def whole(a):
         return pl.BlockSpec(a.shape, lambda i, *s: (0,) * a.ndim)
+
+    message = (q.shape[0] // 2, weight.shape[1] // ring.n)
+
+    def fixed(shape):
+        return pl.BlockSpec(shape, lambda i, *s: (0, 0))
 
     def own(base):
         return pl.BlockSpec(
@@ -776,7 +842,7 @@
         )
 
     return pl.pallas_call(
-        functools.partial(attend_kernel, width),
+        functools.partial(attend_kernel, ring.half, width),
         grid_spec=pltpu.PrefetchScalarGridSpec(
             num_scalar_prefetch=4,
             grid=(tenants,),
@@ -786,53 +852,55 @@
                 pl.BlockSpec((1, *up.shape[1:]), lambda i, t, n, a, info: (a[i], 0, 0)),
                 whole(near),
                 whole(far),
+                pl.BlockSpec(memory_space=pl.ANY),
                 own(0),
                 own(KEY_HEADS),
             ]
-            + [rows(a) for a in kv_came],
-            out_specs=rows(q),
-        ),
-        out_shape=jax.ShapeDtypeStruct(q.shape, bf16),
-        compiler_params=pltpu.CompilerParams(vmem_limit_bytes=24 << 20),
+            + [rows(a) for a in came],
+            out_specs=[fixed(q.shape), fixed(message), fixed(message)],
+            scratch_shapes=[
+                pltpu.VMEM((weight.shape[0], message[1]), bf16),
+                pltpu.SemaphoreType.DMA,
+            ],
+        ),
+        out_shape=[
+            jax.ShapeDtypeStruct(q.shape, bf16),
+            jax.ShapeDtypeStruct(message, bf16),
+            jax.ShapeDtypeStruct(message, bf16),
+        ],
+        compiler_params=pltpu.CompilerParams(vmem_limit_bytes=46 << 20),
         cost_estimate=pl.CostEstimate(
             flops=tenants * 4 * length * q.shape[1] * 288,
             bytes_accessed=near.size * 4 + q.size * 6 + up.size,
             transcendentals=0,
         ),
         name="attend",
-    )(table, limit, adapter, info, q, low, up, near, far, kv, kv, *kv_came)
-
-
-def pick_kernel(info, key_ref, value_ref, o_ref):
-    o_ref[0, :, :, :HEAD_SIZE] = key_ref[...]
-    o_ref[0, :, :, HEAD_SIZE:] = value_ref[...]
-
-
-def pick_heads(info, pool, devices, pools):
-    count, block_len, _ = pool.shape
+    )(table, limit, adapter, info, q, low, up, near, far, weight, kv, kv, *came)
+
+
+def pick_kernel(heads, info, pool_ref, o_ref):
+    for d, head in enumerate(heads):
+        for k in range(2):
+            at = (head + k * KEY_HEADS) * HEAD_SIZE
+            o_ref[d, :, :, k * HEAD_SIZE : (k + 1) * HEAD_SIZE] = pool_ref[:, :, at : at + HEAD_SIZE]
+
+
+def pick_heads(info, pool, heads, pools):
+    count, block_len, wide = pool.shape
     part = block_len // pools
-    each = QUERY_HEADS // devices
-    group = QUERY_HEADS // KEY_HEADS
-
-    def lanes(base):
-        return pl.BlockSpec(
-            (count, part, HEAD_SIZE),
-            lambda d, info: (0, info[info.shape[0] - 1], base + lax.div(d * each, group)),
-        )
-
-    shape = (devices, count, part, 2 * HEAD_SIZE)
+    shape = (len(heads), count, part, 2 * HEAD_SIZE)
     return pl.pallas_call(
-        pick_kernel,
+        functools.partial(pick_kernel, heads),
         grid_spec=pltpu.PrefetchScalarGridSpec(
             num_scalar_prefetch=1,
-            grid=(devices,),
-            in_specs=[lanes(0), lanes(KEY_HEADS)],
-            out_specs=pl.BlockSpec((1, *shape[1:]), lambda d, info: (d, 0, 0, 0)),
+            grid=(1,),
+            in_specs=[pl.BlockSpec((count, part, wide), lambda j, info: (0, info[info.shape[0] - 1], 0))],
+            out_specs=pl.BlockSpec(shape, lambda j, info: (0, 0, 0, 0)),
         ),
         out_shape=jax.ShapeDtypeStruct(shape, bf16),
         compiler_params=pltpu.CompilerParams(vmem_limit_bytes=8 << 20),
         name="pick_heads",
-    )(info, pool, pool)
+    )(info, pool)
 
 
 def fresh_kernel(kind, offsets, heads_at, info, kv_ref, *refs):
@@ -916,26 +984,22 @@
     flat_pool = saved_state_pool.reshape(slots, heads * HDIM, STATE)
     far_pool = lax.ppermute(flat_pool, "pool", swap)
 
-    keep, give = partial_product(info, own_tokens, state_projection)
-    inner, kept, came = ring.gather(
+    inner, kept, came, cache = ring.gather(
         own_tokens,
         lambda offsets, blocks, acc: in_product(info, offsets, blocks, mamba_in_weight, depth, acc),
-        keep,
-        give,
-    )
-
-    mine = pick_heads(info, key_value_pool, n, pools)
-    mine, inner = lax.optimization_barrier((mine, inner))
-    cache = lax.all_to_all(mine, "tensor", 0, 0, tiled=True)
+        lambda x: partial_product(info, x, state_projection),
+        pick_heads(info, key_value_pool, ring.heads, pools),
+    )
     cache = cache.reshape(-1, *cache.shape[2:])
-    far_cache = lax.ppermute(cache, "pool", swap)
-
-    gated, energy, final_state = state_pass(
+
+    gated, energy, final_state, a, b = state_pass(
+        half,
         info,
         tenant_state_slot,
         inner,
         kept,
         came,
+        mamba_out_weight,
         inner_history.astype(f32),
         state_history,
         inner_taps.astype(f32),
@@ -947,7 +1011,9 @@
         flat_pool,
         far_pool,
     )
-    terms, got = ring_sum(ring, info, gated, mamba_out_weight, depth, energy)
+    a, b, cache = lax.optimization_barrier((a, b, cache))
+    far_cache = lax.ppermute(cache, "pool", swap)
+    terms, got, far_cache = ring_sum(ring, info, a, b, gated, mamba_out_weight, depth, energy, far_cache)
     first, message = mixer_step(
         info,
         tenant_adapter,
@@ -978,7 +1044,7 @@
             ka, kb = fresh_join(info, kind, [half - s, n - half + s], n, kv, [ka, kb])
     kv_came = [ka, kb] if half > 1 else [jnp.concatenate([ka, kb], axis=0)]
     query, low = query_step(info, *ready, query_matrix, depth, accs)
-    heads_out = attend(
+    heads_out, a, b = attend(
         ring,
         width,
         tenant_blocks,
@@ -990,10 +1056,11 @@
         adapter_up,
         cache,
         far_cache,
+        attention_out_weight,
         kv,
         kv_came,
     )
-    terms, got = ring_sum(ring, info, heads_out, attention_out_weight, depth)
+    terms, got, _ = ring_sum(ring, info, a, b, heads_out, attention_out_weight, depth)
     second = terms + first.astype(f32)
     for g in got:
         second = second + g.astype(f32)

time: 194 us -> 183 us (0.943)
  local copies, waits for them, and re-layouts: 11 us -> 1.83 us
  waiting for transfers between devices: 39 us -> 34.7 us
  Pallas kernels: 84 us -> 86 us
    unnamed x59 -> x41, local copies, waits for them, and re-layouts: 10.2 us -> 1.08 us
    pallas_call x5, Pallas kernels: 6.96 us -> 15.4 us  [query_step(): pl.pallas_call(functools.partial(query_kernel, offsets, count, accs is No...]
    pallas_call x10 -> x8, Pallas kernels: 30.2 us -> 24.7 us  [terms_of(): pl.pallas_call(term_kernel, grid_spec=pltpu.PrefetchScalarGridSpec(num_sc...]
    ppermute x20, starting transfers between devices: 30.2 us -> 27.7 us  [right(): return lax.ppermute(x, 'tensor', self.cw)]
    ppermute x4, starting transfers between devices: 6.37 us -> 8.58 us  [gather(): came = lax.ppermute(give, 'tensor', exchange[s - 1])]
    ppermute x4, waiting for transfers between devices: 5.2 us -> 3.25 us  [gather(): came = lax.ppermute(give, 'tensor', exchange[s - 1])]
  transfers between devices with their start and end apart: 47 -> 47, of which waited for: 21 -> 26; matrix products, arithmetic and copies ran while one was open for 1% -> 1% of each run, Pallas kernels for 33% -> 42%
where the time goes in v4:
time: 183 us
  Pallas kernels  86 us (47%)
  starting transfers between devices  57.3 us (31%)
  waiting for transfers between devices  34.7 us (19%)
  local copies, waits for them, and re-layouts  1.83 us (1%)
    ppermute x20, starting transfers between devices, right(): return lax.ppermute(x, 'tensor', self.cw)  27.7 us
    pallas_call x8, Pallas kernels, terms_of(): pl.pallas_call(term_kernel, grid_spec=pltpu.PrefetchScalarGridSpec(num_sc...  24.7 us
    pallas_call x5, Pallas kernels, in_product(): pl.pallas_call(functools.partial(in_kernel, offsets, count, chunks, acc i...  24.1 us
    ppermute x20, waiting for transfers between devices, right(): return lax.ppermute(x, 'tensor', self.cw)  20 us
    ppermute x20, starting transfers between devices, left(): return lax.ppermute(x, 'tensor', self.ccw)  17 us
    pallas_call x5, Pallas kernels, query_step(): pl.pallas_call(functools.partial(query_kernel, offsets, count, accs is No...  15.4 us
    ppermute x20, waiting for transfers between devices, left(): return lax.ppermute(x, 'tensor', self.ccw)  11.4 us
    pallas_call x1, Pallas kernels, state_pass(): pl.pallas_call(functools.partial(state_kernel, slots=slots, half=half), g...  10.2 us
  transfers between devices with their start and end apart: 47, of which 26 were waited for; matrix products, arithmetic and copies ran while one was open for 1% of the time, Pallas kernels for 42%

profile of v4, /device:TPU:0, one launch (start us, length us, event | category | flops | bytes accessed | tf_op | source)
XLA Modules:
  0.0 182.9 jit_solution(17160626509387384719)
XLA Ops:
  5.5 3.8 %in_product.5.refs_3_ = f32[256,1024]{1,0:T(8,128)S(1)} custom-call(s32[18]{0:T(128)S(1)} %dynamic-slice_bitcast_fusion.info, bf16[128,1024]{1,0:T(8,128)(2,1)S(1)} %bitcast.20, bf16[8192,2,1024]{2,1,0:T(2,128)(2,1)} %refs_2_.11), custom_call_target="tpu_custom_call" | custom-call | flops 1073741824 | bytes 8388608 | tf_op jit(solution)/shard_map/in_product/pallas_call | solution.py:204
  18.9 5.5 %in_product.6.refs_3_ = f32[256,1024]{1,0:T(8,128)S(1)} custom-call(s32[18]{0:T(128)S(1)} %dynamic-slice_bitcast_fusion.info, bf16[128,1024]{1,0:T(8,128)(2,1)S(1)} %collective-permute-done.refs_0_, bf16[128,1024]{1,0:T(8,128)(2,1)S(1)} %collective-permute-done.1.refs_1_, bf16[8192,2,1024]{2,1,0:T(2,128)(2,1)} %refs_2_.11, ...), custom_call_target="tpu_custom_call", output_to_operand_aliasing={{}: (4, {})} | custom-call | flops 2147483648 | bytes 16777216 | tf_op jit(solution)/shard_map/in_product/pallas_call | solution.py:204
  27.3 2.7 %collective-permute-start.8 = (bf16[64,640]{1,0:T(8,128)(2,1)S(1)}, bf16[64,640]{1,0:T(8,128)(2,1)S(1)}, u32[]{:S(2)}, u32[]{:S(2)}) collective-permute-start(bf16[64,640]{1,0:T(8,128)(2,1)S(1)} %fusion.3), channel_id=1, source_target_pairs={{0,8},{2,10},{4,12},{6,14},{8,0},{10,2},{12,4},{14,6},{1,9},{3,11}... | collective-permute-start | bytes 245768 | tf_op jit(solution)/shard_map/ppermute | solution.py:92
  29.9 5.5 %in_product.7.refs_3_ = f32[256,1024]{1,0:T(8,128)S(1)} custom-call(s32[18]{0:T(128)S(1)} %dynamic-slice_bitcast_fusion.info, bf16[128,1024]{1,0:T(8,128)(2,1)S(1)} %collective-permute-done.3.refs_0_, bf16[128,1024]{1,0:T(8,128)(2,1)S(1)} %collective-permute-done.4.refs_1_, bf16[8192,2,1024]{2,1,0:T(2,128)(2,1)} %refs_2_.11, ...), custom_call_target="tpu_custom_call", output_to_operand_aliasing={{}: (4, {})} | custom-call | flops 2147483648 | bytes 16777216 | tf_op jit(solution)/shard_map/in_product/pallas_call | solution.py:204
  36.8 3.5 %all-to-all-start = ((bf16[8,8,16,256]{3,2,1,0:T(8,128)(2,1)}), bf16[8,8,16,256]{3,2,1,0:T(8,128)(2,1)S(1)}, u32[]{:S(2)}, u32[]{:S(2)}) async-start(bf16[8,8,16,256]{3,2,1,0:T(8,128)(2,1)} %pick_heads.1), calls=%async_computation | async-start | bytes 1048576 | tf_op jit(solution)/shard_map/all_to_all | solution.py:84
  44.4 5.5 %in_product.8.refs_3_ = f32[256,1024]{1,0:T(8,128)S(1)} custom-call(s32[18]{0:T(128)S(1)} %dynamic-slice_bitcast_fusion.info, bf16[128,1024]{1,0:T(8,128)(2,1)S(1)} %collective-permute-done.6.refs_0_, bf16[128,1024]{1,0:T(8,128)(2,1)S(1)} %collective-permute-done.7.refs_1_, bf16[8192,2,1024]{2,1,0:T(2,128)(2,1)} %refs_2_.11, ...), custom_call_target="tpu_custom_call", output_to_operand_aliasing={{}: (4, {})} | custom-call | flops 2147483648 | bytes 16777216 | tf_op jit(solution)/shard_map/in_product/pallas_call | solution.py:204
  50.1 4.0 %in_product.9.x_ref.z_ref = f32[256,1024]{1,0:T(8,128)S(1)} custom-call(s32[18]{0:T(128)S(1)} %dynamic-slice_bitcast_fusion.info, bf16[64,1024]{1,0:T(8,128)(2,1)S(1)} %collective-permute-done.9.refs_0_, bf16[64,1024]{1,0:T(8,128)(2,1)S(1)} %collective-permute-done.10.refs_1_, bf16[8192,2,1024]{2,1,0:T(2,128)(2,1)} %refs_2_.11, ...), custom_call_target="tpu_custom_call", output_to_operand_aliasing={{}: (4, {})} | custom-call | flops 1073741824 | bytes 8388608 | tf_op jit(solution)/shard_map/in_product/pallas_call | solution.py:204
  54.1 10.2 %state_pass.1 = (bf16[128,1024]{1,0:T(8,128)(2,1)S(1)}, f32[128,1]{1,0:T(8,128)S(1)}, f32[4,1024,256]{2,1,0:T(8,128)}, bf16[64,1152]{1,0:T(8,128)(2,1)S(1)}, bf16[64,1152]{1,0:T(8,128)(2,1)S(1)}) custom-call(s32[4]{0:T(128)S(1)} %copy-done.10, s32[18]{0:T(128)S(1)} %dynamic-slice_bitcast_fusion.info, f32[256,1024]{1,0:T(8,128)S(1)} %in_product.9.x_ref.z_ref, ...), custom_call_target="tpu_custom_call" | custom-call | flops 201326592 | bytes 10485760 | tf_op jit(solution)/shard_map/state_pass/pallas_call | solution.py:708
  64.4 4.5 %collective-permute-start.13 = (bf16[64,1152]{1,0:T(8,128)(2,1)S(1)}, bf16[64,1152]{1,0:T(8,128)(2,1)S(1)}, u32[]{:S(2)}, u32[]{:S(2)}) collective-permute-start(bf16[64,1152]{1,0:T(8,128)(2,1)S(1)} %get-tuple-element.168), channel_id=1, source_target_pairs={{0,4},{4,8},{8,12},{12,14},{14,10},{10,6},{6,2},{2,0},{1,5},{5,9},... | collective-permute-start | bytes 442376 | tf_op jit(solution)/shard_map/ppermute | solution.py:62
  68.8 3.2 %terms.8.refs_1_ = f32[256,1024]{1,0:T(8,128)S(1)} custom-call(s32[18]{0:T(128)S(1)} %dynamic-slice_bitcast_fusion.info, bf16[128,1024]{1,0:T(8,128)(2,1)S(1)} %get-tuple-element.192.lhs_ref, bf16[1024,8192]{1,0:T(8,128)(2,1)} %w_ref.16), custom_call_target="tpu_custom_call" | custom-call | flops 536870912 | bytes 4194304 | tf_op jit(solution)/shard_map/terms/pallas_call | solution.py:294
  77.1 3.2 %terms.9.refs_1_ = f32[256,1024]{1,0:T(8,128)S(1)} custom-call(s32[18]{0:T(128)S(1)} %dynamic-slice_bitcast_fusion.info, bf16[128,1024]{1,0:T(8,128)(2,1)S(1)} %get-tuple-element.192.lhs_ref, bf16[1024,8192]{1,0:T(8,128)(2,1)} %w_ref.16), custom_call_target="tpu_custom_call" | custom-call | flops 536870912 | bytes 4194304 | tf_op jit(solution)/shard_map/terms/pallas_call | solution.py:294
  80.3 3.0 %collective-permute-done.15.refs_2_ = bf16[128,1152]{1,0:T(8,128)(2,1)S(1)} collective-permute-done((bf16[128,1152]{1,0:T(8,128)(2,1)S(1)}, bf16[128,1152]{1,0:T(8,128)(2,1)S(1)}, u32[]{:S(2)}, u32[]{:S(2)}) %collective-permute-start.15) | collective-permute-done | bytes 294944 | tf_op jit(solution)/shard_map/ppermute | solution.py:62
  86.0 3.2 %terms.10.refs_1_ = f32[256,1024]{1,0:T(8,128)S(1)} custom-call(s32[18]{0:T(128)S(1)} %dynamic-slice_bitcast_fusion.info, bf16[128,1024]{1,0:T(8,128)(2,1)S(1)} %get-tuple-element.192.lhs_ref, bf16[1024,8192]{1,0:T(8,128)(2,1)} %w_ref.16), custom_call_target="tpu_custom_call" | custom-call | flops 536870912 | bytes 4194304 | tf_op jit(solution)/shard_map/terms/pallas_call | solution.py:294
  116.3 3.2 %query_step.6 = (f32[128,1024]{1,0:T(8,128)S(1)}, f32[128,128]{1,0:T(8,128)S(1)}) custom-call(s32[18]{0:T(128)S(1)} %dynamic-slice_bitcast_fusion.info, bf16[128,1152]{1,0:T(8,128)(2,1)S(1)} %collective-permute-done.22.refs_0_, bf16[128,1152]{1,0:T(8,128)(2,1)S(1)} %collective-permute-done.23.refs_1_, ...), custom_call_target="tpu_custom_call", output_to_operand_aliasing={{0}: (4, {}), {1}: (5, {})} | custom-call | flops 536870912 | bytes 4194304 | tf_op jit(solution)/shard_map/query_step/pallas_call | solution.py:473
  119.5 2.7 %collective-permute-done.28.refs_0_ = bf16[128,256]{1,0:T(8,128)(2,1)S(1)} collective-permute-done((bf16[128,256]{1,0:T(8,128)(2,1)S(1)}, bf16[128,256]{1,0:T(8,128)(2,1)S(1)}, u32[]{:S(2)}, u32[]{:S(2)}) %collective-permute-start.28) | collective-permute-done | bytes 65568 | tf_op jit(solution)/shard_map/ppermute | solution.py:62
  129.0 3.3 %query_step.7 = (f32[128,1024]{1,0:T(8,128)S(1)}, f32[128,128]{1,0:T(8,128)S(1)}) custom-call(s32[18]{0:T(128)S(1)} %dynamic-slice_bitcast_fusion.info, bf16[128,1152]{1,0:T(8,128)(2,1)S(1)} %collective-permute-done.26.refs_0_, bf16[128,1152]{1,0:T(8,128)(2,1)S(1)} %collective-permute-done.27.refs_1_, ...), custom_call_target="tpu_custom_call", output_to_operand_aliasing={{0}: (4, {}), {1}: (5, {})} | custom-call | flops 536870912 | bytes 4194304 | tf_op jit(solution)/shard_map/query_step/pallas_call | solution.py:473
  139.0 3.3 %query_step.8 = (f32[128,1024]{1,0:T(8,128)S(1)}, f32[128,128]{1,0:T(8,128)S(1)}) custom-call(s32[18]{0:T(128)S(1)} %dynamic-slice_bitcast_fusion.info, bf16[128,1152]{1,0:T(8,128)(2,1)S(1)} %collective-permute-done.30.refs_0_, bf16[128,1152]{1,0:T(8,128)(2,1)S(1)} %collective-permute-done.31.refs_1_, ...), custom_call_target="tpu_custom_call", output_to_operand_aliasing={{0}: (4, {}), {1}: (5, {})} | custom-call | flops 536870912 | bytes 4194304 | tf_op jit(solution)/shard_map/query_step/pallas_call | solution.py:473
  142.5 3.1 %query_step.9 = (f32[128,1024]{1,0:T(8,128)S(1)}, f32[128,128]{1,0:T(8,128)S(1)}) custom-call(s32[18]{0:T(128)S(1)} %dynamic-slice_bitcast_fusion.info, bf16[64,1152]{1,0:T(8,128)(2,1)S(1)} %collective-permute-done.34.refs_0_, bf16[64,1152]{1,0:T(8,128)(2,1)S(1)} %collective-permute-done.35.refs_1_, ...), custom_call_target="tpu_custom_call", output_to_operand_aliasing={{0}: (4, {}), {1}: (5, {})} | custom-call | flops 268435456 | bytes 2097152 | tf_op jit(solution)/shard_map/query_step/pallas_call | solution.py:473
  145.7 4.8 %attend.1 = (bf16[128,1024]{1,0:T(8,128)(2,1)S(1)}, bf16[64,1024]{1,0:T(8,128)(2,1)S(1)}, bf16[64,1024]{1,0:T(8,128)(2,1)S(1)}) custom-call(s32[4,8]{1,0:T(4,128)S(1)} %copy-done.9, s32[4]{0:T(128)S(1)} %copy-done.14, s32[4]{0:T(128)S(1)} %copy-done.8, s32[18]{0:T(128)S(1)} %dynamic-slice_bitcast_fusion.info, f32[128,1024]{1,0:T(8,128)S(1)} %get-tuple-element.237.q_ref, ...), custom_call_target="tpu_custom_call" | custom-call | flops 150994944 | bytes 2883584 | tf_op jit(solution)/shard_map/attend/pallas_call | solution.py:844
  152.5 3.3 %terms.12.refs_0_ = f32[256,1024]{1,0:T(8,128)S(1)} custom-call(s32[18]{0:T(128)S(1)} %dynamic-slice_bitcast_fusion.info, bf16[128,1024]{1,0:T(8,128)(2,1)S(1)} %get-tuple-element.266.lhs_ref, bf16[1024,8192]{1,0:T(8,128)(2,1)} %w_ref.21), custom_call_target="tpu_custom_call" | custom-call | flops 536870912 | bytes 4194304 | tf_op jit(solution)/shard_map/terms/pallas_call | solution.py:294
  160.1 3.3 %terms.13.refs_0_ = f32[256,1024]{1,0:T(8,128)S(1)} custom-call(s32[18]{0:T(128)S(1)} %dynamic-slice_bitcast_fusion.info, bf16[128,1024]{1,0:T(8,128)(2,1)S(1)} %get-tuple-element.266.lhs_ref, bf16[1024,8192]{1,0:T(8,128)(2,1)} %w_ref.21), custom_call_target="tpu_custom_call" | custom-call | flops 536870912 | bytes 4194304 | tf_op jit(solution)/shard_map/terms/pallas_call | solution.py:294
  163.3 3.3 %collective-permute-done.40.refs_1_ = bf16[128,1024]{1,0:T(8,128)(2,1)S(1)} collective-permute-done((bf16[128,1024]{1,0:T(8,128)(2,1)S(1)}, bf16[128,1024]{1,0:T(8,128)(2,1)S(1)}, u32[]{:S(2)}, u32[]{:S(2)}) %collective-permute-start.40) | collective-permute-done | bytes 262176 | tf_op jit(solution)/shard_map/ppermute | solution.py:62
  169.3 3.2 %terms.14.refs_0_ = f32[256,1024]{1,0:T(8,128)S(1)} custom-call(s32[18]{0:T(128)S(1)} %dynamic-slice_bitcast_fusion.info, bf16[128,1024]{1,0:T(8,128)(2,1)S(1)} %get-tuple-element.266.lhs_ref, bf16[1024,8192]{1,0:T(8,128)(2,1)} %w_ref.21), custom_call_target="tpu_custom_call" | custom-call | flops 536870912 | bytes 4194304 | tf_op jit(solution)/shard_map/terms/pallas_call | solution.py:294
  176.7 2.6 %terms.15 = f32[128,1024]{1,0:T(8,128)S(1)} custom-call(s32[18]{0:T(128)S(1)} %dynamic-slice_bitcast_fusion.info, bf16[128,1024]{1,0:T(8,128)(2,1)S(1)} %get-tuple-element.266.lhs_ref, bf16[1024,8192]{1,0:T(8,128)(2,1)} %w_ref.21), custom_call_target="tpu_custom_call" | custom-call | flops 268435456 | bytes 2097152 | tf_op jit(solution)/shard_map/terms/pallas_call | solution.py:294
  (157 shorter events, 88.0 us)
Async XLA Ops:
  0.6 53.4 %collective-permute-start.12 = (f32[6,1024,256]{2,1,0:T(8,128)}, f32[6,1024,256]{2,1,0:T(8,128)}, u32[]{:S(2)}, u32[]{:S(2)}) collective-permute-start(f32[6,1024,256]{2,1,0:T(8,128)} %bitcast.30), channel_id=1, source_target_pairs={{0,1},{1,0},{2,3},{3,2},{4,5},{5,4},{6,7},{7,6},{8,9},{9,8},{10,11... | collective-permute-start | bytes 18874376 | tf_op jit(solution)/shard_map/ppermute | solution.py:985
  1.1 13.7 %collective-permute-start.1 = (bf16[128,1024]{1,0:T(8,128)(2,1)}, bf16[128,1024]{1,0:T(8,128)(2,1)S(1)}, u32[]{:S(2)}, u32[]{:S(2)}) collective-permute-start(bf16[128,1024]{1,0:T(8,128)(2,1)} %bitcast.18), channel_id=1, source_target_pairs={{0,2},{4,0},{8,4},{12,8},{14,12},{10,14},{6,10},{2,6},{1,3},{5,1},... | collective-permute-start | bytes 786440 | tf_op jit(solution)/shard_map/ppermute | solution.py:65
  3.7 11.1 %collective-permute-start = (bf16[128,1024]{1,0:T(8,128)(2,1)}, bf16[128,1024]{1,0:T(8,128)(2,1)S(1)}, u32[]{:S(2)}, u32[]{:S(2)}) collective-permute-start(bf16[128,1024]{1,0:T(8,128)(2,1)} %bitcast.19), channel_id=1, source_target_pairs={{0,4},{4,8},{8,12},{12,14},{14,10},{10,6},{6,2},{2,0},{1,5},{5,9},... | collective-permute-start | bytes 786440 | tf_op jit(solution)/shard_map/ppermute | solution.py:62
  14.8 10.4 %collective-permute-start.3 = (bf16[128,1024]{1,0:T(8,128)(2,1)S(1)}, bf16[128,1024]{1,0:T(8,128)(2,1)S(1)}, u32[]{:S(2)}, u32[]{:S(2)}) collective-permute-start(bf16[128,1024]{1,0:T(8,128)(2,1)S(1)} %collective-permute-done.refs_0_), channel_id=1, source_target_pairs={{0,4},{4,8},{8,12},{12,14},{14,10},{10,6},{6,2},{2,0},{1,5},{5,9},... | collective-permute-start | bytes 786440 | tf_op jit(solution)/shard_map/ppermute | solution.py:62
  16.7 8.4 %collective-permute-start.4 = (bf16[128,1024]{1,0:T(8,128)(2,1)S(1)}, bf16[128,1024]{1,0:T(8,128)(2,1)S(1)}, u32[]{:S(2)}, u32[]{:S(2)}) collective-permute-start(bf16[128,1024]{1,0:T(8,128)(2,1)S(1)} %collective-permute-done.1.refs_1_), channel_id=1, source_target_pairs={{0,2},{4,0},{8,4},{12,8},{14,12},{10,14},{6,10},{2,6},{1,3},{5,1},... | collective-permute-start | bytes 786440 | tf_op jit(solution)/shard_map/ppermute | solution.py:65
  16.9 8.3 %collective-permute-start.5 = (bf16[64,640]{1,0:T(8,128)(2,1)S(1)}, bf16[64,640]{1,0:T(8,128)(2,1)S(1)}, u32[]{:S(2)}, u32[]{:S(2)}) collective-permute-start(bf16[64,640]{1,0:T(8,128)(2,1)S(1)} %fusion.2), channel_id=1, source_target_pairs={{0,4},{2,6},{4,0},{6,2},{8,12},{10,14},{12,8},{14,10},{1,5},{3,7},... | collective-permute-start | bytes 245768 | tf_op jit(solution)/shard_map/ppermute | solution.py:92
  25.2 11.6 %collective-permute-start.6 = (bf16[128,1024]{1,0:T(8,128)(2,1)S(1)}, bf16[128,1024]{1,0:T(8,128)(2,1)S(1)}, u32[]{:S(2)}, u32[]{:S(2)}) collective-permute-start(bf16[128,1024]{1,0:T(8,128)(2,1)S(1)} %collective-permute-done.3.refs_0_), channel_id=1, source_target_pairs={{0,4},{4,8},{8,12},{12,14},{14,10},{10,6},{6,2},{2,0},{1,5},{5,9},... | collective-permute-start | bytes 786440 | tf_op jit(solution)/shard_map/ppermute | solution.py:62
  25.4 11.3 %collective-permute-start.7 = (bf16[128,1024]{1,0:T(8,128)(2,1)S(1)}, bf16[128,1024]{1,0:T(8,128)(2,1)S(1)}, u32[]{:S(2)}, u32[]{:S(2)}) collective-permute-start(bf16[128,1024]{1,0:T(8,128)(2,1)S(1)} %collective-permute-done.4.refs_1_), channel_id=1, source_target_pairs={{0,2},{4,0},{8,4},{12,8},{14,12},{10,14},{6,10},{2,6},{1,3},{5,1},... | collective-permute-start | bytes 786440 | tf_op jit(solution)/shard_map/ppermute | solution.py:65
  27.3 9.4 %collective-permute-start.8 = (bf16[64,640]{1,0:T(8,128)(2,1)S(1)}, bf16[64,640]{1,0:T(8,128)(2,1)S(1)}, u32[]{:S(2)}, u32[]{:S(2)}) collective-permute-start(bf16[64,640]{1,0:T(8,128)(2,1)S(1)} %fusion.3), channel_id=1, source_target_pairs={{0,8},{2,10},{4,12},{6,14},{8,0},{10,2},{12,4},{14,6},{1,9},{3,11}... | collective-permute-start | bytes 245768 | tf_op jit(solution)/shard_map/ppermute | solution.py:92
  36.8 27.5 %all-to-all-start = ((bf16[8,8,16,256]{3,2,1,0:T(8,128)(2,1)}), bf16[8,8,16,256]{3,2,1,0:T(8,128)(2,1)S(1)}, u32[]{:S(2)}, u32[]{:S(2)}) async-start(bf16[8,8,16,256]{3,2,1,0:T(8,128)(2,1)} %pick_heads.1), calls=%async_computation | async-start | bytes 1048576 | tf_op jit(solution)/shard_map/all_to_all | solution.py:84
  40.4 9.5 %collective-permute-start.11 = (bf16[64,640]{1,0:T(8,128)(2,1)S(1)}, bf16[64,640]{1,0:T(8,128)(2,1)S(1)}, u32[]{:S(2)}, u32[]{:S(2)}) collective-permute-start(bf16[64,640]{1,0:T(8,128)(2,1)S(1)} %get-tuple-element.274), channel_id=1, source_target_pairs={{0,2},{2,0},{4,6},{6,4},{8,10},{10,8},{12,14},{14,12},{1,3},{3,1},... | collective-permute-start | bytes 245768 | tf_op jit(solution)/shard_map/ppermute | solution.py:92
  64.3 19.3 %collective-permute-start.17 = (bf16[64,16,256]{2,1,0:T(8,128)(2,1)S(1)}, bf16[64,16,256]{2,1,0:T(8,128)(2,1)S(1)}, u32[]{:S(2)}, u32[]{:S(2)}) collective-permute-start(bf16[64,16,256]{2,1,0:T(8,128)(2,1)S(1)} %bitcast.23), channel_id=1, source_target_pairs={{0,1},{1,0},{2,3},{3,2},{4,5},{5,4},{6,7},{7,6},{8,9},{9,8},{10,11... | collective-permute-start | bytes 1572872 | tf_op jit(solution)/shard_map/ppermute | solution.py:1015
  75.0 8.3 %collective-permute-start.15 = (bf16[128,1152]{1,0:T(8,128)(2,1)S(1)}, bf16[128,1152]{1,0:T(8,128)(2,1)S(1)}, u32[]{:S(2)}, u32[]{:S(2)}) collective-permute-start(bf16[128,1152]{1,0:T(8,128)(2,1)S(1)} %get-tuple-element.176), channel_id=1, source_target_pairs={{0,4},{4,8},{8,12},{12,14},{14,10},{10,6},{6,2},{2,0},{1,5},{5,9},... | collective-permute-start | bytes 884744 | tf_op jit(solution)/shard_map/ppermute | solution.py:62
  75.3 8.3 %collective-permute-start.16 = (bf16[128,1152]{1,0:T(8,128)(2,1)S(1)}, bf16[128,1152]{1,0:T(8,128)(2,1)S(1)}, u32[]{:S(2)}, u32[]{:S(2)}) collective-permute-start(bf16[128,1152]{1,0:T(8,128)(2,1)S(1)} %get-tuple-element.177), channel_id=1, source_target_pairs={{0,2},{4,0},{8,4},{12,8},{14,12},{10,14},{6,10},{2,6},{1,3},{5,1},... | collective-permute-start | bytes 884744 | tf_op jit(solution)/shard_map/ppermute | solution.py:65
  101.4 9.9 %collective-permute-start.23 = (bf16[128,1152]{1,0:T(8,128)(2,1)S(1)}, bf16[128,1152]{1,0:T(8,128)(2,1)S(1)}, u32[]{:S(2)}, u32[]{:S(2)}) collective-permute-start(bf16[128,1152]{1,0:T(8,128)(2,1)S(1)} %get-tuple-element.198.refs_0_), channel_id=1, source_target_pairs={{0,2},{4,0},{8,4},{12,8},{14,12},{10,14},{6,10},{2,6},{1,3},{5,1},... | collective-permute-start | bytes 884744 | tf_op jit(solution)/shard_map/ppermute | solution.py:65
  102.1 9.2 %collective-permute-start.22 = (bf16[128,1152]{1,0:T(8,128)(2,1)S(1)}, bf16[128,1152]{1,0:T(8,128)(2,1)S(1)}, u32[]{:S(2)}, u32[]{:S(2)}) collective-permute-start(bf16[128,1152]{1,0:T(8,128)(2,1)S(1)} %get-tuple-element.198.refs_0_), channel_id=1, source_target_pairs={{0,4},{4,8},{8,12},{12,14},{14,10},{10,6},{6,2},{2,0},{1,5},{5,9},... | collective-permute-start | bytes 884744 | tf_op jit(solution)/shard_map/ppermute | solution.py:62
  111.3 13.1 %collective-permute-start.26 = (bf16[128,1152]{1,0:T(8,128)(2,1)S(1)}, bf16[128,1152]{1,0:T(8,128)(2,1)S(1)}, u32[]{:S(2)}, u32[]{:S(2)}) collective-permute-start(bf16[128,1152]{1,0:T(8,128)(2,1)S(1)} %collective-permute-done.22.refs_0_), channel_id=1, source_target_pairs={{0,4},{4,8},{8,12},{12,14},{14,10},{10,6},{6,2},{2,0},{1,5},{5,9},... | collective-permute-start | bytes 884744 | tf_op jit(solution)/shard_map/ppermute | solution.py:62
  113.4 10.9 %collective-permute-start.27 = (bf16[128,1152]{1,0:T(8,128)(2,1)S(1)}, bf16[128,1152]{1,0:T(8,128)(2,1)S(1)}, u32[]{:S(2)}, u32[]{:S(2)}) collective-permute-start(bf16[128,1152]{1,0:T(8,128)(2,1)S(1)} %collective-permute-done.23.refs_1_), channel_id=1, source_target_pairs={{0,2},{4,0},{8,4},{12,8},{14,12},{10,14},{6,10},{2,6},{1,3},{5,1},... | collective-permute-start | bytes 884744 | tf_op jit(solution)/shard_map/ppermute | solution.py:65
  116.1 8.3 %collective-permute-start.29 = (bf16[128,256]{1,0:T(8,128)(2,1)S(1)}, bf16[128,256]{1,0:T(8,128)(2,1)S(1)}, u32[]{:S(2)}, u32[]{:S(2)}) collective-permute-start(bf16[128,256]{1,0:T(8,128)(2,1)S(1)} %get-tuple-element.208), channel_id=1, source_target_pairs={{0,2},{4,0},{8,4},{12,8},{14,12},{10,14},{6,10},{2,6},{1,3},{5,1},... | collective-permute-start | bytes 196616 | tf_op jit(solution)/shard_map/ppermute | solution.py:65
  124.3 9.9 %collective-permute-start.30 = (bf16[128,1152]{1,0:T(8,128)(2,1)S(1)}, bf16[128,1152]{1,0:T(8,128)(2,1)S(1)}, u32[]{:S(2)}, u32[]{:S(2)}) collective-permute-start(bf16[128,1152]{1,0:T(8,128)(2,1)S(1)} %collective-permute-done.26.refs_0_), channel_id=1, source_target_pairs={{0,4},{4,8},{8,12},{12,14},{14,10},{10,6},{6,2},{2,0},{1,5},{5,9},... | collective-permute-start | bytes 884744 | tf_op jit(solution)/shard_map/ppermute | solution.py:62
  126.1 8.2 %collective-permute-start.31 = (bf16[128,1152]{1,0:T(8,128)(2,1)S(1)}, bf16[128,1152]{1,0:T(8,128)(2,1)S(1)}, u32[]{:S(2)}, u32[]{:S(2)}) collective-permute-start(bf16[128,1152]{1,0:T(8,128)(2,1)S(1)} %collective-permute-done.27.refs_1_), channel_id=1, source_target_pairs={{0,2},{4,0},{8,4},{12,8},{14,12},{10,14},{6,10},{2,6},{1,3},{5,1},... | collective-permute-start | bytes 884744 | tf_op jit(solution)/shard_map/ppermute | solution.py:65
  134.3 8.2 %collective-permute-start.34 = (bf16[64,1152]{1,0:T(8,128)(2,1)S(1)}, bf16[64,1152]{1,0:T(8,128)(2,1)S(1)}, u32[]{:S(2)}, u32[]{:S(2)}) collective-permute-start(bf16[64,1152]{1,0:T(8,128)(2,1)S(1)} %slice.18), channel_id=1, source_target_pairs={{0,4},{4,8},{8,12},{12,14},{14,10},{10,6},{6,2},{2,0},{1,5},{5,9},... | collective-permute-start | bytes 442376 | tf_op jit(solution)/shard_map/ppermute | solution.py:62
  158.0 8.6 %collective-permute-start.40 = (bf16[128,1024]{1,0:T(8,128)(2,1)S(1)}, bf16[128,1024]{1,0:T(8,128)(2,1)S(1)}, u32[]{:S(2)}, u32[]{:S(2)}) collective-permute-start(bf16[128,1024]{1,0:T(8,128)(2,1)S(1)} %get-tuple-element.251), channel_id=1, source_target_pairs={{0,4},{4,8},{8,12},{12,14},{14,10},{10,6},{6,2},{2,0},{1,5},{5,9},... | collective-permute-start | bytes 786440 | tf_op jit(solution)/shard_map/ppermute | solution.py:62
  158.8 8.3 %collective-permute-start.41 = (bf16[128,1024]{1,0:T(8,128)(2,1)S(1)}, bf16[128,1024]{1,0:T(8,128)(2,1)S(1)}, u32[]{:S(2)}, u32[]{:S(2)}) collective-permute-start(bf16[128,1024]{1,0:T(8,128)(2,1)S(1)} %get-tuple-element.252), channel_id=1, source_target_pairs={{0,2},{4,0},{8,4},{12,8},{14,12},{10,14},{6,10},{2,6},{1,3},{5,1},... | collective-permute-start | bytes 786440 | tf_op jit(solution)/shard_map/ppermute | solution.py:65
  (43 other events, 276.9 us)

commit v5 on v4

--- a/solution.py
+++ b/solution.py
@@ -80,8 +80,7 @@
         a = b = x
         for s in range(1, max(half, len(exchange)) + 1):
             if s == half:
-                a, b, aside = lax.optimization_barrier((a[:h], b[h:], aside))
-                aside = lax.all_to_all(aside, "tensor", 0, 0, tiled=True)
+                a, b = a[:h], b[h:]
             if s <= half:
                 a, b = self.right(a), self.left(b)
             if s == 1:
@@ -101,7 +100,9 @@
                 give = keep.astype(bf16)
             if s <= half:
                 ready = ([n - s, s], [a, b]) if s < half else ([half], [a, b])
-        return weigh(*ready, sums), keep, came, aside
+        x, aside, sums = lax.optimization_barrier((ready[1], aside, sums))
+        aside = lax.all_to_all(aside, "tensor", 0, 0, tiled=True)
+        return weigh(ready[0], x, sums), keep, came, aside
 
 
 def split(x):
@@ -338,8 +339,10 @@
         lhs, a, b = lax.optimization_barrier((lhs, a, b))
         a, b = ring.right(a), ring.left(b)
         terms = terms_of(info, [d, n - d] if d > 0 else [0], lhs, weight, depth)
-        if d == max(half - 2, 0) and aside is not None:
+        if d == half - 1 and aside is not None:
             terms, a, b, aside = lax.optimization_barrier((terms, a, b, aside))
+            swap = [(i, (i + 1) % ring.pools) for i in range(ring.pools)]
+            aside = aside, lax.ppermute(aside, "pool", swap)
         else:
             terms, a, b = lax.optimization_barrier((terms, a, b))
         if d > 0:
@@ -1011,9 +1014,7 @@
         flat_pool,
         far_pool,
     )
-    a, b, cache = lax.optimization_barrier((a, b, cache))
-    far_cache = lax.ppermute(cache, "pool", swap)
-    terms, got, far_cache = ring_sum(ring, info, a, b, gated, mamba_out_weight, depth, energy, far_cache)
+    terms, got, (cache, far_cache) = ring_sum(ring, info, a, b, gated, mamba_out_weight, depth, energy, cache)
     first, message = mixer_step(
         info,
         tenant_adapter,

time: 183 us -> 179 us (0.978)
  starting transfers between devices: 57.3 us -> 53.2 us
    ppermute x20, starting transfers between devices: 27.7 us -> 18.4 us  [right(): return lax.ppermute(x, 'tensor', self.cw)]
    ppermute x20, starting transfers between devices: 17 us -> 23.7 us  [left(): return lax.ppermute(x, 'tensor', self.ccw)]
    ppermute x20, waiting for transfers between devices: 11.4 us -> 9.42 us  [left(): return lax.ppermute(x, 'tensor', self.ccw)]
    ppermute x4, starting transfers between devices: 8.58 us -> 6.68 us  [gather(): came = lax.ppermute(give, 'tensor', exchange[s - 1])]
  transfers between devices with their start and end apart: 47 -> 47, of which waited for: 26 -> 22; matrix products, arithmetic and copies ran while one was open for 1% -> 1% of each run, Pallas kernels for 42% -> 45%
where the time goes in v5:
time: 179 us; the launch traced here: 178 us
  Pallas kernels  86 us (48%)
  starting transfers between devices  53.2 us (30%)
  waiting for transfers between devices  33.5 us (19%)
  local copies, waits for them, and re-layouts  1.83 us (1%)
    pallas_call x8, Pallas kernels, terms_of(): pl.pallas_call(term_kernel, grid_spec=pltpu.PrefetchScalarGridSpec(num_sc...  24.7 us
    pallas_call x5, Pallas kernels, in_product(): pl.pallas_call(functools.partial(in_kernel, offsets, count, chunks, acc i...  24.1 us
    ppermute x20, starting transfers between devices, left(): return lax.ppermute(x, 'tensor', self.ccw)  23.7 us
    ppermute x20, waiting for transfers between devices, right(): return lax.ppermute(x, 'tensor', self.cw)  20.2 us
    ppermute x20, starting transfers between devices, right(): return lax.ppermute(x, 'tensor', self.cw)  18.4 us
    pallas_call x5, Pallas kernels, query_step(): pl.pallas_call(functools.partial(query_kernel, offsets, count, accs is No...  15.4 us
    pallas_call x1, Pallas kernels, state_pass(): pl.pallas_call(functools.partial(state_kernel, slots=slots, half=half), g...  10.1 us
    ppermute x20, waiting for transfers between devices, left(): return lax.ppermute(x, 'tensor', self.ccw)  9.42 us
  transfers between devices with their start and end apart: 47, of which 22 were waited for; matrix products, arithmetic and copies ran while one was open for 1% of the time, Pallas kernels for 45%

profile of v5, /device:TPU:0, one launch (start us, length us, event | category | flops | bytes accessed | tf_op | source)
XLA Modules:
  0.0 177.6 jit_solution(13146092711488985883)
XLA Ops:
  5.5 3.8 %in_product.5.refs_3_ = f32[256,1024]{1,0:T(8,128)S(1)} custom-call(s32[18]{0:T(128)S(1)} %dynamic-slice_bitcast_fusion.info, bf16[128,1024]{1,0:T(8,128)(2,1)S(1)} %bitcast.20, bf16[8192,2,1024]{2,1,0:T(2,128)(2,1)} %refs_2_.11), custom_call_target="tpu_custom_call" | custom-call | flops 1073741824 | bytes 8388608 | tf_op jit(solution)/shard_map/in_product/pallas_call | solution.py:205
  18.9 5.5 %in_product.6.refs_3_ = f32[256,1024]{1,0:T(8,128)S(1)} custom-call(s32[18]{0:T(128)S(1)} %dynamic-slice_bitcast_fusion.info, bf16[128,1024]{1,0:T(8,128)(2,1)S(1)} %collective-permute-done.refs_0_, bf16[128,1024]{1,0:T(8,128)(2,1)S(1)} %collective-permute-done.1.refs_1_, bf16[8192,2,1024]{2,1,0:T(2,128)(2,1)} %refs_2_.11, ...), custom_call_target="tpu_custom_call", output_to_operand_aliasing={{}: (4, {})} | custom-call | flops 2147483648 | bytes 16777216 | tf_op jit(solution)/shard_map/in_product/pallas_call | solution.py:205
  27.2 2.7 %collective-permute-start.8 = (bf16[64,640]{1,0:T(8,128)(2,1)S(1)}, bf16[64,640]{1,0:T(8,128)(2,1)S(1)}, u32[]{:S(2)}, u32[]{:S(2)}) collective-permute-start(bf16[64,640]{1,0:T(8,128)(2,1)S(1)} %fusion.3), channel_id=1, source_target_pairs={{0,8},{2,10},{4,12},{6,14},{8,0},{10,2},{12,4},{14,6},{1,9},{3,11}... | collective-permute-start | bytes 245768 | tf_op jit(solution)/shard_map/ppermute | solution.py:91
  29.9 5.5 %in_product.7.refs_3_ = f32[256,1024]{1,0:T(8,128)S(1)} custom-call(s32[18]{0:T(128)S(1)} %dynamic-slice_bitcast_fusion.info, bf16[128,1024]{1,0:T(8,128)(2,1)S(1)} %collective-permute-done.3.refs_0_, bf16[128,1024]{1,0:T(8,128)(2,1)S(1)} %collective-permute-done.4.refs_1_, bf16[8192,2,1024]{2,1,0:T(2,128)(2,1)} %refs_2_.11, ...), custom_call_target="tpu_custom_call", output_to_operand_aliasing={{}: (4, {})} | custom-call | flops 2147483648 | bytes 16777216 | tf_op jit(solution)/shard_map/in_product/pallas_call | solution.py:205
  39.6 5.5 %in_product.8.refs_3_ = f32[256,1024]{1,0:T(8,128)S(1)} custom-call(s32[18]{0:T(128)S(1)} %dynamic-slice_bitcast_fusion.info, bf16[128,1024]{1,0:T(8,128)(2,1)S(1)} %collective-permute-done.6.refs_0_, bf16[128,1024]{1,0:T(8,128)(2,1)S(1)} %collective-permute-done.7.refs_1_, bf16[8192,2,1024]{2,1,0:T(2,128)(2,1)} %refs_2_.11, ...), custom_call_target="tpu_custom_call", output_to_operand_aliasing={{}: (4, {})} | custom-call | flops 2147483648 | bytes 16777216 | tf_op jit(solution)/shard_map/in_product/pallas_call | solution.py:205
  45.1 4.0 %all-to-all-start = ((bf16[8,8,16,256]{3,2,1,0:T(8,128)(2,1)}), bf16[8,8,16,256]{3,2,1,0:T(8,128)(2,1)S(1)}, u32[]{:S(2)}, u32[]{:S(2)}) async-start(bf16[8,8,16,256]{3,2,1,0:T(8,128)(2,1)} %pick_heads.1), calls=%async_computation | async-start | bytes 1048576 | tf_op jit(solution)/shard_map/all_to_all | solution.py:104
  49.2 3.9 %in_product.9.x_ref.z_ref = f32[256,1024]{1,0:T(8,128)S(1)} custom-call(s32[18]{0:T(128)S(1)} %dynamic-slice_bitcast_fusion.info, bf16[64,1024]{1,0:T(8,128)(2,1)S(1)} %collective-permute-done.9.refs_0_, bf16[64,1024]{1,0:T(8,128)(2,1)S(1)} %collective-permute-done.10.refs_1_, bf16[8192,2,1024]{2,1,0:T(2,128)(2,1)} %refs_2_.11, ...), custom_call_target="tpu_custom_call", output_to_operand_aliasing={{}: (4, {})} | custom-call | flops 1073741824 | bytes 8388608 | tf_op jit(solution)/shard_map/in_product/pallas_call | solution.py:205
  53.2 10.1 %state_pass.1 = (bf16[128,1024]{1,0:T(8,128)(2,1)S(1)}, f32[128,1]{1,0:T(8,128)S(1)}, f32[4,1024,256]{2,1,0:T(8,128)}, bf16[64,1152]{1,0:T(8,128)(2,1)S(1)}, bf16[64,1152]{1,0:T(8,128)(2,1)S(1)}) custom-call(s32[4]{0:T(128)S(1)} %copy-done.10, s32[18]{0:T(128)S(1)} %dynamic-slice_bitcast_fusion.info, f32[256,1024]{1,0:T(8,128)S(1)} %in_product.9.x_ref.z_ref, ...), custom_call_target="tpu_custom_call" | custom-call | flops 201326592 | bytes 10485760 | tf_op jit(solution)/shard_map/state_pass/pallas_call | solution.py:711
  65.5 3.3 %terms.8.refs_1_ = f32[256,1024]{1,0:T(8,128)S(1)} custom-call(s32[18]{0:T(128)S(1)} %dynamic-slice_bitcast_fusion.info, bf16[128,1024]{1,0:T(8,128)(2,1)S(1)} %get-tuple-element.188.lhs_ref, bf16[1024,8192]{1,0:T(8,128)(2,1)} %w_ref.16), custom_call_target="tpu_custom_call" | custom-call | flops 536870912 | bytes 4194304 | tf_op jit(solution)/shard_map/terms/pallas_call | solution.py:295
  74.5 3.2 %terms.9.refs_1_ = f32[256,1024]{1,0:T(8,128)S(1)} custom-call(s32[18]{0:T(128)S(1)} %dynamic-slice_bitcast_fusion.info, bf16[128,1024]{1,0:T(8,128)(2,1)S(1)} %get-tuple-element.188.lhs_ref, bf16[1024,8192]{1,0:T(8,128)(2,1)} %w_ref.16), custom_call_target="tpu_custom_call" | custom-call | flops 536870912 | bytes 4194304 | tf_op jit(solution)/shard_map/terms/pallas_call | solution.py:295
  77.7 3.7 %collective-permute-done.15.refs_2_ = bf16[128,1152]{1,0:T(8,128)(2,1)S(1)} collective-permute-done((bf16[128,1152]{1,0:T(8,128)(2,1)S(1)}, bf16[128,1152]{1,0:T(8,128)(2,1)S(1)}, u32[]{:S(2)}, u32[]{:S(2)}) %collective-permute-start.15) | collective-permute-done | bytes 294944 | tf_op jit(solution)/shard_map/ppermute | solution.py:62
  85.1 3.3 %terms.10.refs_1_ = f32[256,1024]{1,0:T(8,128)S(1)} custom-call(s32[18]{0:T(128)S(1)} %dynamic-slice_bitcast_fusion.info, bf16[128,1024]{1,0:T(8,128)(2,1)S(1)} %get-tuple-element.188.lhs_ref, bf16[1024,8192]{1,0:T(8,128)(2,1)} %w_ref.16), custom_call_target="tpu_custom_call" | custom-call | flops 536870912 | bytes 4194304 | tf_op jit(solution)/shard_map/terms/pallas_call | solution.py:295
  88.3 2.7 %collective-permute-done.17.refs_2_ = bf16[128,1152]{1,0:T(8,128)(2,1)S(1)} collective-permute-done((bf16[128,1152]{1,0:T(8,128)(2,1)S(1)}, bf16[128,1152]{1,0:T(8,128)(2,1)S(1)}, u32[]{:S(2)}, u32[]{:S(2)}) %collective-permute-start.17) | collective-permute-done | bytes 294944 | tf_op jit(solution)/shard_map/ppermute | solution.py:62
  97.3 3.4 %collective-permute-done.19.refs_0_ = bf16[128,1152]{1,0:T(8,128)(2,1)S(1)} collective-permute-done((bf16[128,1152]{1,0:T(8,128)(2,1)S(1)}, bf16[128,1152]{1,0:T(8,128)(2,1)S(1)}, u32[]{:S(2)}, u32[]{:S(2)}) %collective-permute-start.19) | collective-permute-done | bytes 294944 | tf_op jit(solution)/shard_map/ppermute | solution.py:62
  115.8 3.2 %query_step.6 = (f32[128,1024]{1,0:T(8,128)S(1)}, f32[128,128]{1,0:T(8,128)S(1)}) custom-call(s32[18]{0:T(128)S(1)} %dynamic-slice_bitcast_fusion.info, bf16[128,1152]{1,0:T(8,128)(2,1)S(1)} %collective-permute-done.21.refs_0_, bf16[128,1152]{1,0:T(8,128)(2,1)S(1)} %collective-permute-done.22.refs_1_, ...), custom_call_target="tpu_custom_call", output_to_operand_aliasing={{0}: (4, {}), {1}: (5, {})} | custom-call | flops 536870912 | bytes 4194304 | tf_op jit(solution)/shard_map/query_step/pallas_call | solution.py:476
  124.0 3.3 %query_step.7 = (f32[128,1024]{1,0:T(8,128)S(1)}, f32[128,128]{1,0:T(8,128)S(1)}) custom-call(s32[18]{0:T(128)S(1)} %dynamic-slice_bitcast_fusion.info, bf16[128,1152]{1,0:T(8,128)(2,1)S(1)} %collective-permute-done.25.refs_0_, bf16[128,1152]{1,0:T(8,128)(2,1)S(1)} %collective-permute-done.26.refs_1_, ...), custom_call_target="tpu_custom_call", output_to_operand_aliasing={{0}: (4, {}), {1}: (5, {})} | custom-call | flops 536870912 | bytes 4194304 | tf_op jit(solution)/shard_map/query_step/pallas_call | solution.py:476
  127.3 2.6 %collective-permute-done.31.refs_0_ = bf16[128,256]{1,0:T(8,128)(2,1)S(1)} collective-permute-done((bf16[128,256]{1,0:T(8,128)(2,1)S(1)}, bf16[128,256]{1,0:T(8,128)(2,1)S(1)}, u32[]{:S(2)}, u32[]{:S(2)}) %collective-permute-start.31) | collective-permute-done | bytes 65568 | tf_op jit(solution)/shard_map/ppermute | solution.py:62
  135.3 3.3 %query_step.8 = (f32[128,1024]{1,0:T(8,128)S(1)}, f32[128,128]{1,0:T(8,128)S(1)}) custom-call(s32[18]{0:T(128)S(1)} %dynamic-slice_bitcast_fusion.info, bf16[128,1152]{1,0:T(8,128)(2,1)S(1)} %collective-permute-done.29.refs_0_, bf16[128,1152]{1,0:T(8,128)(2,1)S(1)} %collective-permute-done.30.refs_1_, ...), custom_call_target="tpu_custom_call", output_to_operand_aliasing={{0}: (4, {}), {1}: (5, {})} | custom-call | flops 536870912 | bytes 4194304 | tf_op jit(solution)/shard_map/query_step/pallas_call | solution.py:476
  138.7 3.1 %query_step.9 = (f32[128,1024]{1,0:T(8,128)S(1)}, f32[128,128]{1,0:T(8,128)S(1)}) custom-call(s32[18]{0:T(128)S(1)} %dynamic-slice_bitcast_fusion.info, bf16[64,1152]{1,0:T(8,128)(2,1)S(1)} %collective-permute-done.33.refs_0_, bf16[64,1152]{1,0:T(8,128)(2,1)S(1)} %collective-permute-done.34.refs_1_, ...), custom_call_target="tpu_custom_call", output_to_operand_aliasing={{0}: (4, {}), {1}: (5, {})} | custom-call | flops 268435456 | bytes 2097152 | tf_op jit(solution)/shard_map/query_step/pallas_call | solution.py:476
  141.8 4.8 %attend.1 = (bf16[128,1024]{1,0:T(8,128)(2,1)S(1)}, bf16[64,1024]{1,0:T(8,128)(2,1)S(1)}, bf16[64,1024]{1,0:T(8,128)(2,1)S(1)}) custom-call(s32[4,8]{1,0:T(4,128)S(1)} %copy-done.9, s32[4]{0:T(128)S(1)} %copy-done.14, s32[4]{0:T(128)S(1)} %copy-done.8, s32[18]{0:T(128)S(1)} %dynamic-slice_bitcast_fusion.info, f32[128,1024]{1,0:T(8,128)S(1)} %get-tuple-element.233.q_ref, ...), custom_call_target="tpu_custom_call" | custom-call | flops 150994944 | bytes 2883584 | tf_op jit(solution)/shard_map/attend/pallas_call | solution.py:847
  148.6 3.3 %terms.12.refs_0_ = f32[256,1024]{1,0:T(8,128)S(1)} custom-call(s32[18]{0:T(128)S(1)} %dynamic-slice_bitcast_fusion.info, bf16[128,1024]{1,0:T(8,128)(2,1)S(1)} %get-tuple-element.262.lhs_ref, bf16[1024,8192]{1,0:T(8,128)(2,1)} %w_ref.21), custom_call_target="tpu_custom_call" | custom-call | flops 536870912 | bytes 4194304 | tf_op jit(solution)/shard_map/terms/pallas_call | solution.py:295
  154.4 3.2 %terms.13.refs_0_ = f32[256,1024]{1,0:T(8,128)S(1)} custom-call(s32[18]{0:T(128)S(1)} %dynamic-slice_bitcast_fusion.info, bf16[128,1024]{1,0:T(8,128)(2,1)S(1)} %get-tuple-element.262.lhs_ref, bf16[1024,8192]{1,0:T(8,128)(2,1)} %w_ref.21), custom_call_target="tpu_custom_call" | custom-call | flops 536870912 | bytes 4194304 | tf_op jit(solution)/shard_map/terms/pallas_call | solution.py:295
  162.0 3.3 %terms.14.refs_0_ = f32[256,1024]{1,0:T(8,128)S(1)} custom-call(s32[18]{0:T(128)S(1)} %dynamic-slice_bitcast_fusion.info, bf16[128,1024]{1,0:T(8,128)(2,1)S(1)} %get-tuple-element.262.lhs_ref, bf16[1024,8192]{1,0:T(8,128)(2,1)} %w_ref.21), custom_call_target="tpu_custom_call" | custom-call | flops 536870912 | bytes 4194304 | tf_op jit(solution)/shard_map/terms/pallas_call | solution.py:295
  165.3 2.9 %collective-permute-done.42.refs_1_ = bf16[128,1024]{1,0:T(8,128)(2,1)S(1)} collective-permute-done((bf16[128,1024]{1,0:T(8,128)(2,1)S(1)}, bf16[128,1024]{1,0:T(8,128)(2,1)S(1)}, u32[]{:S(2)}, u32[]{:S(2)}) %collective-permute-start.42) | collective-permute-done | bytes 262176 | tf_op jit(solution)/shard_map/ppermute | solution.py:62
  (157 shorter events, 82.9 us)
Async XLA Ops:
  0.6 52.5 %collective-permute-start.12 = (f32[6,1024,256]{2,1,0:T(8,128)}, f32[6,1024,256]{2,1,0:T(8,128)}, u32[]{:S(2)}, u32[]{:S(2)}) collective-permute-start(f32[6,1024,256]{2,1,0:T(8,128)} %bitcast.30), channel_id=1, source_target_pairs={{0,1},{1,0},{2,3},{3,2},{4,5},{5,4},{6,7},{7,6},{8,9},{9,8},{10,11... | collective-permute-start | bytes 18874376 | tf_op jit(solution)/shard_map/ppermute | solution.py:988
  1.1 13.7 %collective-permute-start.1 = (bf16[128,1024]{1,0:T(8,128)(2,1)}, bf16[128,1024]{1,0:T(8,128)(2,1)S(1)}, u32[]{:S(2)}, u32[]{:S(2)}) collective-permute-start(bf16[128,1024]{1,0:T(8,128)(2,1)} %bitcast.18), channel_id=1, source_target_pairs={{0,2},{4,0},{8,4},{12,8},{14,12},{10,14},{6,10},{2,6},{1,3},{5,1},... | collective-permute-start | bytes 786440 | tf_op jit(solution)/shard_map/ppermute | solution.py:65
  3.7 11.1 %collective-permute-start = (bf16[128,1024]{1,0:T(8,128)(2,1)}, bf16[128,1024]{1,0:T(8,128)(2,1)S(1)}, u32[]{:S(2)}, u32[]{:S(2)}) collective-permute-start(bf16[128,1024]{1,0:T(8,128)(2,1)} %bitcast.19), channel_id=1, source_target_pairs={{0,4},{4,8},{8,12},{12,14},{14,10},{10,6},{6,2},{2,0},{1,5},{5,9},... | collective-permute-start | bytes 786440 | tf_op jit(solution)/shard_map/ppermute | solution.py:62
  14.8 10.4 %collective-permute-start.3 = (bf16[128,1024]{1,0:T(8,128)(2,1)S(1)}, bf16[128,1024]{1,0:T(8,128)(2,1)S(1)}, u32[]{:S(2)}, u32[]{:S(2)}) collective-permute-start(bf16[128,1024]{1,0:T(8,128)(2,1)S(1)} %collective-permute-done.refs_0_), channel_id=1, source_target_pairs={{0,4},{4,8},{8,12},{12,14},{14,10},{10,6},{6,2},{2,0},{1,5},{5,9},... | collective-permute-start | bytes 786440 | tf_op jit(solution)/shard_map/ppermute | solution.py:62
  16.7 8.4 %collective-permute-start.4 = (bf16[128,1024]{1,0:T(8,128)(2,1)S(1)}, bf16[128,1024]{1,0:T(8,128)(2,1)S(1)}, u32[]{:S(2)}, u32[]{:S(2)}) collective-permute-start(bf16[128,1024]{1,0:T(8,128)(2,1)S(1)} %collective-permute-done.1.refs_1_), channel_id=1, source_target_pairs={{0,2},{4,0},{8,4},{12,8},{14,12},{10,14},{6,10},{2,6},{1,3},{5,1},... | collective-permute-start | bytes 786440 | tf_op jit(solution)/shard_map/ppermute | solution.py:65
  16.9 8.3 %collective-permute-start.5 = (bf16[64,640]{1,0:T(8,128)(2,1)S(1)}, bf16[64,640]{1,0:T(8,128)(2,1)S(1)}, u32[]{:S(2)}, u32[]{:S(2)}) collective-permute-start(bf16[64,640]{1,0:T(8,128)(2,1)S(1)} %fusion.2), channel_id=1, source_target_pairs={{0,4},{2,6},{4,0},{6,2},{8,12},{10,14},{12,8},{14,10},{1,5},{3,7},... | collective-permute-start | bytes 245768 | tf_op jit(solution)/shard_map/ppermute | solution.py:91
  25.2 12.1 %collective-permute-start.6 = (bf16[128,1024]{1,0:T(8,128)(2,1)S(1)}, bf16[128,1024]{1,0:T(8,128)(2,1)S(1)}, u32[]{:S(2)}, u32[]{:S(2)}) collective-permute-start(bf16[128,1024]{1,0:T(8,128)(2,1)S(1)} %collective-permute-done.3.refs_0_), channel_id=1, source_target_pairs={{0,4},{4,8},{8,12},{12,14},{14,10},{10,6},{6,2},{2,0},{1,5},{5,9},... | collective-permute-start | bytes 786440 | tf_op jit(solution)/shard_map/ppermute | solution.py:62
  25.4 11.8 %collective-permute-start.7 = (bf16[128,1024]{1,0:T(8,128)(2,1)S(1)}, bf16[128,1024]{1,0:T(8,128)(2,1)S(1)}, u32[]{:S(2)}, u32[]{:S(2)}) collective-permute-start(bf16[128,1024]{1,0:T(8,128)(2,1)S(1)} %collective-permute-done.4.refs_1_), channel_id=1, source_target_pairs={{0,2},{4,0},{8,4},{12,8},{14,12},{10,14},{6,10},{2,6},{1,3},{5,1},... | collective-permute-start | bytes 786440 | tf_op jit(solution)/shard_map/ppermute | solution.py:65
  27.2 10.0 %collective-permute-start.8 = (bf16[64,640]{1,0:T(8,128)(2,1)S(1)}, bf16[64,640]{1,0:T(8,128)(2,1)S(1)}, u32[]{:S(2)}, u32[]{:S(2)}) collective-permute-start(bf16[64,640]{1,0:T(8,128)(2,1)S(1)} %fusion.3), channel_id=1, source_target_pairs={{0,8},{2,10},{4,12},{6,14},{8,0},{10,2},{12,4},{14,6},{1,9},{3,11}... | collective-permute-start | bytes 245768 | tf_op jit(solution)/shard_map/ppermute | solution.py:91
  45.1 23.7 %all-to-all-start = ((bf16[8,8,16,256]{3,2,1,0:T(8,128)(2,1)}), bf16[8,8,16,256]{3,2,1,0:T(8,128)(2,1)S(1)}, u32[]{:S(2)}, u32[]{:S(2)}) async-start(bf16[8,8,16,256]{3,2,1,0:T(8,128)(2,1)} %pick_heads.1), calls=%async_computation | async-start | bytes 1048576 | tf_op jit(solution)/shard_map/all_to_all | solution.py:104
  72.4 9.1 %collective-permute-start.15 = (bf16[128,1152]{1,0:T(8,128)(2,1)S(1)}, bf16[128,1152]{1,0:T(8,128)(2,1)S(1)}, u32[]{:S(2)}, u32[]{:S(2)}) collective-permute-start(bf16[128,1152]{1,0:T(8,128)(2,1)S(1)} %get-tuple-element.173), channel_id=1, source_target_pairs={{0,4},{4,8},{8,12},{12,14},{14,10},{10,6},{6,2},{2,0},{1,5},{5,9},... | collective-permute-start | bytes 884744 | tf_op jit(solution)/shard_map/ppermute | solution.py:62
  73.9 8.8 %collective-permute-start.16 = (bf16[128,1152]{1,0:T(8,128)(2,1)S(1)}, bf16[128,1152]{1,0:T(8,128)(2,1)S(1)}, u32[]{:S(2)}, u32[]{:S(2)}) collective-permute-start(bf16[128,1152]{1,0:T(8,128)(2,1)S(1)} %get-tuple-element.174), channel_id=1, source_target_pairs={{0,2},{4,0},{8,4},{12,8},{14,12},{10,14},{6,10},{2,6},{1,3},{5,1},... | collective-permute-start | bytes 884744 | tf_op jit(solution)/shard_map/ppermute | solution.py:65
  83.0 8.0 %collective-permute-start.17 = (bf16[128,1152]{1,0:T(8,128)(2,1)S(1)}, bf16[128,1152]{1,0:T(8,128)(2,1)S(1)}, u32[]{:S(2)}, u32[]{:S(2)}) collective-permute-start(bf16[128,1152]{1,0:T(8,128)(2,1)S(1)} %get-tuple-element.181), channel_id=1, source_target_pairs={{0,4},{4,8},{8,12},{12,14},{14,10},{10,6},{6,2},{2,0},{1,5},{5,9},... | collective-permute-start | bytes 884744 | tf_op jit(solution)/shard_map/ppermute | solution.py:62
  92.6 8.0 %collective-permute-start.19 = (bf16[128,1152]{1,0:T(8,128)(2,1)S(1)}, bf16[128,1152]{1,0:T(8,128)(2,1)S(1)}, u32[]{:S(2)}, u32[]{:S(2)}) collective-permute-start(bf16[128,1152]{1,0:T(8,128)(2,1)S(1)} %get-tuple-element.189), channel_id=1, source_target_pairs={{0,4},{4,8},{8,12},{12,14},{14,10},{10,6},{6,2},{2,0},{1,5},{5,9},... | collective-permute-start | bytes 884744 | tf_op jit(solution)/shard_map/ppermute | solution.py:62
  101.7 9.3 %collective-permute-start.22 = (bf16[128,1152]{1,0:T(8,128)(2,1)S(1)}, bf16[128,1152]{1,0:T(8,128)(2,1)S(1)}, u32[]{:S(2)}, u32[]{:S(2)}) collective-permute-start(bf16[128,1152]{1,0:T(8,128)(2,1)S(1)} %get-tuple-element.194.refs_0_), channel_id=1, source_target_pairs={{0,2},{4,0},{8,4},{12,8},{14,12},{10,14},{6,10},{2,6},{1,3},{5,1},... | collective-permute-start | bytes 884744 | tf_op jit(solution)/shard_map/ppermute | solution.py:65
  102.9 8.2 %collective-permute-start.21 = (bf16[128,1152]{1,0:T(8,128)(2,1)S(1)}, bf16[128,1152]{1,0:T(8,128)(2,1)S(1)}, u32[]{:S(2)}, u32[]{:S(2)}) collective-permute-start(bf16[128,1152]{1,0:T(8,128)(2,1)S(1)} %get-tuple-element.194.refs_0_), channel_id=1, source_target_pairs={{0,4},{4,8},{8,12},{12,14},{14,10},{10,6},{6,2},{2,0},{1,5},{5,9},... | collective-permute-start | bytes 884744 | tf_op jit(solution)/shard_map/ppermute | solution.py:62
  111.1 8.3 %collective-permute-start.25 = (bf16[128,1152]{1,0:T(8,128)(2,1)S(1)}, bf16[128,1152]{1,0:T(8,128)(2,1)S(1)}, u32[]{:S(2)}, u32[]{:S(2)}) collective-permute-start(bf16[128,1152]{1,0:T(8,128)(2,1)S(1)} %collective-permute-done.21.refs_0_), channel_id=1, source_target_pairs={{0,4},{4,8},{8,12},{12,14},{14,10},{10,6},{6,2},{2,0},{1,5},{5,9},... | collective-permute-start | bytes 884744 | tf_op jit(solution)/shard_map/ppermute | solution.py:62
  115.8 26.0 %collective-permute-start.37 = (bf16[64,16,256]{2,1,0:T(8,128)(2,1)S(1)}, bf16[64,16,256]{2,1,0:T(8,128)(2,1)S(1)}, u32[]{:S(2)}, u32[]{:S(2)}) collective-permute-start(bf16[64,16,256]{2,1,0:T(8,128)(2,1)S(1)} %bitcast.23), channel_id=1, source_target_pairs={{0,1},{1,0},{2,3},{3,2},{4,5},{5,4},{6,7},{7,6},{8,9},{9,8},{10,11... | collective-permute-start | bytes 1572872 | tf_op jit(solution)/shard_map/ppermute | solution.py:345
  119.3 11.2 %collective-permute-start.29 = (bf16[128,1152]{1,0:T(8,128)(2,1)S(1)}, bf16[128,1152]{1,0:T(8,128)(2,1)S(1)}, u32[]{:S(2)}, u32[]{:S(2)}) collective-permute-start(bf16[128,1152]{1,0:T(8,128)(2,1)S(1)} %collective-permute-done.25.refs_0_), channel_id=1, source_target_pairs={{0,4},{4,8},{8,12},{12,14},{14,10},{10,6},{6,2},{2,0},{1,5},{5,9},... | collective-permute-start | bytes 884744 | tf_op jit(solution)/shard_map/ppermute | solution.py:62
  120.0 10.5 %collective-permute-start.30 = (bf16[128,1152]{1,0:T(8,128)(2,1)S(1)}, bf16[128,1152]{1,0:T(8,128)(2,1)S(1)}, u32[]{:S(2)}, u32[]{:S(2)}) collective-permute-start(bf16[128,1152]{1,0:T(8,128)(2,1)S(1)} %collective-permute-done.26.refs_1_), channel_id=1, source_target_pairs={{0,2},{4,0},{8,4},{12,8},{14,12},{10,14},{6,10},{2,6},{1,3},{5,1},... | collective-permute-start | bytes 884744 | tf_op jit(solution)/shard_map/ppermute | solution.py:65
  122.0 8.0 %collective-permute-start.31 = (bf16[128,256]{1,0:T(8,128)(2,1)S(1)}, bf16[128,256]{1,0:T(8,128)(2,1)S(1)}, u32[]{:S(2)}, u32[]{:S(2)}) collective-permute-start(bf16[128,256]{1,0:T(8,128)(2,1)S(1)} %get-tuple-element.213), channel_id=1, source_target_pairs={{0,4},{4,8},{8,12},{12,14},{14,10},{10,6},{6,2},{2,0},{1,5},{5,9},... | collective-permute-start | bytes 196616 | tf_op jit(solution)/shard_map/ppermute | solution.py:62
  130.6 8.0 %collective-permute-start.33 = (bf16[64,1152]{1,0:T(8,128)(2,1)S(1)}, bf16[64,1152]{1,0:T(8,128)(2,1)S(1)}, u32[]{:S(2)}, u32[]{:S(2)}) collective-permute-start(bf16[64,1152]{1,0:T(8,128)(2,1)S(1)} %slice.18), channel_id=1, source_target_pairs={{0,4},{4,8},{8,12},{12,14},{14,10},{10,6},{6,2},{2,0},{1,5},{5,9},... | collective-permute-start | bytes 442376 | tf_op jit(solution)/shard_map/ppermute | solution.py:62
  160.0 8.2 %collective-permute-start.42 = (bf16[128,1024]{1,0:T(8,128)(2,1)S(1)}, bf16[128,1024]{1,0:T(8,128)(2,1)S(1)}, u32[]{:S(2)}, u32[]{:S(2)}) collective-permute-start(bf16[128,1024]{1,0:T(8,128)(2,1)S(1)} %get-tuple-element.255), channel_id=1, source_target_pairs={{0,4},{4,8},{8,12},{12,14},{14,10},{10,6},{6,2},{2,0},{1,5},{5,9},... | collective-permute-start | bytes 786440 | tf_op jit(solution)/shard_map/ppermute | solution.py:62
  160.7 8.6 %collective-permute-start.43 = (bf16[128,1024]{1,0:T(8,128)(2,1)S(1)}, bf16[128,1024]{1,0:T(8,128)(2,1)S(1)}, u32[]{:S(2)}, u32[]{:S(2)}) collective-permute-start(bf16[128,1024]{1,0:T(8,128)(2,1)S(1)} %get-tuple-element.256), channel_id=1, source_target_pairs={{0,2},{4,0},{8,4},{12,8},{14,12},{10,14},{6,10},{2,6},{1,3},{5,1},... | collective-permute-start | bytes 786440 | tf_op jit(solution)/shard_map/ppermute | solution.py:65
  (43 other events, 267.9 us)

commit v6 on v5

--- a/solution.py
+++ b/solution.py
@@ -187,7 +187,7 @@
     count = len(blocks)
     rows = sum(b.shape[0] for b in blocks) // len(offsets)
     cols = weight.shape[2]
-    chunks = 2 if depth % 512 == 0 else 1
+    chunks = 4 if depth % 1024 == 0 else 1
     slots = chunks * len(offsets)
 
     def fixed(shape):

time: 179 us -> 177 us (0.989)
  transfers between devices with their start and end apart: 47 -> 47, of which waited for: 22 -> 22; matrix products, arithmetic and copies ran while one was open for 1% -> 1% of each run, Pallas kernels for 45% -> 44%
where the time goes in v6:
time: 177 us
  Pallas kernels  85 us (48%)
  starting transfers between devices  53.3 us (30%)
  waiting for transfers between devices  34 us (19%)
  local copies, waits for them, and re-layouts  1.83 us (1%)
    pallas_call x8, Pallas kernels, terms_of(): pl.pallas_call(term_kernel, grid_spec=pltpu.PrefetchScalarGridSpec(num_sc...  24.7 us
    pallas_call x5, Pallas kernels, in_product(): pl.pallas_call(functools.partial(in_kernel, offsets, count, chunks, acc i...  23.5 us
    ppermute x20, starting transfers between devices, left(): return lax.ppermute(x, 'tensor', self.ccw)  22 us
    ppermute x20, starting transfers between devices, right(): return lax.ppermute(x, 'tensor', self.cw)  20.1 us
    ppermute x20, waiting for transfers between devices, right(): return lax.ppermute(x, 'tensor', self.cw)  19.8 us
    pallas_call x5, Pallas kernels, query_step(): pl.pallas_call(functools.partial(query_kernel, offsets, count, accs is No...  15.4 us
    ppermute x20, waiting for transfers between devices, left(): return lax.ppermute(x, 'tensor', self.ccw)  10.1 us
    pallas_call x1, Pallas kernels, state_pass(): pl.pallas_call(functools.partial(state_kernel, slots=slots, half=half), g...  9.85 us
  transfers between devices with their start and end apart: 47, of which 22 were waited for; matrix products, arithmetic and copies ran while one was open for 1% of the time, Pallas kernels for 44%

profile of v6, /device:TPU:0, one launch (start us, length us, event | category | flops | bytes accessed | tf_op | source)
XLA Modules:
  0.0 177.2 jit_solution(6484712314225585149)
XLA Ops:
  5.5 3.6 %in_product.5.refs_3_ = f32[256,1024]{1,0:T(8,128)S(1)} custom-call(s32[18]{0:T(128)S(1)} %dynamic-slice_bitcast_fusion.info, bf16[128,1024]{1,0:T(8,128)(2,1)S(1)} %bitcast.20, bf16[8192,2,1024]{2,1,0:T(2,128)(2,1)} %refs_2_.11), custom_call_target="tpu_custom_call" | custom-call | flops 1073741824 | bytes 8388608 | tf_op jit(solution)/shard_map/in_product/pallas_call | solution.py:205
  18.6 5.4 %in_product.6.refs_3_ = f32[256,1024]{1,0:T(8,128)S(1)} custom-call(s32[18]{0:T(128)S(1)} %dynamic-slice_bitcast_fusion.info, bf16[128,1024]{1,0:T(8,128)(2,1)S(1)} %collective-permute-done.refs_0_, bf16[128,1024]{1,0:T(8,128)(2,1)S(1)} %collective-permute-done.1.refs_1_, bf16[8192,2,1024]{2,1,0:T(2,128)(2,1)} %refs_2_.11, ...), custom_call_target="tpu_custom_call", output_to_operand_aliasing={{}: (4, {})} | custom-call | flops 2147483648 | bytes 16777216 | tf_op jit(solution)/shard_map/in_product/pallas_call | solution.py:205
  27.0 2.6 %collective-permute-start.8 = (bf16[64,640]{1,0:T(8,128)(2,1)S(1)}, bf16[64,640]{1,0:T(8,128)(2,1)S(1)}, u32[]{:S(2)}, u32[]{:S(2)}) collective-permute-start(bf16[64,640]{1,0:T(8,128)(2,1)S(1)} %fusion.3), channel_id=1, source_target_pairs={{0,8},{2,10},{4,12},{6,14},{8,0},{10,2},{12,4},{14,6},{1,9},{3,11}... | collective-permute-start | bytes 245768 | tf_op jit(solution)/shard_map/ppermute | solution.py:91
  29.7 5.4 %in_product.7.refs_3_ = f32[256,1024]{1,0:T(8,128)S(1)} custom-call(s32[18]{0:T(128)S(1)} %dynamic-slice_bitcast_fusion.info, bf16[128,1024]{1,0:T(8,128)(2,1)S(1)} %collective-permute-done.3.refs_0_, bf16[128,1024]{1,0:T(8,128)(2,1)S(1)} %collective-permute-done.4.refs_1_, bf16[8192,2,1024]{2,1,0:T(2,128)(2,1)} %refs_2_.11, ...), custom_call_target="tpu_custom_call", output_to_operand_aliasing={{}: (4, {})} | custom-call | flops 2147483648 | bytes 16777216 | tf_op jit(solution)/shard_map/in_product/pallas_call | solution.py:205
  39.4 5.4 %in_product.8.refs_3_ = f32[256,1024]{1,0:T(8,128)S(1)} custom-call(s32[18]{0:T(128)S(1)} %dynamic-slice_bitcast_fusion.info, bf16[128,1024]{1,0:T(8,128)(2,1)S(1)} %collective-permute-done.6.refs_0_, bf16[128,1024]{1,0:T(8,128)(2,1)S(1)} %collective-permute-done.7.refs_1_, bf16[8192,2,1024]{2,1,0:T(2,128)(2,1)} %refs_2_.11, ...), custom_call_target="tpu_custom_call", output_to_operand_aliasing={{}: (4, {})} | custom-call | flops 2147483648 | bytes 16777216 | tf_op jit(solution)/shard_map/in_product/pallas_call | solution.py:205
  44.8 4.0 %all-to-all-start = ((bf16[8,8,16,256]{3,2,1,0:T(8,128)(2,1)}), bf16[8,8,16,256]{3,2,1,0:T(8,128)(2,1)S(1)}, u32[]{:S(2)}, u32[]{:S(2)}) async-start(bf16[8,8,16,256]{3,2,1,0:T(8,128)(2,1)} %pick_heads.1), calls=%async_computation | async-start | bytes 1048576 | tf_op jit(solution)/shard_map/all_to_all | solution.py:104
  49.0 3.7 %in_product.9.x_ref.z_ref = f32[256,1024]{1,0:T(8,128)S(1)} custom-call(s32[18]{0:T(128)S(1)} %dynamic-slice_bitcast_fusion.info, bf16[64,1024]{1,0:T(8,128)(2,1)S(1)} %collective-permute-done.9.refs_0_, bf16[64,1024]{1,0:T(8,128)(2,1)S(1)} %collective-permute-done.10.refs_1_, bf16[8192,2,1024]{2,1,0:T(2,128)(2,1)} %refs_2_.11, ...), custom_call_target="tpu_custom_call", output_to_operand_aliasing={{}: (4, {})} | custom-call | flops 1073741824 | bytes 8388608 | tf_op jit(solution)/shard_map/in_product/pallas_call | solution.py:205
  52.8 9.8 %state_pass.1 = (bf16[128,1024]{1,0:T(8,128)(2,1)S(1)}, f32[128,1]{1,0:T(8,128)S(1)}, f32[4,1024,256]{2,1,0:T(8,128)}, bf16[64,1152]{1,0:T(8,128)(2,1)S(1)}, bf16[64,1152]{1,0:T(8,128)(2,1)S(1)}) custom-call(s32[4]{0:T(128)S(1)} %copy-done.10, s32[18]{0:T(128)S(1)} %dynamic-slice_bitcast_fusion.info, f32[256,1024]{1,0:T(8,128)S(1)} %in_product.9.x_ref.z_ref, ...), custom_call_target="tpu_custom_call" | custom-call | flops 201326592 | bytes 10485760 | tf_op jit(solution)/shard_map/state_pass/pallas_call | solution.py:711
  64.8 3.2 %terms.8.refs_1_ = f32[256,1024]{1,0:T(8,128)S(1)} custom-call(s32[18]{0:T(128)S(1)} %dynamic-slice_bitcast_fusion.info, bf16[128,1024]{1,0:T(8,128)(2,1)S(1)} %get-tuple-element.188.lhs_ref, bf16[1024,8192]{1,0:T(8,128)(2,1)} %w_ref.16), custom_call_target="tpu_custom_call" | custom-call | flops 536870912 | bytes 4194304 | tf_op jit(solution)/shard_map/terms/pallas_call | solution.py:295
  73.5 3.3 %terms.9.refs_1_ = f32[256,1024]{1,0:T(8,128)S(1)} custom-call(s32[18]{0:T(128)S(1)} %dynamic-slice_bitcast_fusion.info, bf16[128,1024]{1,0:T(8,128)(2,1)S(1)} %get-tuple-element.188.lhs_ref, bf16[1024,8192]{1,0:T(8,128)(2,1)} %w_ref.16), custom_call_target="tpu_custom_call" | custom-call | flops 536870912 | bytes 4194304 | tf_op jit(solution)/shard_map/terms/pallas_call | solution.py:295
  76.8 3.5 %collective-permute-done.15.refs_2_ = bf16[128,1152]{1,0:T(8,128)(2,1)S(1)} collective-permute-done((bf16[128,1152]{1,0:T(8,128)(2,1)S(1)}, bf16[128,1152]{1,0:T(8,128)(2,1)S(1)}, u32[]{:S(2)}, u32[]{:S(2)}) %collective-permute-start.15) | collective-permute-done | bytes 294944 | tf_op jit(solution)/shard_map/ppermute | solution.py:62
  83.9 3.2 %terms.10.refs_1_ = f32[256,1024]{1,0:T(8,128)S(1)} custom-call(s32[18]{0:T(128)S(1)} %dynamic-slice_bitcast_fusion.info, bf16[128,1024]{1,0:T(8,128)(2,1)S(1)} %get-tuple-element.188.lhs_ref, bf16[1024,8192]{1,0:T(8,128)(2,1)} %w_ref.16), custom_call_target="tpu_custom_call" | custom-call | flops 536870912 | bytes 4194304 | tf_op jit(solution)/shard_map/terms/pallas_call | solution.py:295
  95.8 3.2 %collective-permute-done.19.refs_0_ = bf16[128,1152]{1,0:T(8,128)(2,1)S(1)} collective-permute-done((bf16[128,1152]{1,0:T(8,128)(2,1)S(1)}, bf16[128,1152]{1,0:T(8,128)(2,1)S(1)}, u32[]{:S(2)}, u32[]{:S(2)}) %collective-permute-start.19) | collective-permute-done | bytes 294944 | tf_op jit(solution)/shard_map/ppermute | solution.py:62
  113.7 3.2 %query_step.6 = (f32[128,1024]{1,0:T(8,128)S(1)}, f32[128,128]{1,0:T(8,128)S(1)}) custom-call(s32[18]{0:T(128)S(1)} %dynamic-slice_bitcast_fusion.info, bf16[128,1152]{1,0:T(8,128)(2,1)S(1)} %collective-permute-done.21.refs_0_, bf16[128,1152]{1,0:T(8,128)(2,1)S(1)} %collective-permute-done.22.refs_1_, ...), custom_call_target="tpu_custom_call", output_to_operand_aliasing={{0}: (4, {}), {1}: (5, {})} | custom-call | flops 536870912 | bytes 4194304 | tf_op jit(solution)/shard_map/query_step/pallas_call | solution.py:476
  122.0 3.2 %query_step.7 = (f32[128,1024]{1,0:T(8,128)S(1)}, f32[128,128]{1,0:T(8,128)S(1)}) custom-call(s32[18]{0:T(128)S(1)} %dynamic-slice_bitcast_fusion.info, bf16[128,1152]{1,0:T(8,128)(2,1)S(1)} %collective-permute-done.25.refs_0_, bf16[128,1152]{1,0:T(8,128)(2,1)S(1)} %collective-permute-done.26.refs_1_, ...), custom_call_target="tpu_custom_call", output_to_operand_aliasing={{0}: (4, {}), {1}: (5, {})} | custom-call | flops 536870912 | bytes 4194304 | tf_op jit(solution)/shard_map/query_step/pallas_call | solution.py:476
  125.2 2.7 %collective-permute-done.31.refs_0_ = bf16[128,256]{1,0:T(8,128)(2,1)S(1)} collective-permute-done((bf16[128,256]{1,0:T(8,128)(2,1)S(1)}, bf16[128,256]{1,0:T(8,128)(2,1)S(1)}, u32[]{:S(2)}, u32[]{:S(2)}) %collective-permute-start.31) | collective-permute-done | bytes 65568 | tf_op jit(solution)/shard_map/ppermute | solution.py:62
  133.2 3.3 %query_step.8 = (f32[128,1024]{1,0:T(8,128)S(1)}, f32[128,128]{1,0:T(8,128)S(1)}) custom-call(s32[18]{0:T(128)S(1)} %dynamic-slice_bitcast_fusion.info, bf16[128,1152]{1,0:T(8,128)(2,1)S(1)} %collective-permute-done.29.refs_0_, bf16[128,1152]{1,0:T(8,128)(2,1)S(1)} %collective-permute-done.30.refs_1_, ...), custom_call_target="tpu_custom_call", output_to_operand_aliasing={{0}: (4, {}), {1}: (5, {})} | custom-call | flops 536870912 | bytes 4194304 | tf_op jit(solution)/shard_map/query_step/pallas_call | solution.py:476
  136.6 3.1 %query_step.9 = (f32[128,1024]{1,0:T(8,128)S(1)}, f32[128,128]{1,0:T(8,128)S(1)}) custom-call(s32[18]{0:T(128)S(1)} %dynamic-slice_bitcast_fusion.info, bf16[64,1152]{1,0:T(8,128)(2,1)S(1)} %collective-permute-done.33.refs_0_, bf16[64,1152]{1,0:T(8,128)(2,1)S(1)} %collective-permute-done.34.refs_1_, ...), custom_call_target="tpu_custom_call", output_to_operand_aliasing={{0}: (4, {}), {1}: (5, {})} | custom-call | flops 268435456 | bytes 2097152 | tf_op jit(solution)/shard_map/query_step/pallas_call | solution.py:476
  139.7 4.8 %attend.1 = (bf16[128,1024]{1,0:T(8,128)(2,1)S(1)}, bf16[64,1024]{1,0:T(8,128)(2,1)S(1)}, bf16[64,1024]{1,0:T(8,128)(2,1)S(1)}) custom-call(s32[4,8]{1,0:T(4,128)S(1)} %copy-done.9, s32[4]{0:T(128)S(1)} %copy-done.14, s32[4]{0:T(128)S(1)} %copy-done.8, s32[18]{0:T(128)S(1)} %dynamic-slice_bitcast_fusion.info, f32[128,1024]{1,0:T(8,128)S(1)} %get-tuple-element.233.q_ref, ...), custom_call_target="tpu_custom_call" | custom-call | flops 150994944 | bytes 2883584 | tf_op jit(solution)/shard_map/attend/pallas_call | solution.py:847
  146.6 3.3 %terms.12.refs_0_ = f32[256,1024]{1,0:T(8,128)S(1)} custom-call(s32[18]{0:T(128)S(1)} %dynamic-slice_bitcast_fusion.info, bf16[128,1024]{1,0:T(8,128)(2,1)S(1)} %get-tuple-element.262.lhs_ref, bf16[1024,8192]{1,0:T(8,128)(2,1)} %w_ref.21), custom_call_target="tpu_custom_call" | custom-call | flops 536870912 | bytes 4194304 | tf_op jit(solution)/shard_map/terms/pallas_call | solution.py:295
  152.5 3.2 %terms.13.refs_0_ = f32[256,1024]{1,0:T(8,128)S(1)} custom-call(s32[18]{0:T(128)S(1)} %dynamic-slice_bitcast_fusion.info, bf16[128,1024]{1,0:T(8,128)(2,1)S(1)} %get-tuple-element.262.lhs_ref, bf16[1024,8192]{1,0:T(8,128)(2,1)} %w_ref.21), custom_call_target="tpu_custom_call" | custom-call | flops 536870912 | bytes 4194304 | tf_op jit(solution)/shard_map/terms/pallas_call | solution.py:295
  160.5 3.2 %terms.14.refs_0_ = f32[256,1024]{1,0:T(8,128)S(1)} custom-call(s32[18]{0:T(128)S(1)} %dynamic-slice_bitcast_fusion.info, bf16[128,1024]{1,0:T(8,128)(2,1)S(1)} %get-tuple-element.262.lhs_ref, bf16[1024,8192]{1,0:T(8,128)(2,1)} %w_ref.21), custom_call_target="tpu_custom_call" | custom-call | flops 536870912 | bytes 4194304 | tf_op jit(solution)/shard_map/terms/pallas_call | solution.py:295
  163.7 3.1 %collective-permute-done.42.refs_1_ = bf16[128,1024]{1,0:T(8,128)(2,1)S(1)} collective-permute-done((bf16[128,1024]{1,0:T(8,128)(2,1)S(1)}, bf16[128,1024]{1,0:T(8,128)(2,1)S(1)}, u32[]{:S(2)}, u32[]{:S(2)}) %collective-permute-start.42) | collective-permute-done | bytes 262176 | tf_op jit(solution)/shard_map/ppermute | solution.py:62
  170.9 2.6 %terms.15 = f32[128,1024]{1,0:T(8,128)S(1)} custom-call(s32[18]{0:T(128)S(1)} %dynamic-slice_bitcast_fusion.info, bf16[128,1024]{1,0:T(8,128)(2,1)S(1)} %get-tuple-element.262.lhs_ref, bf16[1024,8192]{1,0:T(8,128)(2,1)} %w_ref.21), custom_call_target="tpu_custom_call" | custom-call | flops 268435456 | bytes 2097152 | tf_op jit(solution)/shard_map/terms/pallas_call | solution.py:295
  (157 shorter events, 83.8 us)
Async XLA Ops:
  0.6 52.1 %collective-permute-start.12 = (f32[6,1024,256]{2,1,0:T(8,128)}, f32[6,1024,256]{2,1,0:T(8,128)}, u32[]{:S(2)}, u32[]{:S(2)}) collective-permute-start(f32[6,1024,256]{2,1,0:T(8,128)} %bitcast.30), channel_id=1, source_target_pairs={{0,1},{1,0},{2,3},{3,2},{4,5},{5,4},{6,7},{7,6},{8,9},{9,8},{10,11... | collective-permute-start | bytes 18874376 | tf_op jit(solution)/shard_map/ppermute | solution.py:988
  1.1 13.4 %collective-permute-start.1 = (bf16[128,1024]{1,0:T(8,128)(2,1)}, bf16[128,1024]{1,0:T(8,128)(2,1)S(1)}, u32[]{:S(2)}, u32[]{:S(2)}) collective-permute-start(bf16[128,1024]{1,0:T(8,128)(2,1)} %bitcast.18), channel_id=1, source_target_pairs={{0,2},{4,0},{8,4},{12,8},{14,12},{10,14},{6,10},{2,6},{1,3},{5,1},... | collective-permute-start | bytes 786440 | tf_op jit(solution)/shard_map/ppermute | solution.py:65
  3.7 10.8 %collective-permute-start = (bf16[128,1024]{1,0:T(8,128)(2,1)}, bf16[128,1024]{1,0:T(8,128)(2,1)S(1)}, u32[]{:S(2)}, u32[]{:S(2)}) collective-permute-start(bf16[128,1024]{1,0:T(8,128)(2,1)} %bitcast.19), channel_id=1, source_target_pairs={{0,4},{4,8},{8,12},{12,14},{14,10},{10,6},{6,2},{2,0},{1,5},{5,9},... | collective-permute-start | bytes 786440 | tf_op jit(solution)/shard_map/ppermute | solution.py:62
  14.6 10.4 %collective-permute-start.3 = (bf16[128,1024]{1,0:T(8,128)(2,1)S(1)}, bf16[128,1024]{1,0:T(8,128)(2,1)S(1)}, u32[]{:S(2)}, u32[]{:S(2)}) collective-permute-start(bf16[128,1024]{1,0:T(8,128)(2,1)S(1)} %collective-permute-done.refs_0_), channel_id=1, source_target_pairs={{0,4},{4,8},{8,12},{12,14},{14,10},{10,6},{6,2},{2,0},{1,5},{5,9},... | collective-permute-start | bytes 786440 | tf_op jit(solution)/shard_map/ppermute | solution.py:62
  16.5 8.4 %collective-permute-start.4 = (bf16[128,1024]{1,0:T(8,128)(2,1)S(1)}, bf16[128,1024]{1,0:T(8,128)(2,1)S(1)}, u32[]{:S(2)}, u32[]{:S(2)}) collective-permute-start(bf16[128,1024]{1,0:T(8,128)(2,1)S(1)} %collective-permute-done.1.refs_1_), channel_id=1, source_target_pairs={{0,2},{4,0},{8,4},{12,8},{14,12},{10,14},{6,10},{2,6},{1,3},{5,1},... | collective-permute-start | bytes 786440 | tf_op jit(solution)/shard_map/ppermute | solution.py:65
  16.6 8.3 %collective-permute-start.5 = (bf16[64,640]{1,0:T(8,128)(2,1)S(1)}, bf16[64,640]{1,0:T(8,128)(2,1)S(1)}, u32[]{:S(2)}, u32[]{:S(2)}) collective-permute-start(bf16[64,640]{1,0:T(8,128)(2,1)S(1)} %fusion.2), channel_id=1, source_target_pairs={{0,4},{2,6},{4,0},{6,2},{8,12},{10,14},{12,8},{14,10},{1,5},{3,7},... | collective-permute-start | bytes 245768 | tf_op jit(solution)/shard_map/ppermute | solution.py:91
  25.0 12.1 %collective-permute-start.6 = (bf16[128,1024]{1,0:T(8,128)(2,1)S(1)}, bf16[128,1024]{1,0:T(8,128)(2,1)S(1)}, u32[]{:S(2)}, u32[]{:S(2)}) collective-permute-start(bf16[128,1024]{1,0:T(8,128)(2,1)S(1)} %collective-permute-done.3.refs_0_), channel_id=1, source_target_pairs={{0,4},{4,8},{8,12},{12,14},{14,10},{10,6},{6,2},{2,0},{1,5},{5,9},... | collective-permute-start | bytes 786440 | tf_op jit(solution)/shard_map/ppermute | solution.py:62
  25.3 11.9 %collective-permute-start.7 = (bf16[128,1024]{1,0:T(8,128)(2,1)S(1)}, bf16[128,1024]{1,0:T(8,128)(2,1)S(1)}, u32[]{:S(2)}, u32[]{:S(2)}) collective-permute-start(bf16[128,1024]{1,0:T(8,128)(2,1)S(1)} %collective-permute-done.4.refs_1_), channel_id=1, source_target_pairs={{0,2},{4,0},{8,4},{12,8},{14,12},{10,14},{6,10},{2,6},{1,3},{5,1},... | collective-permute-start | bytes 786440 | tf_op jit(solution)/shard_map/ppermute | solution.py:65
  27.0 10.1 %collective-permute-start.8 = (bf16[64,640]{1,0:T(8,128)(2,1)S(1)}, bf16[64,640]{1,0:T(8,128)(2,1)S(1)}, u32[]{:S(2)}, u32[]{:S(2)}) collective-permute-start(bf16[64,640]{1,0:T(8,128)(2,1)S(1)} %fusion.3), channel_id=1, source_target_pairs={{0,8},{2,10},{4,12},{6,14},{8,0},{10,2},{12,4},{14,6},{1,9},{3,11}... | collective-permute-start | bytes 245768 | tf_op jit(solution)/shard_map/ppermute | solution.py:91
  44.8 23.3 %all-to-all-start = ((bf16[8,8,16,256]{3,2,1,0:T(8,128)(2,1)}), bf16[8,8,16,256]{3,2,1,0:T(8,128)(2,1)S(1)}, u32[]{:S(2)}, u32[]{:S(2)}) async-start(bf16[8,8,16,256]{3,2,1,0:T(8,128)(2,1)} %pick_heads.1), calls=%async_computation | async-start | bytes 1048576 | tf_op jit(solution)/shard_map/all_to_all | solution.py:104
  71.4 8.8 %collective-permute-start.15 = (bf16[128,1152]{1,0:T(8,128)(2,1)S(1)}, bf16[128,1152]{1,0:T(8,128)(2,1)S(1)}, u32[]{:S(2)}, u32[]{:S(2)}) collective-permute-start(bf16[128,1152]{1,0:T(8,128)(2,1)S(1)} %get-tuple-element.173), channel_id=1, source_target_pairs={{0,4},{4,8},{8,12},{12,14},{14,10},{10,6},{6,2},{2,0},{1,5},{5,9},... | collective-permute-start | bytes 884744 | tf_op jit(solution)/shard_map/ppermute | solution.py:62
  73.0 8.5 %collective-permute-start.16 = (bf16[128,1152]{1,0:T(8,128)(2,1)S(1)}, bf16[128,1152]{1,0:T(8,128)(2,1)S(1)}, u32[]{:S(2)}, u32[]{:S(2)}) collective-permute-start(bf16[128,1152]{1,0:T(8,128)(2,1)S(1)} %get-tuple-element.174), channel_id=1, source_target_pairs={{0,2},{4,0},{8,4},{12,8},{14,12},{10,14},{6,10},{2,6},{1,3},{5,1},... | collective-permute-start | bytes 884744 | tf_op jit(solution)/shard_map/ppermute | solution.py:65
  81.8 7.7 %collective-permute-start.17 = (bf16[128,1152]{1,0:T(8,128)(2,1)S(1)}, bf16[128,1152]{1,0:T(8,128)(2,1)S(1)}, u32[]{:S(2)}, u32[]{:S(2)}) collective-permute-start(bf16[128,1152]{1,0:T(8,128)(2,1)S(1)} %get-tuple-element.181), channel_id=1, source_target_pairs={{0,4},{4,8},{8,12},{12,14},{14,10},{10,6},{6,2},{2,0},{1,5},{5,9},... | collective-permute-start | bytes 884744 | tf_op jit(solution)/shard_map/ppermute | solution.py:62
  91.1 7.8 %collective-permute-start.19 = (bf16[128,1152]{1,0:T(8,128)(2,1)S(1)}, bf16[128,1152]{1,0:T(8,128)(2,1)S(1)}, u32[]{:S(2)}, u32[]{:S(2)}) collective-permute-start(bf16[128,1152]{1,0:T(8,128)(2,1)S(1)} %get-tuple-element.189), channel_id=1, source_target_pairs={{0,4},{4,8},{8,12},{12,14},{14,10},{10,6},{6,2},{2,0},{1,5},{5,9},... | collective-permute-start | bytes 884744 | tf_op jit(solution)/shard_map/ppermute | solution.py:62
  100.0 9.0 %collective-permute-start.22 = (bf16[128,1152]{1,0:T(8,128)(2,1)S(1)}, bf16[128,1152]{1,0:T(8,128)(2,1)S(1)}, u32[]{:S(2)}, u32[]{:S(2)}) collective-permute-start(bf16[128,1152]{1,0:T(8,128)(2,1)S(1)} %get-tuple-element.194.refs_0_), channel_id=1, source_target_pairs={{0,2},{4,0},{8,4},{12,8},{14,12},{10,14},{6,10},{2,6},{1,3},{5,1},... | collective-permute-start | bytes 884744 | tf_op jit(solution)/shard_map/ppermute | solution.py:65
  101.3 7.8 %collective-permute-start.21 = (bf16[128,1152]{1,0:T(8,128)(2,1)S(1)}, bf16[128,1152]{1,0:T(8,128)(2,1)S(1)}, u32[]{:S(2)}, u32[]{:S(2)}) collective-permute-start(bf16[128,1152]{1,0:T(8,128)(2,1)S(1)} %get-tuple-element.194.refs_0_), channel_id=1, source_target_pairs={{0,4},{4,8},{8,12},{12,14},{14,10},{10,6},{6,2},{2,0},{1,5},{5,9},... | collective-permute-start | bytes 884744 | tf_op jit(solution)/shard_map/ppermute | solution.py:62
  109.0 8.3 %collective-permute-start.25 = (bf16[128,1152]{1,0:T(8,128)(2,1)S(1)}, bf16[128,1152]{1,0:T(8,128)(2,1)S(1)}, u32[]{:S(2)}, u32[]{:S(2)}) collective-permute-start(bf16[128,1152]{1,0:T(8,128)(2,1)S(1)} %collective-permute-done.21.refs_0_), channel_id=1, source_target_pairs={{0,4},{4,8},{8,12},{12,14},{14,10},{10,6},{6,2},{2,0},{1,5},{5,9},... | collective-permute-start | bytes 884744 | tf_op jit(solution)/shard_map/ppermute | solution.py:62
  113.7 26.0 %collective-permute-start.37 = (bf16[64,16,256]{2,1,0:T(8,128)(2,1)S(1)}, bf16[64,16,256]{2,1,0:T(8,128)(2,1)S(1)}, u32[]{:S(2)}, u32[]{:S(2)}) collective-permute-start(bf16[64,16,256]{2,1,0:T(8,128)(2,1)S(1)} %bitcast.23), channel_id=1, source_target_pairs={{0,1},{1,0},{2,3},{3,2},{4,5},{5,4},{6,7},{7,6},{8,9},{9,8},{10,11... | collective-permute-start | bytes 1572872 | tf_op jit(solution)/shard_map/ppermute | solution.py:345
  117.3 11.2 %collective-permute-start.29 = (bf16[128,1152]{1,0:T(8,128)(2,1)S(1)}, bf16[128,1152]{1,0:T(8,128)(2,1)S(1)}, u32[]{:S(2)}, u32[]{:S(2)}) collective-permute-start(bf16[128,1152]{1,0:T(8,128)(2,1)S(1)} %collective-permute-done.25.refs_0_), channel_id=1, source_target_pairs={{0,4},{4,8},{8,12},{12,14},{14,10},{10,6},{6,2},{2,0},{1,5},{5,9},... | collective-permute-start | bytes 884744 | tf_op jit(solution)/shard_map/ppermute | solution.py:62
  118.2 10.3 %collective-permute-start.30 = (bf16[128,1152]{1,0:T(8,128)(2,1)S(1)}, bf16[128,1152]{1,0:T(8,128)(2,1)S(1)}, u32[]{:S(2)}, u32[]{:S(2)}) collective-permute-start(bf16[128,1152]{1,0:T(8,128)(2,1)S(1)} %collective-permute-done.26.refs_1_), channel_id=1, source_target_pairs={{0,2},{4,0},{8,4},{12,8},{14,12},{10,14},{6,10},{2,6},{1,3},{5,1},... | collective-permute-start | bytes 884744 | tf_op jit(solution)/shard_map/ppermute | solution.py:65
  119.9 8.0 %collective-permute-start.31 = (bf16[128,256]{1,0:T(8,128)(2,1)S(1)}, bf16[128,256]{1,0:T(8,128)(2,1)S(1)}, u32[]{:S(2)}, u32[]{:S(2)}) collective-permute-start(bf16[128,256]{1,0:T(8,128)(2,1)S(1)} %get-tuple-element.213), channel_id=1, source_target_pairs={{0,4},{4,8},{8,12},{12,14},{14,10},{10,6},{6,2},{2,0},{1,5},{5,9},... | collective-permute-start | bytes 196616 | tf_op jit(solution)/shard_map/ppermute | solution.py:62
  128.5 8.0 %collective-permute-start.33 = (bf16[64,1152]{1,0:T(8,128)(2,1)S(1)}, bf16[64,1152]{1,0:T(8,128)(2,1)S(1)}, u32[]{:S(2)}, u32[]{:S(2)}) collective-permute-start(bf16[64,1152]{1,0:T(8,128)(2,1)S(1)} %slice.18), channel_id=1, source_target_pairs={{0,4},{4,8},{8,12},{12,14},{14,10},{10,6},{6,2},{2,0},{1,5},{5,9},... | collective-permute-start | bytes 442376 | tf_op jit(solution)/shard_map/ppermute | solution.py:62
  158.4 8.4 %collective-permute-start.42 = (bf16[128,1024]{1,0:T(8,128)(2,1)S(1)}, bf16[128,1024]{1,0:T(8,128)(2,1)S(1)}, u32[]{:S(2)}, u32[]{:S(2)}) collective-permute-start(bf16[128,1024]{1,0:T(8,128)(2,1)S(1)} %get-tuple-element.255), channel_id=1, source_target_pairs={{0,4},{4,8},{8,12},{12,14},{14,10},{10,6},{6,2},{2,0},{1,5},{5,9},... | collective-permute-start | bytes 786440 | tf_op jit(solution)/shard_map/ppermute | solution.py:62
  159.8 8.9 %collective-permute-start.43 = (bf16[128,1024]{1,0:T(8,128)(2,1)S(1)}, bf16[128,1024]{1,0:T(8,128)(2,1)S(1)}, u32[]{:S(2)}, u32[]{:S(2)}) collective-permute-start(bf16[128,1024]{1,0:T(8,128)(2,1)S(1)} %get-tuple-element.256), channel_id=1, source_target_pairs={{0,2},{4,0},{8,4},{12,8},{14,12},{10,14},{6,10},{2,6},{1,3},{5,1},... | collective-permute-start | bytes 786440 | tf_op jit(solution)/shard_map/ppermute | solution.py:65
  (43 other events, 263.8 us)
